TPU v7x, 512 devices: a whole 4x4x16 slice. The times are simulated.
512 devices in a mesh: ocx: 16 (over z), ocy: 4 (over x), ml: 8 (over y, core).
Axes of the slice: x: 4, y: 4, z: 16, core: 2. Of those that a mesh axis runs over, the one named last changes fastest.
Arguments:
- tracer: float32 [75, 64, 4096], P(None, 'ocx', ('ocy', 'ml')), may hold values from -4 to 4
- east_velocity: float32 [75, 64, 4096], P(None, 'ocx', ('ocy', 'ml')), may hold values from -0.15 to 0.15
- north_velocity: float32 [75, 64, 4096], P(None, 'ocx', ('ocy', 'ml')), may hold values from -0.15 to 0.15
- target_increment: bfloat16 [75, 64, 4096], P(None, 'ocx', ('ocy', 'ml')), may hold values from -21 to 21
- depth_levels: int32 [64, 4096], P('ocx', ('ocy', 'ml')), may hold values from 0 to 75, as said below
- relay_slots: int32 [16, 32, 32, 12], P('ocx', ('ocy', 'ml')), may hold values from 0 to 512, as said below
- closure_w1: bfloat16 [225, 1024], replicated, may hold values from -0.375 to 0.375
- closure_b1: float32 [1024], replicated, may hold values from -3 to 3
- closure_w2: bfloat16 [1024, 75], replicated, may hold values from -0.1875 to 0.1875
- closure_b2: float32 [75], replicated, may hold values from -3 to 3
Outputs:
- tracer_out: float32 [75, 64, 4096], P(None, 'ocx', ('ocy', 'ml'))
- misfit_out: bfloat16 [75, 64, 4096], P(None, 'ocx', ('ocy', 'ml'))
- grad_w1: float32 [225, 1024], replicated
- grad_b1: float32 [1024], replicated
- grad_w2: float32 [1024, 75], replicated
- grad_b2: float32 [75], replicated
Inputs may be any that keep to these rules, and one draw needn't show every extreme that they name: A column has depth_levels > 0 exactly when relay_slots names it. relay_slots[a, b, r, q] names a column of tile (a, b), the cells with longitude a * 4 to a * 4 + 3 and latitude b * 128 to b * 128 + 127, numbered i * 128 + j inside the tile, whose closure is computed by shard r of the tiles with the same a; the value 4 * 128 marks an unused entry. No column is named twice. For every a, one shard r receives 12 named columns from every tile b.
All inputs are finite; a program needn't handle non-finite values.
Results may differ from a plain program's by a relative error of at most 0.0044.
Values may be sent and summed in bfloat16 or wider, within the bound.
A program may use at most 64 MiB of HBM per device.

v0:
```python
import jax
import jax.numpy as jnp
from jax import lax
from jax.sharding import PartitionSpec as P

STEPS = 3


KAPPA = 0.1


def padded_2(value, sides, width):
    for axis, dim in sides:
        size, length = (lax.axis_size(axis), value.shape[dim])
        up = [(i, (i + 1) % size) for i in range(size)]
        down = [(j, i) for i, j in up]
        last = lax.slice_in_dim(value, length - width, length, axis=dim)
        first = lax.slice_in_dim(value, 0, width, axis=dim)
        before = lax.ppermute(last, axis, up)
        after = lax.ppermute(first, axis, down)
        value = jnp.concatenate([before, value, after], axis=dim)
    return value


def closure(row_data, depth_rows, closure_w1, closure_b1, closure_w2, closure_b2, columns):
    levels_n = closure_w2.shape[1]
    inputs = row_data[:, : 3 * levels_n]
    wanted = row_data[:, 3 * levels_n :].astype(jnp.float32)
    level_ids = jnp.arange(levels_n, dtype=jnp.float32)
    level_mask = (level_ids[None, :] < depth_rows.astype(jnp.float32)[:, None]).astype(jnp.float32)
    before = jnp.dot(inputs, closure_w1, preferred_element_type=jnp.float32) + closure_b1
    stash = lax.optimization_barrier(before.astype(jnp.bfloat16)).astype(jnp.float32)
    gate_sig = jax.nn.sigmoid(stash)
    hidden = (stash * gate_sig).astype(jnp.bfloat16)
    output = jnp.dot(hidden, closure_w2, preferred_element_type=jnp.float32) + closure_b2
    tendency = (output * level_mask).astype(jnp.bfloat16)
    misfit = tendency.astype(jnp.float32) - wanted
    d_output = (misfit / columns).astype(jnp.bfloat16)
    grad_w2 = jnp.dot(hidden.T, d_output, preferred_element_type=jnp.float32)
    grad_b2 = jnp.sum(d_output.astype(jnp.float32), axis=0)
    d_hidden = jnp.dot(d_output, closure_w2.T, preferred_element_type=jnp.float32)
    d_before = (d_hidden * gate_sig * (1.0 + stash * (1.0 - gate_sig))).astype(jnp.bfloat16)
    grad_w1 = jnp.dot(inputs.T, d_before, preferred_element_type=jnp.float32)
    grad_b1 = jnp.sum(d_before.astype(jnp.float32), axis=0)
    return (tendency, (grad_w1, grad_b1, grad_w2, grad_b2))


def run_blocks(row_data, depth_rows, closure_w1, closure_b1, closure_w2, closure_b2, columns):
    total_rows = row_data.shape[0]
    blocks = max(1, total_rows // 1024)
    while total_rows % blocks:
        blocks = blocks - 1
    block_rows = total_rows // blocks

    def one_block(running, pieces):
        tendency, grads = closure(
            pieces[0], pieces[1], closure_w1, closure_b1, closure_w2, closure_b2, columns
        )
        return (tuple((earlier + update for earlier, update in zip(running, grads))), tendency)

    start = (
        jnp.zeros(closure_w1.shape, jnp.float32),
        jnp.zeros(closure_b1.shape, jnp.float32),
        jnp.zeros(closure_w2.shape, jnp.float32),
        jnp.zeros(closure_b2.shape, jnp.float32),
    )
    totals, tendency = lax.scan(
        one_block,
        start,
        (
            row_data.reshape(blocks, block_rows, row_data.shape[1]),
            depth_rows.reshape(blocks, block_rows),
        ),
    )
    return (tendency.reshape(total_rows, tendency.shape[2]), totals)


def on_device(
    tracer,
    east_velocity,
    north_velocity,
    target_increment,
    depth_levels,
    relay_slots,
    closure_w1,
    closure_b1,
    closure_w2,
    closure_b2,
):
    levels_n, tile_x, tile_y = tracer.shape
    cells = tile_x * tile_y
    members = relay_slots.shape[2]
    capacity = relay_slots.shape[3]
    lat_count = lax.axis_size("ocy")
    shard_count = lax.axis_size("ml")
    lat_total = tile_y * lax.axis_size(("ocy", "ml"))
    columns = cells * lax.axis_size("ocx") * lat_count * shard_count
    margin = 1
    depth_f = depth_levels.astype(jnp.float32)[None]
    east_ext, north_ext, depth_ext = (
        padded_2(
            east_velocity.astype(jnp.bfloat16), (("ocx", 1), (("ocy", "ml"), 2)), margin
        ).astype(east_velocity.dtype),
        padded_2(
            north_velocity.astype(jnp.bfloat16), (("ocx", 1), (("ocy", "ml"), 2)), margin
        ).astype(north_velocity.dtype),
        padded_2(depth_f.astype(jnp.bfloat16), (("ocx", 1), (("ocy", "ml"), 2)), margin).astype(
            depth_f.dtype
        ),
    )
    level_ids = jnp.arange(levels_n, dtype=jnp.float32)[:, None, None]
    lat_start = lax.axis_index(("ocy", "ml")) * tile_y
    tracer_now = tracer
    for number in range(STEPS):
        advance_current = padded_2(tracer_now, (("ocx", 1), (("ocy", "ml"), 2)), margin)
        east_open = level_ids < jnp.minimum(depth_ext[:, :-1, :], depth_ext[:, 1:, :])
        east_speed = east_ext[:, :-1, :]
        west_side = advance_current[:, :-1, :]
        east_side = advance_current[:, 1:, :]
        east_flux = jnp.where(
            east_open,
            jnp.maximum(east_speed, 0.0) * west_side
            + jnp.minimum(east_speed, 0.0) * east_side
            - KAPPA * (east_side - west_side),
            0.0,
        )
        face_rows = lat_start - 1 + jnp.arange(advance_current.shape[2] - 1, dtype=jnp.int32)
        north_open = (level_ids < jnp.minimum(depth_ext[:, :, :-1], depth_ext[:, :, 1:])) & (
            jnp.mod(face_rows, lat_total) != lat_total - 1
        )[None, None, :]
        north_speed = north_ext[:, :, :-1]
        south_side = advance_current[:, :, :-1]
        north_side = advance_current[:, :, 1:]
        north_flux = jnp.where(
            north_open,
            jnp.maximum(north_speed, 0.0) * south_side
            + jnp.minimum(north_speed, 0.0) * north_side
            - KAPPA * (north_side - south_side),
            0.0,
        )
        tracer_now = (
            advance_current[:, 1:-1, 1:-1]
            + east_flux[:, :-1, 1:-1]
            - east_flux[:, 1:, 1:-1]
            + north_flux[:, 1:-1, :-1]
            - north_flux[:, 1:-1, 1:]
        )
    wet = level_ids < depth_f
    target_wet = jnp.where(wet, target_increment, jnp.zeros((), jnp.bfloat16))
    features = jnp.concatenate(
        [
            jnp.where(wet, tracer_now, 0.0).astype(jnp.bfloat16),
            jnp.where(wet, east_velocity, 0.0).astype(jnp.bfloat16),
            jnp.where(wet, north_velocity, 0.0).astype(jnp.bfloat16),
            target_wet,
        ],
        axis=0,
    )
    row_data = features.reshape(4 * levels_n, cells).T
    depth_col = depth_f.reshape(cells)
    slots = relay_slots.reshape(members * capacity)
    padded = jnp.concatenate([row_data, jnp.zeros((1, 4 * levels_n), jnp.bfloat16)], axis=0)
    depth_pad = jnp.concatenate([depth_col, jnp.zeros((1,), jnp.float32)])[slots].astype(
        jnp.bfloat16
    )
    gathered = padded[slots]
    outgoing = gathered.reshape(members, capacity, 4 * levels_n)
    depth_out = depth_pad.reshape(members, capacity)
    arrived, depth_in = (
        lax.all_to_all(outgoing, ("ocy", "ml"), split_axis=0, concat_axis=0, tiled=True),
        lax.all_to_all(depth_out, ("ocy", "ml"), split_axis=0, concat_axis=0, tiled=True),
    )
    tendency_rows, grads = run_blocks(
        arrived.reshape(members * capacity, 4 * levels_n),
        depth_in.reshape(members * capacity),
        closure_w1,
        closure_b1,
        closure_w2,
        closure_b2,
        columns,
    )
    returning = tendency_rows.reshape(members, capacity * levels_n)
    landed = lax.all_to_all(returning, ("ocy", "ml"), split_axis=0, concat_axis=0, tiled=True)
    tendency_cols = (
        jnp.zeros((cells + 1, levels_n), jnp.bfloat16)
        .at[slots]
        .set(landed.reshape(members * capacity, levels_n))[:cells]
    )
    tendency_grid = tendency_cols.T.reshape(levels_n, tile_x, tile_y).astype(jnp.float32)
    tracer_out = tracer_now + tendency_grid
    misfit_out = (tendency_grid - target_wet.astype(jnp.float32)).astype(jnp.bfloat16)
    grad_w1, grad_b1, grad_w2, grad_b2 = lax.psum(
        (grads[0], grads[1], grads[2], grads[3]), ("ocx", "ocy", "ml")
    )
    return (tracer_out, misfit_out, grad_w1, grad_b1, grad_w2, grad_b2)


def solution(mesh):
    placed = (
        P(None, "ocx", ("ocy", "ml")),
        P(None, "ocx", ("ocy", "ml")),
        P(None, "ocx", ("ocy", "ml")),
        P(None, "ocx", ("ocy", "ml")),
        P("ocx", ("ocy", "ml")),
        P("ocx", ("ocy", "ml"), None, None),
        P(),
        P(),
        P(),
        P(),
    )
    return jax.shard_map(
        on_device,
        mesh=mesh,
        in_specs=placed,
        out_specs=(
            P(None, "ocx", ("ocy", "ml")),
            P(None, "ocx", ("ocy", "ml")),
            P(),
            P(),
            P(),
            P(),
        ),
        check_vma=False,
    )
```

profile of v0, /device:TPU:1, one launch (start us, length us, event | category | flops | bytes accessed | tf_op | source)
XLA Modules:
  0.0 634.9 jit_solution(10593059639412030177)
XLA Ops:
  7.2 0.8 convert_bitcast_fusion.1
  8.0 4.4 collective-permute-start
  12.3 9.5 %collective-permute-start.1 = (bf16[1,1,128]{2,1,0:T(2,128)(2,1)S(1)}, bf16[1,1,128]{2,1,0:T(2,128)(2,1)S(1)}, u32[]{:S(2)}, u32[]{:S(2)}) collective-permute-start(bf16[1,1,128]{2,1,0:T(2,128)(2,1)S(1)} %get-tuple-element.77), channel_id=1, source_target_pairs={{32,0},{64,32},{96,64},{128,96},{160,128},{192,160},{224,192},{256... | collective-permute-start | bytes 776 | tf_op jit(solution)/shard_map/ppermute | solution.py:20
  21.9 0.9 convert_element_type.124
  22.9 1.9 collective-permute-start.12
  24.8 4.6 collective-permute-start.13
  29.4 0.9 convert_element_type.123
  30.4 1.9 collective-permute-start.4
  32.3 1.1 fusion.58
  33.4 4.6 collective-permute-start.5
  38.1 5.2 collective-permute-start.2
  43.3 0.7 collective-permute-done.2
  44.0 6.3 collective-permute-start.3
  50.3 0.8 collective-permute-done.3
  51.1 1.9 collective-permute-start.8
  53.2 4.6 collective-permute-start.9
  58.0 1.9 collective-permute-start.14
  60.4 1.9 collective-permute-start.10
  62.3 3.0 collective-permute-start.11
  65.4 2.6 collective-permute-start.6
  68.0 6.3 collective-permute-start.7
  74.3 1.0 fusion.32
  75.4 0.6 pad_maximum_fusion
  76.0 0.6 fusion.23
  77.1 1.9 collective-permute-start.15
  79.0 4.6 collective-permute-start.16
  83.8 0.8 collective-permute-done.16
  84.9 1.9 collective-permute-start.17
  86.8 9.1 %collective-permute-start.18 = (f32[75,6,1]{2,1,0:T(8,128)S(1)}, f32[75,6,1]{2,1,0:T(8,128)S(1)}, u32[]{:S(2)}, u32[]{:S(2)}) collective-permute-start(f32[75,6,1]{2,1,0:T(8,128)S(1)} %get-tuple-element.51), channel_id=1, source_target_pairs={{1,0},{2,1},{3,2},{4,3},{5,4},{6,5},{7,6},{8,7},{9,8},{10,9},{11,1... | collective-permute-start | bytes 5408 | tf_op jit(solution)/shard_map/ppermute | solution.py:20
  95.9 1.2 collective-permute-done.18
  97.1 1.0 fusion.35
  98.2 0.6 pad_maximum_fusion.2
  98.8 0.6 fusion.26
  99.8 1.9 collective-permute-start.19
  101.7 5.2 collective-permute-start.20
  106.9 1.0 collective-permute-done.20
  108.2 1.9 collective-permute-start.21
  110.2 11.0 %collective-permute-start.22 = (f32[75,6,1]{2,1,0:T(8,128)S(1)}, f32[75,6,1]{2,1,0:T(8,128)S(1)}, u32[]{:S(2)}, u32[]{:S(2)}) collective-permute-start(f32[75,6,1]{2,1,0:T(8,128)S(1)} %get-tuple-element.49), channel_id=1, source_target_pairs={{1,0},{2,1},{3,2},{4,3},{5,4},{6,5},{7,6},{8,7},{9,8},{10,9},{11,1... | collective-permute-start | bytes 5408 | tf_op jit(solution)/shard_map/ppermute | solution.py:20
  121.1 2.8 gather_fusion
  124.0 0.7 convert_element_type.150
  124.7 8.5 %all-to-all-start = ((bf16[32,1,12]{2,1,0:T(2,128)(2,1)}), bf16[32,1,12]{2,1,0:T(2,128)(2,1)S(1)}, u32[]{:S(2)}, u32[]{:S(2)}) async-start(bf16[32,1,12]{2,1,0:T(2,128)(2,1)} %convert_element_type.150), calls=%async_computation | async-start | bytes 32768 | tf_op jit(solution)/shard_map/all_to_all | solution.py:171
  133.3 1.0 fusion.38
  134.3 0.6 pad_maximum_fusion.4
  135.0 0.6 fusion.29
  136.9 2.1 gather_fusion.1
  139.1 0.8 reshape.147
  140.2 7.3 %all-to-all-start.1 = ((bf16[32,12,300]{2,1,0:T(8,128)(2,1)}), bf16[32,12,300]{2,1,0:T(8,128)(2,1)S(1)}, u32[]{:S(2)}, u32[]{:S(2)}) async-start(bf16[32,12,300]{2,1,0:T(8,128)(2,1)} %reshape.147), calls=%async_computation.1 | async-start | bytes 786432 | tf_op jit(solution)/shard_map/all_to_all | solution.py:170
  147.8 10.1 %all-to-all-done.1 = bf16[32,12,300]{2,1,0:T(8,128)(2,1)S(1)} async-done(((bf16[32,12,300]{2,1,0:T(8,128)(2,1)}), bf16[32,12,300]{2,1,0:T(8,128)(2,1)S(1)}, u32[]{:S(2)}, u32[]{:S(2)}) %all-to-all-start.1) | async-done | bytes 230432 | tf_op jit(solution)/shard_map/all_to_all | solution.py:170
  158.6 0.5 fusion.3
  159.1 0.4 copy-done.7
  159.5 0.5 convert_reduce_fusion.1
  160.0 1.0 fusion.51
  161.0 0.8 convert_reduce_fusion
  161.8 1.4 fusion.40
  163.5 0.5 broadcast.131
  164.1 1.0 reduce.7
  165.1 0.8 reshape.186
  165.8 3.6 all-to-all-start.2
  169.5 106.0 %all-reduce.1 = (f32[1024]{0:T(1024)}, f32[75]{0:T(128)}) all-reduce(f32[1024]{0:T(1024)S(1)} %get-tuple-element.78, f32[75]{0:T(128)S(1)} %get-tuple-element.80), channel_id=1, replica_groups=mesh['ocx'=16,'ocy'=4,'ml'=8] {'ocx','ocy','ml'}, use_global_device_ids=true, to_apply=%region_3.4 | all-reduce | flops 1099 | bytes 8792 | tf_op jit(solution)/shard_map/psum | solution.py:192
  276.1 1.5 scatter_custom_fusion
  277.8 0.8 subtract_convert_fusion
  278.6 346.5 %all-reduce.5.cloned.1.call-done = (f32[225,1024]{1,0:T(8,128)}, f32[1024,75]{0,1:T(8,128)}) async-done(((f32[225,1024]{1,0:T(8,128)}, f32[1024,75]{0,1:T(8,128)}), (f32[225,1024]{1,0:T(8,128)}, f32[1024,75]{0,1:T(8,128)})) %all-reduce.5.cloned.1.call-update) | async-done | bytes 1228816 | tf_op jit(solution)/shard_map/psum | solution.py:192
  625.1 2.3 copy.35
  627.4 0.7 copy.36
  (85 shorter events, 6.4 us)
Async XLA Ops:
  7.2 151.1 %copy-start = (bf16[225,1024]{1,0:T(8,128)(2,1)S(1)}, bf16[225,1024]{1,0:T(8,128)(2,1)}, u32[]{:S(2)}) copy-start(bf16[225,1024]{1,0:T(8,128)(2,1)} %param.16) | copy-start | bytes 1382404
  7.2 52.9 %copy-start.1 = (f32[75,4,128]{2,1,0:T(4,128)S(1)}, f32[75,4,128]{2,1,0:T(4,128)}, u32[]{:S(2)}) copy-start(f32[75,4,128]{2,1,0:T(4,128)} %param.10) | copy-start | bytes 460804
  8.0 25.4 %collective-permute-start = (bf16[1,1,128]{2,1,0:T(2,128)(2,1)S(1)}, bf16[1,1,128]{2,1,0:T(2,128)(2,1)S(1)}, u32[]{:S(2)}, u32[]{:S(2)}) collective-permute-start(bf16[1,1,128]{2,1,0:T(2,128)(2,1)S(1)} %get-tuple-element.76), channel_id=1, source_target_pairs={{0,32},{32,64},{64,96},{96,128},{128,160},{160,192},{192,224},{224... | collective-permute-start | bytes 776 | tf_op jit(solution)/shard_map/ppermute | solution.py:19
  12.3 25.6 %collective-permute-start.1 = (bf16[1,1,128]{2,1,0:T(2,128)(2,1)S(1)}, bf16[1,1,128]{2,1,0:T(2,128)(2,1)S(1)}, u32[]{:S(2)}, u32[]{:S(2)}) collective-permute-start(bf16[1,1,128]{2,1,0:T(2,128)(2,1)S(1)} %get-tuple-element.77), channel_id=1, source_target_pairs={{32,0},{64,32},{96,64},{128,96},{160,128},{192,160},{224,192},{256... | collective-permute-start | bytes 776 | tf_op jit(solution)/shard_map/ppermute | solution.py:20
  22.9 30.3 %collective-permute-start.12 = (bf16[75,1,128]{2,1,0:T(2,128)(2,1)S(1)}, bf16[75,1,128]{2,1,0:T(2,128)(2,1)S(1)}, u32[]{:S(2)}, u32[]{:S(2)}) collective-permute-start(bf16[75,1,128]{2,1,0:T(2,128)(2,1)S(1)} %get-tuple-element.66), channel_id=1, source_target_pairs={{0,32},{32,64},{64,96},{96,128},{128,160},{160,192},{192,224},{224... | collective-permute-start | bytes 57608 | tf_op jit(solution)/shard_map/ppermute | solution.py:19
  24.8 33.0 %collective-permute-start.13 = (bf16[75,1,128]{2,1,0:T(2,128)(2,1)S(1)}, bf16[75,1,128]{2,1,0:T(2,128)(2,1)S(1)}, u32[]{:S(2)}, u32[]{:S(2)}) collective-permute-start(bf16[75,1,128]{2,1,0:T(2,128)(2,1)S(1)} %get-tuple-element.67), channel_id=1, source_target_pairs={{32,0},{64,32},{96,64},{128,96},{160,128},{192,160},{224,192},{256... | collective-permute-start | bytes 57608 | tf_op jit(solution)/shard_map/ppermute | solution.py:20
  30.4 29.5 %collective-permute-start.4 = (bf16[75,1,128]{2,1,0:T(2,128)(2,1)S(1)}, bf16[75,1,128]{2,1,0:T(2,128)(2,1)S(1)}, u32[]{:S(2)}, u32[]{:S(2)}) collective-permute-start(bf16[75,1,128]{2,1,0:T(2,128)(2,1)S(1)} %get-tuple-element.64), channel_id=1, source_target_pairs={{0,32},{32,64},{64,96},{96,128},{128,160},{160,192},{192,224},{224... | collective-permute-start | bytes 57608 | tf_op jit(solution)/shard_map/ppermute | solution.py:19
  33.4 26.5 %collective-permute-start.5 = (bf16[75,1,128]{2,1,0:T(2,128)(2,1)S(1)}, bf16[75,1,128]{2,1,0:T(2,128)(2,1)S(1)}, u32[]{:S(2)}, u32[]{:S(2)}) collective-permute-start(bf16[75,1,128]{2,1,0:T(2,128)(2,1)S(1)} %get-tuple-element.65), channel_id=1, source_target_pairs={{32,0},{64,32},{96,64},{128,96},{160,128},{192,160},{224,192},{256... | collective-permute-start | bytes 57608 | tf_op jit(solution)/shard_map/ppermute | solution.py:20
  38.1 5.9 collective-permute-start.2
  44.0 7.1 %collective-permute-start.3 = (bf16[1,6,1]{2,1,0:T(8,128)(2,1)S(1)}, bf16[1,6,1]{2,1,0:T(8,128)(2,1)S(1)}, u32[]{:S(2)}, u32[]{:S(2)}) collective-permute-start(bf16[1,6,1]{2,1,0:T(8,128)(2,1)S(1)} %get-tuple-element.75), channel_id=1, source_target_pairs={{1,0},{2,1},{3,2},{4,3},{5,4},{6,5},{7,6},{8,7},{9,8},{10,9},{11,1... | collective-permute-start | bytes 44 | tf_op jit(solution)/shard_map/ppermute | solution.py:20
  51.1 9.0 %collective-permute-start.8 = (f32[75,1,128]{2,1,0:T(1,128)S(1)}, f32[75,1,128]{2,1,0:T(1,128)S(1)}, u32[]{:S(2)}, u32[]{:S(2)}) collective-permute-start(f32[75,1,128]{2,1,0:T(1,128)S(1)} %get-tuple-element.62), channel_id=1, source_target_pairs={{0,32},{32,64},{64,96},{96,128},{128,160},{160,192},{192,224},{224... | collective-permute-start | bytes 115208 | tf_op jit(solution)/shard_map/ppermute | solution.py:19
  53.2 6.9 %collective-permute-start.9 = (f32[75,1,128]{2,1,0:T(1,128)S(1)}, f32[75,1,128]{2,1,0:T(1,128)S(1)}, u32[]{:S(2)}, u32[]{:S(2)}) collective-permute-start(f32[75,1,128]{2,1,0:T(1,128)S(1)} %get-tuple-element.63), channel_id=1, source_target_pairs={{32,0},{64,32},{96,64},{128,96},{160,128},{192,160},{224,192},{256... | collective-permute-start | bytes 115208 | tf_op jit(solution)/shard_map/ppermute | solution.py:20
  58.0 16.3 %collective-permute-start.14 = (bf16[75,6,1]{2,1,0:T(8,128)(2,1)S(1)}, bf16[75,6,1]{2,1,0:T(8,128)(2,1)S(1)}, u32[]{:S(2)}, u32[]{:S(2)}) collective-permute-start(bf16[75,6,1]{2,1,0:T(8,128)(2,1)S(1)} %pad_maximum_fusion.14), channel_id=1, source_target_pairs={{0,1},{1,2},{2,3},{3,4},{4,5},{5,6},{6,7},{7,8},{8,9},{9,10},{10,1... | collective-permute-start | bytes 2708 | tf_op jit(solution)/shard_map/ppermute | solution.py:19
  60.4 13.9 %collective-permute-start.10 = (f32[75,6,1]{2,1,0:T(8,128)S(1)}, f32[75,6,1]{2,1,0:T(8,128)S(1)}, u32[]{:S(2)}, u32[]{:S(2)}) collective-permute-start(f32[75,6,1]{2,1,0:T(8,128)S(1)} %get-tuple-element.52), channel_id=1, source_target_pairs={{0,1},{1,2},{2,3},{3,4},{4,5},{5,6},{6,7},{7,8},{8,9},{9,10},{10,1... | collective-permute-start | bytes 5408 | tf_op jit(solution)/shard_map/ppermute | solution.py:19
  62.3 12.0 %collective-permute-start.11 = (f32[75,6,1]{2,1,0:T(8,128)S(1)}, f32[75,6,1]{2,1,0:T(8,128)S(1)}, u32[]{:S(2)}, u32[]{:S(2)}) collective-permute-start(f32[75,6,1]{2,1,0:T(8,128)S(1)} %get-tuple-element.53), channel_id=1, source_target_pairs={{1,0},{2,1},{3,2},{4,3},{5,4},{6,5},{7,6},{8,7},{9,8},{10,9},{11,1... | collective-permute-start | bytes 5408 | tf_op jit(solution)/shard_map/ppermute | solution.py:20
  65.4 10.6 %collective-permute-start.6 = (bf16[75,6,1]{2,1,0:T(8,128)(2,1)S(1)}, bf16[75,6,1]{2,1,0:T(8,128)(2,1)S(1)}, u32[]{:S(2)}, u32[]{:S(2)}) collective-permute-start(bf16[75,6,1]{2,1,0:T(8,128)(2,1)S(1)} %get-tuple-element.60), channel_id=1, source_target_pairs={{0,1},{1,2},{2,3},{3,4},{4,5},{5,6},{6,7},{7,8},{8,9},{9,10},{10,1... | collective-permute-start | bytes 2708 | tf_op jit(solution)/shard_map/ppermute | solution.py:19
  68.0 8.0 %collective-permute-start.7 = (bf16[75,6,1]{2,1,0:T(8,128)(2,1)S(1)}, bf16[75,6,1]{2,1,0:T(8,128)(2,1)S(1)}, u32[]{:S(2)}, u32[]{:S(2)}) collective-permute-start(bf16[75,6,1]{2,1,0:T(8,128)(2,1)S(1)} %get-tuple-element.61), channel_id=1, source_target_pairs={{1,0},{2,1},{3,2},{4,3},{5,4},{6,5},{7,6},{8,7},{9,8},{10,9},{11,1... | collective-permute-start | bytes 2708 | tf_op jit(solution)/shard_map/ppermute | solution.py:20
  76.7 6.9 %copy-start.6 = (s32[1,1,32,12]{2,1,3,0:T(1,128)S(1)}, s32[1,1,32,12]{2,1,3,0:T(1,128)}, u32[]{:S(2)}) copy-start(s32[1,1,32,12]{2,1,3,0:T(1,128)} %param.15) | copy-start | bytes 4612
  77.1 6.7 %collective-permute-start.15 = (f32[75,1,128]{2,1,0:T(1,128)S(1)}, f32[75,1,128]{2,1,0:T(1,128)S(1)}, u32[]{:S(2)}, u32[]{:S(2)}) collective-permute-start(f32[75,1,128]{2,1,0:T(1,128)S(1)} %get-tuple-element.58), channel_id=1, source_target_pairs={{0,32},{32,64},{64,96},{96,128},{128,160},{160,192},{192,224},{224... | collective-permute-start | bytes 115208 | tf_op jit(solution)/shard_map/ppermute | solution.py:19
  79.0 5.6 collective-permute-start.16
  84.9 11.0 %collective-permute-start.17 = (f32[75,6,1]{2,1,0:T(8,128)S(1)}, f32[75,6,1]{2,1,0:T(8,128)S(1)}, u32[]{:S(2)}, u32[]{:S(2)}) collective-permute-start(f32[75,6,1]{2,1,0:T(8,128)S(1)} %get-tuple-element.50), channel_id=1, source_target_pairs={{0,1},{1,2},{2,3},{3,4},{4,5},{5,6},{6,7},{7,8},{8,9},{9,10},{10,1... | collective-permute-start | bytes 5408 | tf_op jit(solution)/shard_map/ppermute | solution.py:19
  86.8 10.3 %collective-permute-start.18 = (f32[75,6,1]{2,1,0:T(8,128)S(1)}, f32[75,6,1]{2,1,0:T(8,128)S(1)}, u32[]{:S(2)}, u32[]{:S(2)}) collective-permute-start(f32[75,6,1]{2,1,0:T(8,128)S(1)} %get-tuple-element.51), channel_id=1, source_target_pairs={{1,0},{2,1},{3,2},{4,3},{5,4},{6,5},{7,6},{8,7},{9,8},{10,9},{11,1... | collective-permute-start | bytes 5408 | tf_op jit(solution)/shard_map/ppermute | solution.py:20
  99.8 7.1 %collective-permute-start.19 = (f32[75,1,128]{2,1,0:T(1,128)S(1)}, f32[75,1,128]{2,1,0:T(1,128)S(1)}, u32[]{:S(2)}, u32[]{:S(2)}) collective-permute-start(f32[75,1,128]{2,1,0:T(1,128)S(1)} %get-tuple-element.56), channel_id=1, source_target_pairs={{0,32},{32,64},{64,96},{96,128},{128,160},{160,192},{192,224},{224... | collective-permute-start | bytes 115208 | tf_op jit(solution)/shard_map/ppermute | solution.py:19
  101.7 6.2 collective-permute-start.20
  108.2 25.0 %collective-permute-start.21 = (f32[75,6,1]{2,1,0:T(8,128)S(1)}, f32[75,6,1]{2,1,0:T(8,128)S(1)}, u32[]{:S(2)}, u32[]{:S(2)}) collective-permute-start(f32[75,6,1]{2,1,0:T(8,128)S(1)} %get-tuple-element.48), channel_id=1, source_target_pairs={{0,1},{1,2},{2,3},{3,4},{4,5},{5,6},{6,7},{7,8},{8,9},{9,10},{10,1... | collective-permute-start | bytes 5408 | tf_op jit(solution)/shard_map/ppermute | solution.py:19
  110.2 23.1 %collective-permute-start.22 = (f32[75,6,1]{2,1,0:T(8,128)S(1)}, f32[75,6,1]{2,1,0:T(8,128)S(1)}, u32[]{:S(2)}, u32[]{:S(2)}) collective-permute-start(f32[75,6,1]{2,1,0:T(8,128)S(1)} %get-tuple-element.49), channel_id=1, source_target_pairs={{1,0},{2,1},{3,2},{4,3},{5,4},{6,5},{7,6},{8,7},{9,8},{10,9},{11,1... | collective-permute-start | bytes 5408 | tf_op jit(solution)/shard_map/ppermute | solution.py:20
  124.7 15.5 %all-to-all-start = ((bf16[32,1,12]{2,1,0:T(2,128)(2,1)}), bf16[32,1,12]{2,1,0:T(2,128)(2,1)S(1)}, u32[]{:S(2)}, u32[]{:S(2)}) async-start(bf16[32,1,12]{2,1,0:T(2,128)(2,1)} %convert_element_type.150), calls=%async_computation | async-start | bytes 32768 | tf_op jit(solution)/shard_map/all_to_all | solution.py:171
  135.0 0.9 copy-start.2
  135.0 1.0 copy-start.3
  135.0 1.0 copy-start.5
  139.9 18.3 %copy-start.8 = (f32[1024]{0:T(1024)S(1)}, f32[1024]{0:T(1024)}, u32[]{:S(2)}) copy-start(f32[1024]{0:T(1024)} %param.17) | copy-start | bytes 12292
  140.2 17.6 %all-to-all-start.1 = ((bf16[32,12,300]{2,1,0:T(8,128)(2,1)}), bf16[32,12,300]{2,1,0:T(8,128)(2,1)S(1)}, u32[]{:S(2)}, u32[]{:S(2)}) async-start(bf16[32,12,300]{2,1,0:T(8,128)(2,1)} %reshape.147), calls=%async_computation.1 | async-start | bytes 786432 | tf_op jit(solution)/shard_map/all_to_all | solution.py:170
  147.5 477.5 %all-reduce.5.cloned.1.call-start = ((), (), s32[]{:S(2)}) async-start(), calls=%async_computation.3 | async-start | bytes 2555904 | tf_op jit(solution)/shard_map/psum | solution.py:192
  158.6 0.9 copy-start.7
  158.6 0.9 copy-start.9
  165.8 109.6 %all-to-all-start.2 = ((bf16[32,2,450]{2,1,0:T(2,128)(2,1)}), bf16[32,2,450]{2,1,0:T(2,128)(2,1)S(1)}, u32[]{:S(2)}, u32[]{:S(2)}) async-start(bf16[32,2,450]{2,1,0:T(2,128)(2,1)} %reshape.186), calls=%async_computation.2 | async-start | bytes 131072 | tf_op jit(solution)/shard_map/all_to_all | solution.py:183
  625.1 2.3 copy-start.4
Sparse Core Ops, SparseCore 0:
  163.3 461.7 all-reduce.4
where the time goes:
time: 636 us; the launch traced here: 635 us
  waiting for transfers between devices  362 us (57%)
  starting transfers between devices  117 us (18%)
  blocking collectives  106 us (17%)
  local copies, waits for them, and re-layouts  16.8 us (3%)
  between operations  14.8 us (2%)
  other arithmetic  14.4 us (2%)
    psum x1, waiting for transfers between devices, on_device(): lax.psum((grads[0], grads[1], grads[2], grads[3]), ('ocx', 'ocy', 'ml'))  347 us
    psum x1, blocking collectives, on_device(): lax.psum((grads[0], grads[1], grads[2], grads[3]), ('ocx', 'ocy', 'ml'))  106 us
    ppermute x11, starting transfers between devices, padded_2(): after = lax.ppermute(first, axis, down)  68.5 us
    ppermute x12, starting transfers between devices, padded_2(): before = lax.ppermute(last, axis, up)  29.4 us
  transfers between devices with their start and end apart: 27, of which 8 were waited for; matrix products, arithmetic and copies ran while one was open for 3% of the time, Pallas kernels for 0%

commit v1 on v0

v1 whole, which is shorter than its diff:
```python
import jax
import jax.numpy as jnp
from jax import lax
from jax.experimental import pallas as pl
from jax.experimental.pallas import tpu as pltpu
from jax.sharding import PartitionSpec as P

MESH = pl.DeviceIdType.MESH
KAPPA = 0.1
STEPS = 3
LEV = 75
PAD = 80
CX = 4
CY = 128
CELLS = CX * CY
HID = 1024
ROWS = 240
TILES = 32
NZ = 16
COLUMNS = 262144
BLK = 256
F32 = jnp.float32
BF16 = jnp.bfloat16
VMEM_LIMIT = 40 * 1024 * 1024


def place(p):
    return p // 8, p % 8


def faces(opened, speed):
    near = jnp.where(opened, jnp.maximum(speed, 0.0) + KAPPA, 0.0)
    far = jnp.where(opened, jnp.minimum(speed, 0.0) - KAPPA, 0.0)
    return near, far


def transport_kernel(
    tracer_ref, east_ref, north_ref, depth_ref, out_ref,
    cells, side, pack_n, pack_s, halo_w, halo_e, halo_s, halo_n, halo_u,
    send_sems, recv_sems,
):
    z, x, m = lax.axis_index("ocx"), lax.axis_index("ocy"), lax.axis_index("ml")
    p = x * 8 + m
    to_e = (lax.rem(z + 1, NZ), x, m)
    to_w = (lax.rem(z + NZ - 1, NZ), x, m)
    to_n = (z, *place(lax.rem(p + 1, TILES)))
    to_s = (z, *place(lax.rem(p + TILES - 1, TILES)))
    barrier = pltpu.get_barrier_semaphore()
    for target in (to_e, to_w, to_n, to_s):
        pl.semaphore_signal(barrier, inc=1, device_id=target, device_id_type=MESH)

    level = lax.broadcasted_iota(jnp.int32, (PAD, CY), 0).astype(F32)
    lane = lax.broadcasted_iota(jnp.int32, (PAD, CY), 1)
    tail = lax.broadcasted_iota(jnp.int32, (PAD - LEV, CY), 0)
    depth = [depth_ref[i : i + 1, :].astype(F32) for i in range(CX)]
    for i in range(CX):
        cells[0, i, 0:LEV, :] = tracer_ref[:, i, :]
        cells[0, i, LEV:PAD, :] = jnp.where(tail == 0, depth[i], 0.0)
    for i in range(CX):
        side[i, 0:LEV, :] = north_ref[:, i, :]
        side[i, LEV:PAD, :] = jnp.zeros((PAD - LEV, CY), F32)
    side[CX, 0:LEV, :] = east_ref[:, CX - 1, :]
    side[CX, LEV:PAD, :] = jnp.zeros((PAD - LEV, CY), F32)
    pl.semaphore_wait(barrier, 4)

    def remote(src, dst, number, target):
        copy = pltpu.make_async_remote_copy(
            src_ref=src, dst_ref=dst, send_sem=send_sems.at[number], recv_sem=recv_sems.at[number],
            device_id=target, device_id_type=MESH,
        )
        copy.start()
        return copy

    copies = [remote(side.at[CX], halo_u, 12, to_e)]
    coef = None
    for step in range(STEPS):
        rows = [cells[step, i] for i in range(CX)]
        now = [
            remote(cells.at[step, CX - 1], halo_w.at[step], 4 * step, to_e),
            remote(cells.at[step, 0], halo_e.at[step], 4 * step + 1, to_w),
        ]
        up = jnp.zeros((PAD, CY), F32)
        down = jnp.zeros((PAD, CY), F32)
        for i in range(CX):
            up = jnp.where(lane == i, pltpu.roll(rows[i], i + 1, 1), up)
            down = jnp.where(lane == i, pltpu.roll(rows[i], i, 1) if i else rows[i], down)
            if step == 0:
                up = jnp.where(lane == CX + i, pltpu.roll(side[i], CX + i + 1, 1), up)
        pack_n[step] = up
        pack_s[step] = down
        now += [
            remote(pack_n.at[step], halo_s.at[step], 4 * step + 2, to_n),
            remote(pack_s.at[step], halo_n.at[step], 4 * step + 3, to_s),
        ]
        for copy in now:
            copy.wait_recv()
        copies += now
        west, east = halo_w[step], halo_e[step]
        south_pack, north_pack = halo_s[step], halo_n[step]
        south_in = [pltpu.roll(south_pack, (CY - i) % CY, 1) if i else south_pack for i in range(CX)]
        north_in = [pltpu.roll(north_pack, CY - 1 - i, 1) for i in range(CX)]
        if step == 0:
            copies[0].wait_recv()
            deep = [west[LEV : LEV + 1, :]] + depth + [east[LEV : LEV + 1, :]]
            east_faces = []
            for i in range(CX + 1):
                speed = halo_u[...] if i == 0 else None
                if i:
                    speed = jnp.concatenate(
                        [east_ref[:, i - 1, :], jnp.zeros((PAD - LEV, CY), F32)], axis=0
                    ) if i < CX else side[CX]
                east_faces.append(faces(level < jnp.minimum(deep[i], deep[i + 1]), speed))
            coef = []
            for i in range(CX):
                here = jnp.broadcast_to(depth[i], (PAD, CY))
                there = jnp.where(
                    lane == CY - 1,
                    jnp.broadcast_to(north_in[i][LEV : LEV + 1, :], (PAD, CY)),
                    pltpu.roll(here, CY - 1, 1),
                )
                shut_n = jnp.logical_and(lane == CY - 1, p == TILES - 1)
                near_n, far_n = faces(
                    jnp.logical_and(level < jnp.minimum(here, there), jnp.logical_not(shut_n)), side[i]
                )
                below = jnp.broadcast_to(south_in[i][LEV : LEV + 1, :], (PAD, CY))
                near_b, far_b = faces(
                    jnp.logical_and(level < jnp.minimum(here, below), p != 0),
                    pltpu.roll(south_pack, CY - CX - i, 1),
                )
                near_s = jnp.where(lane == 0, near_b, pltpu.roll(near_n, 1, 1))
                far_s = jnp.where(lane == 0, far_b, pltpu.roll(far_n, 1, 1))
                near_w, far_w = east_faces[i]
                near_e, far_e = east_faces[i + 1]
                coef.append((1.0 + far_w - near_e + far_s - near_n, near_w, far_e, near_s, far_n))
        wide = [west] + rows + [east]
        for i in range(CX):
            keep, near_w, far_e, near_s, far_n = coef[i]
            south = jnp.where(lane == 0, south_in[i], pltpu.roll(rows[i], 1, 1))
            north = jnp.where(lane == CY - 1, north_in[i], pltpu.roll(rows[i], CY - 1, 1))
            value = (
                keep * rows[i] + near_w * wide[i] - far_e * wide[i + 2] + near_s * south - far_n * north
            )
            if step == STEPS - 1:
                out_ref[i] = value
            else:
                cells[step + 1, i] = value
    for copy in copies:
        copy.wait_send()


def transport(tracer, east, north, depth):
    vmem = pl.BlockSpec(memory_space=pltpu.VMEM)
    halo = pltpu.VMEM((STEPS, PAD, CY), F32)
    return pl.pallas_call(
        transport_kernel,
        out_shape=jax.ShapeDtypeStruct((CX, PAD, CY), F32),
        in_specs=[vmem] * 4,
        out_specs=vmem,
        scratch_shapes=[
            pltpu.VMEM((STEPS, CX, PAD, CY), F32),
            pltpu.VMEM((CX + 1, PAD, CY), F32),
            halo, halo, halo, halo, halo, halo,
            pltpu.VMEM((PAD, CY), F32),
            pltpu.SemaphoreType.DMA((13,)),
            pltpu.SemaphoreType.DMA((13,)),
        ],
        compiler_params=pltpu.CompilerParams(
            collective_id=0, has_side_effects=True, vmem_limit_bytes=VMEM_LIMIT
        ),
        name="transport",
    )(tracer, east, north, depth)


def dot(a, b, dims):
    return lax.dot_general(a, b, (dims, ((), ())), preferred_element_type=F32)


def closure_kernel(
    moved_ref, east_ref, north_ref, target_ref, depth_ref, w1_ref, b1_ref, w2_ref, b2_ref,
    tracer_out, misfit_out, chunks,
    feat, weights, hidden, slope, total, wanted,
):
    level = lax.broadcasted_iota(jnp.int32, (LEV, CY), 0).astype(F32)
    masks = []
    want = target_ref[...].astype(F32)
    wanted[...] = want
    for i in range(CX):
        at = slice(CY * i, CY * (i + 1))
        mask = level < depth_ref[i : i + 1, :].astype(F32)
        masks.append(mask)
        feat[0:LEV, at] = jnp.where(mask, moved_ref[i, 0:LEV, :], 0.0)
        feat[LEV : 2 * LEV, at] = jnp.where(mask, east_ref[:, i, :], 0.0)
        feat[2 * LEV : 3 * LEV, at] = jnp.where(mask, north_ref[:, i, :], 0.0)
    last = lax.broadcasted_iota(jnp.int32, (ROWS - 3 * LEV, CELLS), 0)
    feat[3 * LEV : ROWS, :] = jnp.where(last < 2, 1.0, 0.0)
    inputs = feat[...].astype(BF16)

    edge = 3 * LEV // 16 * 16
    weights[0:edge, :] = w1_ref[0:edge, :]
    bias = b1_ref[...]
    coarse = bias.astype(BF16).astype(F32)
    row = lax.broadcasted_iota(jnp.int32, (ROWS - edge, HID), 0) + edge
    final = jnp.where(row == 3 * LEV - 1, w1_ref[3 * LEV - 1 : 3 * LEV, :].astype(F32), 0.0)
    final = jnp.where(row == 3 * LEV, coarse, final)
    final = jnp.where(row == 3 * LEV + 1, bias - coarse, final)
    weights[edge:ROWS, :] = final.astype(BF16)

    acc = None
    for b in range(HID // BLK):
        at = slice(b * BLK, (b + 1) * BLK)
        before = dot(weights[:, at], inputs, ((0,), (0,)))
        stash = before.astype(BF16).astype(F32)
        gate = 0.5 * jnp.tanh(0.5 * stash) + 0.5
        act = (stash * gate).astype(BF16)
        hidden[at, :] = act
        slope[at, :] = gate * (1.0 + stash * (1.0 - gate))
        part = dot(w2_ref[at, :], act, ((0,), (0,)))
        acc = part if acc is None else acc + part
    eye = lax.broadcasted_iota(jnp.int32, (LEV, LEV), 0) == lax.broadcasted_iota(jnp.int32, (LEV, LEV), 1)
    bias2 = jnp.sum(jnp.where(eye, b2_ref[...], 0.0), axis=1, keepdims=True)
    output = acc + bias2
    total[...] = jnp.zeros((PAD, CELLS), F32)
    for i in range(CX):
        at = slice(CY * i, CY * (i + 1))
        tendency = jnp.where(masks[i], output[:, at], 0.0).astype(BF16).astype(F32)
        goal = jnp.where(masks[i], wanted[:, i, :], 0.0)
        misfit = tendency - goal
        total[0:LEV, at] = misfit * (1.0 / COLUMNS)
        tracer_out[:, i, :] = moved_ref[i, 0:LEV, :] + tendency
        wanted[:, i, :] = misfit
    misfit_out[...] = wanted[...].astype(BF16)
    d_out = total[...].astype(BF16)
    ones = jnp.ones((16, CELLS), BF16)
    bias_grad = dot(ones, d_out, ((1,), (1,)))
    spread = lax.broadcasted_iota(jnp.int32, (PAD, CY), 0) == LEV
    for b in range(HID // BLK):
        at = slice(b * BLK, (b + 1) * BLK)
        d_hidden = dot(w2_ref[at, :], d_out[0:LEV, :], ((1,), (0,)))
        d_before = (d_hidden * slope[at, :]).astype(BF16)
        g1 = dot(inputs, d_before, ((1,), (1,)))
        g2 = dot(d_out, hidden[at, :], ((1,), (1,)))
        for t in range(BLK // CY):
            lanes = slice(t * CY, (t + 1) * CY)
            first = 4 * (b * (BLK // CY) + t)
            for g in range(3):
                chunks[first + g] = g1[PAD * g : PAD * (g + 1), lanes].astype(BF16)
            last_part = g2[:, lanes]
            if first == 0:
                row = jnp.concatenate([bias_grad[0:1, :], jnp.zeros((1, CY - PAD), F32)], axis=1)
                last_part = jnp.where(spread, row, last_part)
            chunks[first + 3] = last_part.astype(BF16)


def closure(moved, east, north, target, depth, w1, b1, w2, b2):
    vmem = pl.BlockSpec(memory_space=pltpu.VMEM)
    return pl.pallas_call(
        closure_kernel,
        out_shape=(
            jax.ShapeDtypeStruct((LEV, CX, CY), F32),
            jax.ShapeDtypeStruct((LEV, CX, CY), BF16),
            jax.ShapeDtypeStruct((TILES, PAD, CY), BF16),
        ),
        in_specs=[vmem] * 9,
        out_specs=(vmem,) * 3,
        scratch_shapes=[
            pltpu.VMEM((ROWS, CELLS), F32),
            pltpu.VMEM((ROWS, HID), BF16),
            pltpu.VMEM((HID, CELLS), BF16),
            pltpu.VMEM((HID, CELLS), F32),
            pltpu.VMEM((PAD, CELLS), F32),
            pltpu.VMEM((LEV, CX, CY), F32),
        ],
        compiler_params=pltpu.CompilerParams(vmem_limit_bytes=VMEM_LIMIT),
        name="closure",
    )(moved, east, north, target, depth, w1, b1.reshape(1, HID), w2, b2.reshape(1, LEV))


def reduce_kernel(
    chunks, out_ref, landed, strips, strips_in, mine, strips_all, chunk, send_sems, recv_sems
):
    z, x, m = lax.axis_index("ocx"), lax.axis_index("ocy"), lax.axis_index("ml")
    p = x * 8 + m
    barrier = pltpu.get_barrier_semaphore()

    def member(k):
        q = lax.rem(p + k, TILES)
        return q, (z, *place(q))

    def ring(k):
        w = lax.rem(z + k, NZ)
        return w, (w, x, m)

    def greet(k, carry):
        pl.semaphore_signal(barrier, inc=1, device_id=member(k)[1], device_id_type=MESH)
        return carry

    def greet_ring(k, carry):
        pl.semaphore_signal(barrier, inc=1, device_id=ring(k)[1], device_id_type=MESH)
        return carry

    lax.fori_loop(1, TILES, greet, 0)
    lax.fori_loop(1, NZ, greet_ring, 0)
    pl.semaphore_wait(barrier, TILES + NZ - 2)

    def remote(src, dst, number, target):
        return pltpu.make_async_remote_copy(
            src_ref=src, dst_ref=dst, send_sem=send_sems.at[number], recv_sem=recv_sems.at[number],
            device_id=target, device_id_type=MESH,
        )

    def scatter(k, carry):
        q, target = member(k)
        remote(chunks.at[q], landed.at[k - 1], 0, target).start()
        return carry

    lax.fori_loop(1, TILES, scatter, 0)
    remote(landed, landed, 0, ring(1)[1]).wait_recv()
    total = chunks[p].astype(F32)
    total = lax.fori_loop(0, TILES - 1, lambda k, s: s + landed[k].astype(F32), total)
    mine[...] = total
    part = PAD // NZ
    for k in range(NZ):
        strips[k] = mine[part * k : part * (k + 1), :]

    def scatter_ring(k, carry):
        w, target = ring(k)
        remote(strips.at[w], strips_in.at[k - 1], 1, target).start()
        return carry

    lax.fori_loop(1, NZ, scatter_ring, 0)
    remote(strips_in, strips_in, 1, ring(1)[1]).wait_recv()
    strip = strips[z]
    for k in range(NZ - 1):
        strip = strip + strips_in[k]
    strips_all[NZ - 1] = strip

    def gather_ring(k, carry):
        _, target = ring(k)
        remote(strips_all.at[NZ - 1], strips_all.at[k - 1], 2, target).start()
        return carry

    lax.fori_loop(1, NZ, gather_ring, 0)
    arrived = strips_all.at[0 : NZ - 1]
    remote(arrived, arrived, 2, ring(1)[1]).wait_recv()
    for k in range(NZ):
        place_in = lax.rem(z - k + NZ - 1 + NZ, NZ)
        mine[part * k : part * (k + 1), :] = strips_all[place_in]
    chunk[...] = mine[...].astype(BF16)
    out_ref[p] = chunk[...]

    def gather(k, carry):
        _, target = member(k)
        remote(chunk, out_ref.at[p], 3, target).start()
        return carry

    lax.fori_loop(1, TILES, gather, 0)
    remote(landed, landed, 3, ring(1)[1]).wait_recv()
    remote(landed, landed, 0, ring(1)[1]).wait_send()
    remote(strips_in, strips_in, 1, ring(1)[1]).wait_send()
    remote(arrived, arrived, 2, ring(1)[1]).wait_send()
    remote(landed, landed, 3, ring(1)[1]).wait_send()


def reduce(chunks):
    vmem = pl.BlockSpec(memory_space=pltpu.VMEM)
    part = PAD // NZ
    return pl.pallas_call(
        reduce_kernel,
        out_shape=jax.ShapeDtypeStruct((TILES, PAD, CY), BF16),
        in_specs=[vmem],
        out_specs=vmem,
        scratch_shapes=[
            pltpu.VMEM((TILES - 1, PAD, CY), BF16),
            pltpu.VMEM((NZ, part, CY), F32),
            pltpu.VMEM((NZ - 1, part, CY), F32),
            pltpu.VMEM((PAD, CY), F32),
            pltpu.VMEM((NZ, part, CY), F32),
            pltpu.VMEM((PAD, CY), BF16),
            pltpu.SemaphoreType.DMA((4,)),
            pltpu.SemaphoreType.DMA((4,)),
        ],
        compiler_params=pltpu.CompilerParams(
            collective_id=1, has_side_effects=True, vmem_limit_bytes=VMEM_LIMIT
        ),
        name="reduce",
    )(chunks)


def unpack_kernel(chunks, w1_ref, b1_ref, w2_ref, b2_ref):
    for t in range(HID // CY):
        lanes = slice(t * CY, (t + 1) * CY)
        for g in range(2):
            w1_ref[PAD * g : PAD * (g + 1), lanes] = chunks[4 * t + g].astype(F32)
        third = chunks[4 * t + 2].astype(F32)
        rest = 3 * LEV - 2 * PAD
        w1_ref[2 * PAD : 3 * LEV, lanes] = third[0:rest, :]
        b1_ref[:, lanes] = third[rest : rest + 1, :]
        fourth = chunks[4 * t + 3].astype(F32)
        w2_ref[lanes, :] = jnp.transpose(fourth)[:, 0:LEV]
        if t == 0:
            b2_ref[...] = fourth[LEV : LEV + 1, 0:LEV]


def unpack(chunks):
    vmem = pl.BlockSpec(memory_space=pltpu.VMEM)
    return pl.pallas_call(
        unpack_kernel,
        out_shape=(
            jax.ShapeDtypeStruct((3 * LEV, HID), F32),
            jax.ShapeDtypeStruct((1, HID), F32),
            jax.ShapeDtypeStruct((HID, LEV), F32),
            jax.ShapeDtypeStruct((1, LEV), F32),
        ),
        in_specs=[vmem],
        out_specs=(vmem,) * 4,
        compiler_params=pltpu.CompilerParams(vmem_limit_bytes=VMEM_LIMIT),
        name="unpack",
    )(chunks)


def on_device(tracer, east, north, target, depth, slots, w1, b1, w2, b2):
    moved = transport(tracer, east, north, depth)
    tracer_out, misfit_out, chunks = closure(moved, east, north, target, depth, w1, b1, w2, b2)
    grad_w1, grad_b1, grad_w2, grad_b2 = unpack(reduce(chunks))
    return tracer_out, misfit_out, grad_w1, grad_b1.reshape(HID), grad_w2, grad_b2.reshape(LEV)


def solution(mesh):
    grid = P(None, "ocx", ("ocy", "ml"))
    return jax.shard_map(
        on_device,
        mesh=mesh,
        in_specs=(grid, grid, grid, grid, P("ocx", ("ocy", "ml")), P("ocx", ("ocy", "ml"), None, None), P(), P(), P(), P()),
        out_specs=(grid, grid, P(), P(), P(), P()),
        check_vma=False,
    )
```

time: 636 us -> 77.4 us (0.12)
  waiting for transfers between devices: 362 us -> 0 us
  starting transfers between devices: 117 us -> 0 us
  blocking collectives: 106 us -> 0 us
  Pallas kernels: 0 us -> 70.9 us
  other arithmetic: 14.4 us -> 0 us
  between operations: 14.8 us -> 0.76 us
  local copies, waits for them, and re-layouts: 16.8 us -> 5.55 us
    psum x1 -> x0, waiting for transfers between devices: 347 us -> none  [on_device(): lax.psum((grads[0], grads[1], grads[2], grads[3]), ('ocx', 'ocy', 'ml'))]
    psum x1 -> x0, blocking collectives: 106 us -> none  [on_device(): lax.psum((grads[0], grads[1], grads[2], grads[3]), ('ocx', 'ocy', 'ml'))]
    ppermute x23 -> x0, starting transfers between devices: 97.9 us -> none  [the longest x11 68.5 us: padded_2(): after = lax.ppermute(first, axis, down)]
    pallas_call x0 -> x4, Pallas kernels: none -> 70.9 us  [the longest x1 42.7 us: reduce(): pl.pallas_call(reduce_kernel, out_shape=jax.ShapeDtypeStruct((TILES, PAD,...]
    all_to_all x3 -> x0, starting transfers between devices: 19.5 us -> none  [the longest x1 8.54 us: on_device(): lax.all_to_all(depth_out, ('ocy', 'ml'), split_axis=0, concat_axis=0, til...]
    all_to_all x3 -> x0, waiting for transfers between devices: 10.4 us -> none  [the longest x1 10.1 us: on_device(): lax.all_to_all(outgoing, ('ocy', 'ml'), split_axis=0, concat_axis=0, tile...]
  transfers between devices with their start and end apart: 27 -> 0, of which waited for: 8 -> 0; matrix products, arithmetic and copies ran while one was open for 3% -> 0% of each run, Pallas kernels for 0% -> 0%
where the time goes in v1:
time: 77.4 us; the launch traced here: 77.2 us
  Pallas kernels  70.9 us (92%)
  local copies, waits for them, and re-layouts  5.55 us (7%)
    pallas_call x1, Pallas kernels, reduce(): pl.pallas_call(reduce_kernel, out_shape=jax.ShapeDtypeStruct((TILES, PAD,...  42.7 us
    pallas_call x1, Pallas kernels, transport(): pl.pallas_call(transport_kernel, out_shape=jax.ShapeDtypeStruct((CX, PAD,...  24 us
    unnamed x22, local copies, waits for them, and re-layouts  5.55 us
    pallas_call x1, Pallas kernels, closure(): pl.pallas_call(closure_kernel, out_shape=(jax.ShapeDtypeStruct((LEV, CX,...  3.03 us

profile of v1, /device:TPU:1, one launch (start us, length us, event | category | flops | bytes accessed | tf_op | source)
XLA Modules:
  0.0 77.2 jit_solution(13314334040554408890)
XLA Ops:
  0.6 0.0 copy-start.7
  0.6 0.7 copy-done.7
  1.3 0.0 copy-start
  1.3 0.9 %copy-done = f32[75,4,128]{2,1,0:T(4,128)S(1)} copy-done((f32[75,4,128]{2,1,0:T(4,128)S(1)}, f32[75,4,128]{2,1,0:T(4,128)}, u32[]{:S(2)}) %copy-start) | copy-done | bytes 153624
  2.2 0.0 copy-start.2
  2.2 0.9 %copy-done.2 = f32[75,4,128]{2,1,0:T(4,128)S(1)} copy-done((f32[75,4,128]{2,1,0:T(4,128)S(1)}, f32[75,4,128]{2,1,0:T(4,128)}, u32[]{:S(2)}) %copy-start.2) | copy-done | bytes 153624
  3.1 0.0 copy-start.5
  3.1 0.9 %copy-done.5 = f32[75,4,128]{2,1,0:T(4,128)S(1)} copy-done((f32[75,4,128]{2,1,0:T(4,128)S(1)}, f32[75,4,128]{2,1,0:T(4,128)}, u32[]{:S(2)}) %copy-start.5) | copy-done | bytes 153624
  4.1 0.0 copy-start.4
  4.1 24.0 %transport.1.moved_ref = f32[4,80,128]{2,1,0:T(8,128)S(1)} custom-call(f32[75,4,128]{2,1,0:T(4,128)S(1)} %copy-done.5, f32[75,4,128]{2,1,0:T(4,128)S(1)} %copy-done, f32[75,4,128]{2,1,0:T(4,128)S(1)} %copy-done.2, s32[4,128]{1,0:T(4,128)S(1)} %copy-done.7), custom_call_target="tpu_custom_call" | custom-call | tf_op jit(solution)/shard_map/transport/pallas_call | solution.py:154
  28.0 0.0 copy-start.1
  28.1 0.0 copy-start.3
  28.1 0.0 copy-start.6
  28.1 0.0 copy-start.8
  28.1 0.0 copy-start.9
  28.1 1.2 %copy.15.w2_ref = bf16[1024,75]{1,0:T(8,128)(2,1)S(1)} copy(bf16[1024,75]{0,1:T(8,128)(2,1)} %param.17) | data formatting | bytes 307200 | tf_op args[8]
  29.3 0.0 copy-done.4
  29.3 0.0 copy-done.1
  29.3 0.0 copy-done.3
  29.3 0.0 copy-done.6
  29.3 0.0 copy-done.8
  29.3 0.0 copy-done.9
  29.3 3.0 %closure.1 = (f32[75,4,128]{2,1,0:T(4,128)}, bf16[75,4,128]{2,1,0:T(4,128)(2,1)}, bf16[32,80,128]{2,1,0:T(8,128)(2,1)S(1)}) custom-call(f32[4,80,128]{2,1,0:T(8,128)S(1)} %transport.1.moved_ref, f32[75,4,128]{2,1,0:T(4,128)S(1)} %copy-done.1, f32[75,4,128]{2,1,0:T(4,128)S(1)} %copy-done.3, bf16[75,4,128]{2,1,0:T(4,128)(2,1)S(1)} %copy-done.6, ...), custom_call_target="tpu_custom_call" | custom-call | tf_op jit(solution)/shard_map/closure/pallas_call | solution.py:256
  32.4 42.7 %reduce.1.chunks = bf16[32,80,128]{2,1,0:T(8,128)(2,1)S(1)} custom-call(bf16[32,80,128]{2,1,0:T(8,128)(2,1)S(1)} %get-tuple-element.15.chunks), custom_call_target="tpu_custom_call" | custom-call | tf_op jit(solution)/shard_map/reduce/pallas_call | solution.py:367
  75.1 1.1 %unpack.1 = (f32[225,1024]{1,0:T(8,128)}, f32[1,1024]{1,0:T(1,128)}, f32[1024,75]{1,0:T(8,128)S(1)}, f32[1,75]{1,0:T(1,128)}) custom-call(bf16[32,80,128]{2,1,0:T(8,128)(2,1)S(1)} %reduce.1.chunks), custom_call_target="tpu_custom_call" | custom-call | tf_op jit(solution)/shard_map/unpack/pallas_call | solution.py:406
  76.3 0.9 %copy.16 = f32[1024,75]{0,1:T(8,128)} copy(f32[1024,75]{1,0:T(8,128)S(1)} %get-tuple-element.24) | data formatting | bytes 614400
Async XLA Ops:
  0.6 0.7 copy-start.7
  1.3 0.9 %copy-start = (f32[75,4,128]{2,1,0:T(4,128)S(1)}, f32[75,4,128]{2,1,0:T(4,128)}, u32[]{:S(2)}) copy-start(f32[75,4,128]{2,1,0:T(4,128)} %east_ref.3) | copy-start | bytes 460804
  2.2 0.9 %copy-start.2 = (f32[75,4,128]{2,1,0:T(4,128)S(1)}, f32[75,4,128]{2,1,0:T(4,128)}, u32[]{:S(2)}) copy-start(f32[75,4,128]{2,1,0:T(4,128)} %north_ref.3) | copy-start | bytes 460804
  3.1 0.9 %copy-start.5 = (f32[75,4,128]{2,1,0:T(4,128)S(1)}, f32[75,4,128]{2,1,0:T(4,128)}, u32[]{:S(2)}) copy-start(f32[75,4,128]{2,1,0:T(4,128)} %tracer_ref.1) | copy-start | bytes 460804
  4.1 25.2 %copy-start.4 = (bf16[225,1024]{1,0:T(8,128)(2,1)S(1)}, bf16[225,1024]{1,0:T(8,128)(2,1)}, u32[]{:S(2)}) copy-start(bf16[225,1024]{1,0:T(8,128)(2,1)} %w1_ref.1) | copy-start | bytes 1382404
  28.0 1.3 %copy-start.1 = (f32[75,4,128]{2,1,0:T(4,128)S(1)}, f32[75,4,128]{2,1,0:T(4,128)}, u32[]{:S(2)}) copy-start(f32[75,4,128]{2,1,0:T(4,128)} %east_ref.3) | copy-start | bytes 460804
  28.1 1.3 %copy-start.3 = (f32[75,4,128]{2,1,0:T(4,128)S(1)}, f32[75,4,128]{2,1,0:T(4,128)}, u32[]{:S(2)}) copy-start(f32[75,4,128]{2,1,0:T(4,128)} %north_ref.3) | copy-start | bytes 460804
  28.1 1.2 %copy-start.6 = (bf16[75,4,128]{2,1,0:T(4,128)(2,1)S(1)}, bf16[75,4,128]{2,1,0:T(4,128)(2,1)}, u32[]{:S(2)}) copy-start(bf16[75,4,128]{2,1,0:T(4,128)(2,1)} %target_ref.1) | copy-start | bytes 230404
  28.1 1.2 %copy-start.8 = (f32[1024]{0:T(1024)S(1)}, f32[1024]{0:T(1024)}, u32[]{:S(2)}) copy-start(f32[1024]{0:T(1024)} %param.16) | copy-start | bytes 12292
  28.1 1.2 %copy-start.9 = (f32[75]{0:T(128)S(1)}, f32[75]{0:T(128)}, u32[]{:S(2)}) copy-start(f32[75]{0:T(128)} %param.18) | copy-start | bytes 904

commit v2 on v1

--- a/solution.py
+++ b/solution.py
@@ -17,6 +17,7 @@
 ROWS = 240
 TILES = 32
 NZ = 16
+CHIPS = 16
 COLUMNS = 262144
 BLK = 256
 F32 = jnp.float32
@@ -177,9 +178,52 @@
 
 def closure_kernel(
     moved_ref, east_ref, north_ref, target_ref, depth_ref, w1_ref, b1_ref, w2_ref, b2_ref,
-    tracer_out, misfit_out, chunks,
-    feat, weights, hidden, slope, total, wanted,
+    tendency_out, misfit_out, gathered,
+    feat, weights, hidden, slope, total, wanted, chunks, core_in, summed, sending, landed,
+    mine, strips, strips_in, strips_all, chunk, core_send, core_recv, send_sems, recv_sems,
 ):
+    z, x, m = lax.axis_index("ocx"), lax.axis_index("ocy"), lax.axis_index("ml")
+    core = lax.rem(m, 2)
+    chip = x * 4 + m // 2
+    sibling = (z, x, m + 1 - 2 * core)
+    barrier = pltpu.get_barrier_semaphore()
+
+    def other_chip(k):
+        c = lax.rem(chip + k, CHIPS)
+        return c, (z, c // 4, (c % 4) * 2 + core)
+
+    def ring(k):
+        w = lax.rem(z + k, NZ)
+        return w, (w, x, m)
+
+    def far_first(j):
+        half = (j + 1) // 2
+        return NZ // 2 + half * (1 - 2 * lax.rem(j, 2))
+
+    def signal(target):
+        pl.semaphore_signal(barrier, inc=1, device_id=target, device_id_type=MESH)
+
+    def greet_ring(j, carry):
+        signal(ring(far_first(j))[1])
+        return carry
+
+    def greet_chips(k, carry):
+        signal(other_chip(k)[1])
+        return carry
+
+    lax.fori_loop(0, NZ - 1, greet_ring, 0)
+    lax.fori_loop(1, CHIPS, greet_chips, 0)
+    signal(sibling)
+
+    def remote(src, dst, send_sem, recv_sem, target):
+        return pltpu.make_async_remote_copy(
+            src_ref=src, dst_ref=dst, send_sem=send_sem, recv_sem=recv_sem,
+            device_id=target, device_id_type=MESH,
+        )
+
+    def whole(ref, number):
+        return remote(ref, ref, send_sems.at[number], recv_sems.at[number], sibling)
+
     level = lax.broadcasted_iota(jnp.int32, (LEV, CY), 0).astype(F32)
     masks = []
     want = target_ref[...].astype(F32)
@@ -214,7 +258,7 @@
         act = (stash * gate).astype(BF16)
         hidden[at, :] = act
         slope[at, :] = gate * (1.0 + stash * (1.0 - gate))
-        part = dot(w2_ref[at, :], act, ((0,), (0,)))
+        part = dot(w2_ref[:, at], act, ((1,), (0,)))
         acc = part if acc is None else acc + part
     eye = lax.broadcasted_iota(jnp.int32, (LEV, LEV), 0) == lax.broadcasted_iota(jnp.int32, (LEV, LEV), 1)
     bias2 = jnp.sum(jnp.where(eye, b2_ref[...], 0.0), axis=1, keepdims=True)
@@ -226,39 +270,130 @@
         goal = jnp.where(masks[i], wanted[:, i, :], 0.0)
         misfit = tendency - goal
         total[0:LEV, at] = misfit * (1.0 / COLUMNS)
-        tracer_out[:, i, :] = moved_ref[i, 0:LEV, :] + tendency
-        wanted[:, i, :] = misfit
-    misfit_out[...] = wanted[...].astype(BF16)
+        tendency_out[i, 0:LEV, :] = tendency
+        misfit_out[i, 0:LEV, :] = misfit
     d_out = total[...].astype(BF16)
     ones = jnp.ones((16, CELLS), BF16)
     bias_grad = dot(ones, d_out, ((1,), (1,)))
     spread = lax.broadcasted_iota(jnp.int32, (PAD, CY), 0) == LEV
+    per = BLK // CY
+    to_sibling = []
     for b in range(HID // BLK):
         at = slice(b * BLK, (b + 1) * BLK)
-        d_hidden = dot(w2_ref[at, :], d_out[0:LEV, :], ((1,), (0,)))
+        d_hidden = dot(w2_ref[:, at], d_out[0:LEV, :], ((0,), (0,)))
         d_before = (d_hidden * slope[at, :]).astype(BF16)
         g1 = dot(inputs, d_before, ((1,), (1,)))
         g2 = dot(d_out, hidden[at, :], ((1,), (1,)))
-        for t in range(BLK // CY):
+        for t in range(per):
             lanes = slice(t * CY, (t + 1) * CY)
-            first = 4 * (b * (BLK // CY) + t)
+            tile = b * per + t
             for g in range(3):
-                chunks[first + g] = g1[PAD * g : PAD * (g + 1), lanes].astype(BF16)
+                chunks[g % 2, 2 * tile + g // 2] = g1[PAD * g : PAD * (g + 1), lanes]
             last_part = g2[:, lanes]
-            if first == 0:
+            if tile == 0:
                 row = jnp.concatenate([bias_grad[0:1, :], jnp.zeros((1, CY - PAD), F32)], axis=1)
                 last_part = jnp.where(spread, row, last_part)
-            chunks[first + 3] = last_part.astype(BF16)
+            chunks[1, 2 * tile + 1] = last_part
+        if b == 0:
+            pl.semaphore_wait(barrier, NZ - 1 + CHIPS - 1 + 1)
+        some = pl.ds(2 * per * b, 2 * per)
+        copy = remote(chunks.at[1 - core, some], core_in.at[some], core_send.at[b], core_recv.at[b], sibling)
+        copy.start()
+        to_sibling.append(copy)
+    row = lax.broadcasted_iota(jnp.int32, (PAD, CY), 0)
+    bias_row = 3 * LEV - 2 * PAD + core * (LEV - (3 * LEV - 2 * PAD))
+    for b in range(HID // BLK):
+        to_sibling[b].wait_recv()
+        some = pl.ds(2 * per * b, 2 * per)
+        both = chunks[core, some] + core_in[some]
+        for j in range(2 * per):
+            value = both[j]
+            sent = value
+            if j % 2:
+                low = value - value.astype(BF16).astype(F32)
+                value = jnp.where(row == bias_row + 1, 0.0, value)
+                sent = jnp.where(row == bias_row + 1, pltpu.roll(low, 1, 0), value)
+            summed[2 * per * b + j] = value
+            sending[2 * per * b + j] = sent.astype(BF16)
+
+    def scatter(k, carry):
+        c, target = other_chip(k)
+        remote(sending.at[c], landed.at[k - 1], send_sems.at[0], recv_sems.at[0], target).start()
+        return carry
+
+    lax.fori_loop(1, CHIPS, scatter, 0)
+    whole(landed, 0).wait_recv()
+    amount = summed[chip]
+    for k in range(CHIPS - 1):
+        amount = amount + landed[k].astype(F32)
+    mine[...] = amount
+    part = PAD // NZ
+    for k in range(NZ):
+        strips[k] = mine[part * k : part * (k + 1), :]
+
+    def scatter_ring(j, carry):
+        k = far_first(j)
+        w, target = ring(k)
+        remote(strips.at[w], strips_in.at[k - 1], send_sems.at[1], recv_sems.at[1], target).start()
+        return carry
+
+    lax.fori_loop(0, NZ - 1, scatter_ring, 0)
+    whole(strips_in, 1).wait_recv()
+    strip = strips[z]
+    for k in range(NZ - 1):
+        strip = strip + strips_in[k]
+    strips_all[NZ - 1] = strip
+
+    def gather_ring(j, carry):
+        k = far_first(j)
+        _, target = ring(k)
+        remote(
+            strips_all.at[NZ - 1], strips_all.at[k - 1], send_sems.at[2], recv_sems.at[2], target
+        ).start()
+        return carry
+
+    lax.fori_loop(0, NZ - 1, gather_ring, 0)
+    arrived = strips_all.at[0 : NZ - 1]
+    whole(arrived, 2).wait_recv()
+    for k in range(NZ):
+        place_in = lax.rem(z - k + NZ - 1 + NZ, NZ)
+        mine[part * k : part * (k + 1), :] = strips_all[place_in]
+    has_bias = lax.rem(chip, 2) == 1
+    value = mine[...]
+    both = jnp.where(jnp.logical_and(row == bias_row, has_bias), pltpu.roll(value, PAD - 1, 0), 0.0) + value
+    low = both - both.astype(BF16).astype(F32)
+    both = jnp.where(jnp.logical_and(row == bias_row + 1, has_bias), pltpu.roll(low, 1, 0), both)
+    chunk[...] = both.astype(BF16)
+    gathered[core, chip] = chunk[...]
+
+    def gather(k, carry):
+        _, target = other_chip(k)
+        remote(chunk, gathered.at[core, chip], send_sems.at[3], recv_sems.at[3], target).start()
+        return carry
+
+    lax.fori_loop(1, CHIPS, gather, 0)
+    whole(landed, 3).wait_recv()
+    forward = remote(gathered.at[core], gathered.at[core], send_sems.at[4], recv_sems.at[4], sibling)
+    forward.start()
+    for copy in to_sibling:
+        copy.wait_send()
+    whole(landed, 0).wait_send()
+    whole(strips_in, 1).wait_send()
+    whole(arrived, 2).wait_send()
+    whole(landed, 3).wait_send()
+    forward.wait()
 
 
 def closure(moved, east, north, target, depth, w1, b1, w2, b2):
     vmem = pl.BlockSpec(memory_space=pltpu.VMEM)
+    part = PAD // NZ
+    halves = HID // BLK
     return pl.pallas_call(
         closure_kernel,
         out_shape=(
-            jax.ShapeDtypeStruct((LEV, CX, CY), F32),
-            jax.ShapeDtypeStruct((LEV, CX, CY), BF16),
-            jax.ShapeDtypeStruct((TILES, PAD, CY), BF16),
+            jax.ShapeDtypeStruct((CX, PAD, CY), F32),
+            jax.ShapeDtypeStruct((CX, PAD, CY), F32),
+            jax.ShapeDtypeStruct((2, CHIPS, PAD, CY), BF16),
         ),
         in_specs=[vmem] * 9,
         out_specs=(vmem,) * 3,
@@ -269,160 +404,72 @@
             pltpu.VMEM((HID, CELLS), F32),
             pltpu.VMEM((PAD, CELLS), F32),
             pltpu.VMEM((LEV, CX, CY), F32),
-        ],
-        compiler_params=pltpu.CompilerParams(vmem_limit_bytes=VMEM_LIMIT),
-        name="closure",
-    )(moved, east, north, target, depth, w1, b1.reshape(1, HID), w2, b2.reshape(1, LEV))
-
-
-def reduce_kernel(
-    chunks, out_ref, landed, strips, strips_in, mine, strips_all, chunk, send_sems, recv_sems
-):
-    z, x, m = lax.axis_index("ocx"), lax.axis_index("ocy"), lax.axis_index("ml")
-    p = x * 8 + m
-    barrier = pltpu.get_barrier_semaphore()
-
-    def member(k):
-        q = lax.rem(p + k, TILES)
-        return q, (z, *place(q))
-
-    def ring(k):
-        w = lax.rem(z + k, NZ)
-        return w, (w, x, m)
-
-    def greet(k, carry):
-        pl.semaphore_signal(barrier, inc=1, device_id=member(k)[1], device_id_type=MESH)
-        return carry
-
-    def greet_ring(k, carry):
-        pl.semaphore_signal(barrier, inc=1, device_id=ring(k)[1], device_id_type=MESH)
-        return carry
-
-    lax.fori_loop(1, TILES, greet, 0)
-    lax.fori_loop(1, NZ, greet_ring, 0)
-    pl.semaphore_wait(barrier, TILES + NZ - 2)
-
-    def remote(src, dst, number, target):
-        return pltpu.make_async_remote_copy(
-            src_ref=src, dst_ref=dst, send_sem=send_sems.at[number], recv_sem=recv_sems.at[number],
-            device_id=target, device_id_type=MESH,
-        )
-
-    def scatter(k, carry):
-        q, target = member(k)
-        remote(chunks.at[q], landed.at[k - 1], 0, target).start()
-        return carry
-
-    lax.fori_loop(1, TILES, scatter, 0)
-    remote(landed, landed, 0, ring(1)[1]).wait_recv()
-    total = chunks[p].astype(F32)
-    total = lax.fori_loop(0, TILES - 1, lambda k, s: s + landed[k].astype(F32), total)
-    mine[...] = total
-    part = PAD // NZ
-    for k in range(NZ):
-        strips[k] = mine[part * k : part * (k + 1), :]
-
-    def scatter_ring(k, carry):
-        w, target = ring(k)
-        remote(strips.at[w], strips_in.at[k - 1], 1, target).start()
-        return carry
-
-    lax.fori_loop(1, NZ, scatter_ring, 0)
-    remote(strips_in, strips_in, 1, ring(1)[1]).wait_recv()
-    strip = strips[z]
-    for k in range(NZ - 1):
-        strip = strip + strips_in[k]
-    strips_all[NZ - 1] = strip
-
-    def gather_ring(k, carry):
-        _, target = ring(k)
-        remote(strips_all.at[NZ - 1], strips_all.at[k - 1], 2, target).start()
-        return carry
-
-    lax.fori_loop(1, NZ, gather_ring, 0)
-    arrived = strips_all.at[0 : NZ - 1]
-    remote(arrived, arrived, 2, ring(1)[1]).wait_recv()
-    for k in range(NZ):
-        place_in = lax.rem(z - k + NZ - 1 + NZ, NZ)
-        mine[part * k : part * (k + 1), :] = strips_all[place_in]
-    chunk[...] = mine[...].astype(BF16)
-    out_ref[p] = chunk[...]
-
-    def gather(k, carry):
-        _, target = member(k)
-        remote(chunk, out_ref.at[p], 3, target).start()
-        return carry
-
-    lax.fori_loop(1, TILES, gather, 0)
-    remote(landed, landed, 3, ring(1)[1]).wait_recv()
-    remote(landed, landed, 0, ring(1)[1]).wait_send()
-    remote(strips_in, strips_in, 1, ring(1)[1]).wait_send()
-    remote(arrived, arrived, 2, ring(1)[1]).wait_send()
-    remote(landed, landed, 3, ring(1)[1]).wait_send()
-
-
-def reduce(chunks):
-    vmem = pl.BlockSpec(memory_space=pltpu.VMEM)
-    part = PAD // NZ
-    return pl.pallas_call(
-        reduce_kernel,
-        out_shape=jax.ShapeDtypeStruct((TILES, PAD, CY), BF16),
-        in_specs=[vmem],
-        out_specs=vmem,
-        scratch_shapes=[
-            pltpu.VMEM((TILES - 1, PAD, CY), BF16),
+            pltpu.VMEM((2, CHIPS, PAD, CY), F32),
+            pltpu.VMEM((CHIPS, PAD, CY), F32),
+            pltpu.VMEM((CHIPS, PAD, CY), F32),
+            pltpu.VMEM((CHIPS, PAD, CY), BF16),
+            pltpu.VMEM((CHIPS - 1, PAD, CY), BF16),
+            pltpu.VMEM((PAD, CY), F32),
             pltpu.VMEM((NZ, part, CY), F32),
             pltpu.VMEM((NZ - 1, part, CY), F32),
-            pltpu.VMEM((PAD, CY), F32),
             pltpu.VMEM((NZ, part, CY), F32),
             pltpu.VMEM((PAD, CY), BF16),
-            pltpu.SemaphoreType.DMA((4,)),
-            pltpu.SemaphoreType.DMA((4,)),
+            pltpu.SemaphoreType.DMA((halves,)),
+            pltpu.SemaphoreType.DMA((halves,)),
+            pltpu.SemaphoreType.DMA((5,)),
+            pltpu.SemaphoreType.DMA((5,)),
         ],
         compiler_params=pltpu.CompilerParams(
             collective_id=1, has_side_effects=True, vmem_limit_bytes=VMEM_LIMIT
         ),
-        name="reduce",
-    )(chunks)
-
-
-def unpack_kernel(chunks, w1_ref, b1_ref, w2_ref, b2_ref):
+        name="closure",
+    )(moved, east, north, target, depth, w1, b1.reshape(1, HID), w2.T, b2.reshape(1, LEV))
+
+
+def unpack_kernel(moved, tendency, misfit, chunks, tracer_out, misfit_out, w1_ref, b1_ref, w2_ref, b2_ref, wide):
+    for i in range(CX):
+        tracer_out[:, i, :] = moved[i, 0:LEV, :] + tendency[i, 0:LEV, :]
+        wide[:, i, :] = misfit[i, 0:LEV, :]
+    misfit_out[...] = wide[...].astype(BF16)
+    rest = 3 * LEV - 2 * PAD
     for t in range(HID // CY):
         lanes = slice(t * CY, (t + 1) * CY)
         for g in range(2):
-            w1_ref[PAD * g : PAD * (g + 1), lanes] = chunks[4 * t + g].astype(F32)
-        third = chunks[4 * t + 2].astype(F32)
-        rest = 3 * LEV - 2 * PAD
+            w1_ref[PAD * g : PAD * (g + 1), lanes] = chunks[g % 2, 2 * t + g // 2].astype(F32)
+        third = chunks[0, 2 * t + 1].astype(F32)
         w1_ref[2 * PAD : 3 * LEV, lanes] = third[0:rest, :]
-        b1_ref[:, lanes] = third[rest : rest + 1, :]
-        fourth = chunks[4 * t + 3].astype(F32)
-        w2_ref[lanes, :] = jnp.transpose(fourth)[:, 0:LEV]
+        b1_ref[:, lanes] = third[rest : rest + 1, :] + third[rest + 1 : rest + 2, :]
+        fourth = chunks[1, 2 * t + 1].astype(F32)
+        w2_ref[:, lanes] = fourth[0:LEV, :]
         if t == 0:
-            b2_ref[...] = fourth[LEV : LEV + 1, 0:LEV]
-
-
-def unpack(chunks):
+            b2_ref[...] = fourth[LEV : LEV + 1, 0:LEV] + fourth[LEV + 1 : LEV + 2, 0:LEV]
+
+
+def unpack(moved, tendency, misfit, chunks):
     vmem = pl.BlockSpec(memory_space=pltpu.VMEM)
     return pl.pallas_call(
         unpack_kernel,
         out_shape=(
+            jax.ShapeDtypeStruct((LEV, CX, CY), F32),
+            jax.ShapeDtypeStruct((LEV, CX, CY), BF16),
             jax.ShapeDtypeStruct((3 * LEV, HID), F32),
             jax.ShapeDtypeStruct((1, HID), F32),
-            jax.ShapeDtypeStruct((HID, LEV), F32),
+            jax.ShapeDtypeStruct((LEV, HID), F32),
             jax.ShapeDtypeStruct((1, LEV), F32),
         ),
-        in_specs=[vmem],
-        out_specs=(vmem,) * 4,
+        in_specs=[vmem] * 4,
+        out_specs=(vmem,) * 6,
+        scratch_shapes=[pltpu.VMEM((LEV, CX, CY), F32)],
         compiler_params=pltpu.CompilerParams(vmem_limit_bytes=VMEM_LIMIT),
         name="unpack",
-    )(chunks)
+    )(moved, tendency, misfit, chunks)
 
 
 def on_device(tracer, east, north, target, depth, slots, w1, b1, w2, b2):
     moved = transport(tracer, east, north, depth)
-    tracer_out, misfit_out, chunks = closure(moved, east, north, target, depth, w1, b1, w2, b2)
-    grad_w1, grad_b1, grad_w2, grad_b2 = unpack(reduce(chunks))
-    return tracer_out, misfit_out, grad_w1, grad_b1.reshape(HID), grad_w2, grad_b2.reshape(LEV)
+    tendency, misfit, chunks = closure(moved, east, north, target, depth, w1, b1, w2, b2)
+    tracer_out, misfit_out, grad_w1, grad_b1, grad_w2, grad_b2 = unpack(moved, tendency, misfit, chunks)
+    return tracer_out, misfit_out, grad_w1, grad_b1.reshape(HID), grad_w2.T, grad_b2.reshape(LEV)
 
 
 def solution(mesh):

time: 77.4 us -> 71.6 us (0.925)
  Pallas kernels: 70.9 us -> 66.1 us
  local copies, waits for them, and re-layouts: 5.55 us -> 4.45 us
    pallas_call x3 -> x2, Pallas kernels: 46.9 us -> 42.1 us  [the longest x1 40.7 us: closure(): pl.pallas_call(closure_kernel, out_shape=(jax.ShapeDtypeStruct((CX, PAD,...]
    unnamed x22, local copies, waits for them, and re-layouts: 5.55 us -> 4.45 us
where the time goes in v2:
time: 71.6 us; the launch traced here: 71.3 us
  Pallas kernels  66.1 us (92%)
  local copies, waits for them, and re-layouts  4.45 us (6%)
  between operations  0.74 us (1%)
    pallas_call x1, Pallas kernels, closure(): pl.pallas_call(closure_kernel, out_shape=(jax.ShapeDtypeStruct((CX, PAD,...  40.7 us
    pallas_call x1, Pallas kernels, transport(): pl.pallas_call(transport_kernel, out_shape=jax.ShapeDtypeStruct((CX, PAD,...  24 us
    unnamed x22, local copies, waits for them, and re-layouts  4.45 us

profile of v2, /device:TPU:1, one launch (start us, length us, event | category | flops | bytes accessed | tf_op | source)
XLA Modules:
  0.0 71.3 jit_solution(14453604353618731765)
XLA Ops:
  0.6 0.0 copy-start.8
  0.6 0.7 copy-done.8
  1.3 0.0 copy-start
  1.3 0.9 %copy-done = f32[75,4,128]{2,1,0:T(4,128)S(1)} copy-done((f32[75,4,128]{2,1,0:T(4,128)S(1)}, f32[75,4,128]{2,1,0:T(4,128)}, u32[]{:S(2)}) %copy-start) | copy-done | bytes 153624
  2.2 0.0 copy-start.2
  2.2 0.9 %copy-done.2 = f32[75,4,128]{2,1,0:T(4,128)S(1)} copy-done((f32[75,4,128]{2,1,0:T(4,128)S(1)}, f32[75,4,128]{2,1,0:T(4,128)}, u32[]{:S(2)}) %copy-start.2) | copy-done | bytes 153624
  3.1 0.0 copy-start.6
  3.1 0.9 %copy-done.6 = f32[75,4,128]{2,1,0:T(4,128)S(1)} copy-done((f32[75,4,128]{2,1,0:T(4,128)S(1)}, f32[75,4,128]{2,1,0:T(4,128)}, u32[]{:S(2)}) %copy-start.6) | copy-done | bytes 153624
  4.1 0.0 copy-start.1
  4.1 0.0 copy-start.3
  4.1 0.0 copy-start.5
  4.1 0.0 copy-start.7
  4.1 0.0 copy-start.9
  4.1 0.0 copy-start.10
  4.1 24.0 %transport.1.moved_ref.moved = f32[4,80,128]{2,1,0:T(8,128)S(1)} custom-call(f32[75,4,128]{2,1,0:T(4,128)S(1)} %copy-done.6, f32[75,4,128]{2,1,0:T(4,128)S(1)} %copy-done, f32[75,4,128]{2,1,0:T(4,128)S(1)} %copy-done.2, s32[4,128]{1,0:T(4,128)S(1)} %copy-done.8), custom_call_target="tpu_custom_call" | custom-call | tf_op jit(solution)/shard_map/transport/pallas_call | solution.py:155
  28.1 0.0 copy-done.1
  28.1 0.0 copy-done.3
  28.1 0.0 copy-done.5
  28.1 0.0 copy-done.7
  28.1 0.0 copy-done.9
  28.1 0.0 copy-done.10
  28.1 0.0 copy-start.4
  28.2 1.0 %copy-done.4 = bf16[225,1024]{1,0:T(8,128)(2,1)S(1)} copy-done((bf16[225,1024]{1,0:T(8,128)(2,1)S(1)}, bf16[225,1024]{1,0:T(8,128)(2,1)}, u32[]{:S(2)}) %copy-start.4) | copy-done | bytes 460824
  29.2 40.7 %closure.1 = (f32[4,80,128]{2,1,0:T(8,128)S(1)}, f32[4,80,128]{2,1,0:T(8,128)S(1)}, bf16[2,16,80,128]{3,2,1,0:T(8,128)(2,1)S(1)}) custom-call(f32[4,80,128]{2,1,0:T(8,128)S(1)} %transport.1.moved_ref.moved, f32[75,4,128]{2,1,0:T(4,128)S(1)} %copy-done.1, f32[75,4,128]{2,1,0:T(4,128)S(1)} %copy-done.3, bf16[75,4,128]{2,1,0:T(4,128)(2,1)S(1)} %copy-done.7, ...), custom_call_target="tpu_custom_call" | custom-call | tf_op jit(solution)/shard_map/closure/pallas_call | solution.py:391
  69.9 1.4 %unpack.1 = (f32[75,4,128]{2,1,0:T(4,128)}, bf16[75,4,128]{2,1,0:T(4,128)(2,1)}, f32[225,1024]{1,0:T(8,128)}, f32[1,1024]{1,0:T(1,128)}, f32[75,1024]{1,0:T(8,128)}, /*index=5*/f32[1,75]{1,0:T(1,128)}) custom-call(f32[4,80,128]{2,1,0:T(8,128)S(1)} %transport.1.moved_ref.moved, f32[4,80,128]{2,1,0:T(8,128)S(1)} %get-tuple-element.15.tendency, ...), custom_call_target="tpu_custom_call" | custom-call | tf_op jit(solution)/shard_map/unpack/pallas_call | solution.py:450
Async XLA Ops:
  0.6 0.7 copy-start.8
  1.3 0.9 %copy-start = (f32[75,4,128]{2,1,0:T(4,128)S(1)}, f32[75,4,128]{2,1,0:T(4,128)}, u32[]{:S(2)}) copy-start(f32[75,4,128]{2,1,0:T(4,128)} %east_ref.3) | copy-start | bytes 460804
  2.2 0.9 %copy-start.2 = (f32[75,4,128]{2,1,0:T(4,128)S(1)}, f32[75,4,128]{2,1,0:T(4,128)}, u32[]{:S(2)}) copy-start(f32[75,4,128]{2,1,0:T(4,128)} %north_ref.3) | copy-start | bytes 460804
  3.1 0.9 %copy-start.6 = (f32[75,4,128]{2,1,0:T(4,128)S(1)}, f32[75,4,128]{2,1,0:T(4,128)}, u32[]{:S(2)}) copy-start(f32[75,4,128]{2,1,0:T(4,128)} %tracer_ref.1) | copy-start | bytes 460804
  4.1 24.0 %copy-start.1 = (f32[75,4,128]{2,1,0:T(4,128)S(1)}, f32[75,4,128]{2,1,0:T(4,128)}, u32[]{:S(2)}) copy-start(f32[75,4,128]{2,1,0:T(4,128)} %east_ref.3) | copy-start | bytes 460804
  4.1 24.0 %copy-start.3 = (f32[75,4,128]{2,1,0:T(4,128)S(1)}, f32[75,4,128]{2,1,0:T(4,128)}, u32[]{:S(2)}) copy-start(f32[75,4,128]{2,1,0:T(4,128)} %north_ref.3) | copy-start | bytes 460804
  4.1 24.0 %copy-start.5 = (bf16[1024,75]{0,1:T(8,128)(2,1)S(1)}, bf16[1024,75]{0,1:T(8,128)(2,1)}, u32[]{:S(2)}) copy-start(bf16[1024,75]{0,1:T(8,128)(2,1)} %param.17) | copy-start | bytes 460804
  4.1 24.1 %copy-start.7 = (bf16[75,4,128]{2,1,0:T(4,128)(2,1)S(1)}, bf16[75,4,128]{2,1,0:T(4,128)(2,1)}, u32[]{:S(2)}) copy-start(bf16[75,4,128]{2,1,0:T(4,128)(2,1)} %target_ref.1) | copy-start | bytes 230404
  4.1 24.1 %copy-start.9 = (f32[1024]{0:T(1024)S(1)}, f32[1024]{0:T(1024)}, u32[]{:S(2)}) copy-start(f32[1024]{0:T(1024)} %param.16) | copy-start | bytes 12292
  4.1 24.1 %copy-start.10 = (f32[75]{0:T(128)S(1)}, f32[75]{0:T(128)}, u32[]{:S(2)}) copy-start(f32[75]{0:T(128)} %param.18) | copy-start | bytes 904
  28.1 1.0 %copy-start.4 = (bf16[225,1024]{1,0:T(8,128)(2,1)S(1)}, bf16[225,1024]{1,0:T(8,128)(2,1)}, u32[]{:S(2)}) copy-start(bf16[225,1024]{1,0:T(8,128)(2,1)} %w1_ref.1) | copy-start | bytes 1382404

commit v3 on v2

--- a/solution.py
+++ b/solution.py
@@ -22,11 +22,11 @@
 BLK = 256
 F32 = jnp.float32
 BF16 = jnp.bfloat16
-VMEM_LIMIT = 40 * 1024 * 1024
+VMEM_LIMIT = 60 * 1024 * 1024
 
 
 def place(p):
-    return p // 8, p % 8
+    return lax.div(p, 8), lax.rem(p, 8)
 
 
 def faces(opened, speed):
@@ -35,50 +35,129 @@
     return near, far
 
 
-def transport_kernel(
-    tracer_ref, east_ref, north_ref, depth_ref, out_ref,
-    cells, side, pack_n, pack_s, halo_w, halo_e, halo_s, halo_n, halo_u,
-    send_sems, recv_sems,
+def dot(a, b, dims):
+    return lax.dot_general(a, b, (dims, ((), ())), preferred_element_type=F32)
+
+
+def main_kernel(
+    tracer_hbm, east_hbm, north_hbm, target_hbm, depth_hbm, w1_hbm, b1_hbm, w2_hbm, b2_hbm,
+    fresh_out, misfit_out, gathered,
+    tracer_ref, east_ref, north_ref, target_ref, depth_ref, w1_ref, b1_ref, w2_ref, b2_ref,
+    cells, side, side_u, halo_out, halo_w, halo_e, halo_s, halo_n, halo_u,
+    feat, weights, hidden, slope, total, wanted, chunks, core_in, summed, sending, landed,
+    mine, strips, strips_in, strips_all, chunk,
+    load_sems, halo_send, halo_recv, core_send, core_recv, send_sems, recv_sems, known,
 ):
     z, x, m = lax.axis_index("ocx"), lax.axis_index("ocy"), lax.axis_index("ml")
+    core = lax.rem(m, 2)
+    chip = x * 4 + lax.div(m, 2)
     p = x * 8 + m
-    to_e = (lax.rem(z + 1, NZ), x, m)
-    to_w = (lax.rem(z + NZ - 1, NZ), x, m)
+    sibling = (z, x, m + 1 - 2 * core)
+
+    def other_chip(k):
+        c = lax.rem(chip + k, CHIPS)
+        return c, (z, lax.div(c, 4), lax.rem(c, 4) * 2 + core)
+
+    def ring(k):
+        w = lax.rem(z + k, NZ)
+        return w, (w, x, m)
+
+    def far_first(j):
+        half = lax.div(j + 1, 2)
+        return NZ // 2 + half * (1 - 2 * lax.rem(j, 2))
+
+    to_e, to_w = ring(1)[1], ring(NZ - 1)[1]
     to_n = (z, *place(lax.rem(p + 1, TILES)))
     to_s = (z, *place(lax.rem(p + TILES - 1, TILES)))
+
+    pairs = (
+        (depth_hbm, depth_ref), (tracer_hbm, tracer_ref), (north_hbm, north_ref), (east_hbm, east_ref),
+        (target_hbm, target_ref), (w1_hbm, w1_ref), (b1_hbm, b1_ref), (w2_hbm, w2_ref), (b2_hbm, b2_ref),
+    )
+    loads = [pltpu.make_async_copy(src, dst, load_sems.at[i]) for i, (src, dst) in enumerate(pairs)]
+    for load in loads:
+        load.start()
+
     barrier = pltpu.get_barrier_semaphore()
+
+    def signal(target):
+        pl.semaphore_signal(barrier, inc=1, device_id=target, device_id_type=MESH)
+
+    def greet_chips(k, carry):
+        signal(other_chip(k)[1])
+        return carry
+
     for target in (to_e, to_w, to_n, to_s):
-        pl.semaphore_signal(barrier, inc=1, device_id=target, device_id_type=MESH)
+        signal(target)
+    lax.fori_loop(1, CHIPS, greet_chips, 0)
+    signal(sibling)
+
+    def spread_word(number, places):
+        for k in (places, NZ - places):
+            pl.semaphore_signal(known.at[number], inc=1, device_id=ring(k)[1], device_id_type=MESH)
+
+    def remote(src, dst, send_sem, recv_sem, target):
+        return pltpu.make_async_remote_copy(
+            src_ref=src, dst_ref=dst, send_sem=send_sem, recv_sem=recv_sem,
+            device_id=target, device_id_type=MESH,
+        )
+
+    def whole(ref, number):
+        return remote(ref, ref, send_sems.at[number], recv_sems.at[number], sibling)
+
+    def halo(src, dst, number, target):
+        copy = remote(src, dst, halo_send.at[number], halo_recv.at[number], target)
+        copy.start()
+        return copy
 
     level = lax.broadcasted_iota(jnp.int32, (PAD, CY), 0).astype(F32)
     lane = lax.broadcasted_iota(jnp.int32, (PAD, CY), 1)
     tail = lax.broadcasted_iota(jnp.int32, (PAD - LEV, CY), 0)
+    none = jnp.zeros((PAD - LEV, CY), F32)
+    for load in loads[:4]:
+        load.wait()
     depth = [depth_ref[i : i + 1, :].astype(F32) for i in range(CX)]
+    masks = [level[0:LEV, :] < depth[i] for i in range(CX)]
     for i in range(CX):
+        at = slice(CY * i, CY * (i + 1))
         cells[0, i, 0:LEV, :] = tracer_ref[:, i, :]
         cells[0, i, LEV:PAD, :] = jnp.where(tail == 0, depth[i], 0.0)
-    for i in range(CX):
-        side[i, 0:LEV, :] = north_ref[:, i, :]
-        side[i, LEV:PAD, :] = jnp.zeros((PAD - LEV, CY), F32)
-    side[CX, 0:LEV, :] = east_ref[:, CX - 1, :]
-    side[CX, LEV:PAD, :] = jnp.zeros((PAD - LEV, CY), F32)
-    pl.semaphore_wait(barrier, 4)
-
-    def remote(src, dst, number, target):
-        copy = pltpu.make_async_remote_copy(
-            src_ref=src, dst_ref=dst, send_sem=send_sems.at[number], recv_sem=recv_sems.at[number],
-            device_id=target, device_id_type=MESH,
-        )
-        copy.start()
-        return copy
-
-    copies = [remote(side.at[CX], halo_u, 12, to_e)]
+        north_i, east_i = north_ref[:, i, :], east_ref[:, i, :]
+        side[i, 0:LEV, :] = north_i
+        side[i, LEV:PAD, :] = none
+        side[CX + i, 0:LEV, :] = east_i
+        side[CX + i, LEV:PAD, :] = none
+        feat[LEV : 2 * LEV, at] = jnp.where(masks[i], east_i, 0.0)
+        feat[2 * LEV : 3 * LEV, at] = jnp.where(masks[i], north_i, 0.0)
+    last = lax.broadcasted_iota(jnp.int32, (ROWS - 3 * LEV, CELLS), 0)
+    feat[3 * LEV : ROWS, :] = jnp.where(last < 2, 1.0, 0.0)
+    side_u[...] = side[2 * CX - 1].astype(BF16)
+
+    for load in loads[4:]:
+        load.wait()
+    wanted[...] = target_ref[...].astype(F32)
+    edge = 3 * LEV // 16 * 16
+    weights[0:edge, :] = w1_ref[0:edge, :]
+    bias = b1_ref[...]
+    coarse = bias.astype(BF16).astype(F32)
+    row = lax.broadcasted_iota(jnp.int32, (ROWS - edge, HID), 0) + edge
+    final = jnp.where(row == 3 * LEV - 1, w1_ref[3 * LEV - 1 : 3 * LEV, :].astype(F32), 0.0)
+    final = jnp.where(row == 3 * LEV, coarse, final)
+    final = jnp.where(row == 3 * LEV + 1, bias - coarse, final)
+    weights[edge:ROWS, :] = final.astype(BF16)
+
+    pl.semaphore_wait(barrier, 4 + CHIPS - 1 + 1)
+    spread_word(0, 1)
+
+    copies = [halo(side_u, halo_u, 4 * STEPS, to_e)]
     coef = None
     for step in range(STEPS):
         rows = [cells[step, i] for i in range(CX)]
+        halo_out[step, 0] = rows[CX - 1].astype(BF16)
+        halo_out[step, 1] = rows[0].astype(BF16)
         now = [
-            remote(cells.at[step, CX - 1], halo_w.at[step], 4 * step, to_e),
-            remote(cells.at[step, 0], halo_e.at[step], 4 * step + 1, to_w),
+            halo(halo_out.at[step, 0], halo_w.at[step], 4 * step, to_e),
+            halo(halo_out.at[step, 1], halo_e.at[step], 4 * step + 1, to_w),
         ]
         up = jnp.zeros((PAD, CY), F32)
         down = jnp.zeros((PAD, CY), F32)
@@ -87,17 +166,20 @@
             down = jnp.where(lane == i, pltpu.roll(rows[i], i, 1) if i else rows[i], down)
             if step == 0:
                 up = jnp.where(lane == CX + i, pltpu.roll(side[i], CX + i + 1, 1), up)
-        pack_n[step] = up
-        pack_s[step] = down
+        halo_out[step, 2] = up.astype(BF16)
+        halo_out[step, 3] = down.astype(BF16)
         now += [
-            remote(pack_n.at[step], halo_s.at[step], 4 * step + 2, to_n),
-            remote(pack_s.at[step], halo_n.at[step], 4 * step + 3, to_s),
+            halo(halo_out.at[step, 2], halo_s.at[step], 4 * step + 2, to_n),
+            halo(halo_out.at[step, 3], halo_n.at[step], 4 * step + 3, to_s),
         ]
         for copy in now:
             copy.wait_recv()
         copies += now
-        west, east = halo_w[step], halo_e[step]
-        south_pack, north_pack = halo_s[step], halo_n[step]
+        if step < 2:
+            pl.semaphore_wait(known.at[step], 2)
+            spread_word(step + 1, 2 * (step + 1))
+        west, east = halo_w[step].astype(F32), halo_e[step].astype(F32)
+        south_pack, north_pack = halo_s[step].astype(F32), halo_n[step].astype(F32)
         south_in = [pltpu.roll(south_pack, (CY - i) % CY, 1) if i else south_pack for i in range(CX)]
         north_in = [pltpu.roll(north_pack, CY - 1 - i, 1) for i in range(CX)]
         if step == 0:
@@ -105,11 +187,7 @@
             deep = [west[LEV : LEV + 1, :]] + depth + [east[LEV : LEV + 1, :]]
             east_faces = []
             for i in range(CX + 1):
-                speed = halo_u[...] if i == 0 else None
-                if i:
-                    speed = jnp.concatenate(
-                        [east_ref[:, i - 1, :], jnp.zeros((PAD - LEV, CY), F32)], axis=0
-                    ) if i < CX else side[CX]
+                speed = side[CX + i - 1] if i else halo_u[...].astype(F32)
                 east_faces.append(faces(level < jnp.minimum(deep[i], deep[i + 1]), speed))
             coef = []
             for i in range(CX):
@@ -138,116 +216,14 @@
             keep, near_w, far_e, near_s, far_n = coef[i]
             south = jnp.where(lane == 0, south_in[i], pltpu.roll(rows[i], 1, 1))
             north = jnp.where(lane == CY - 1, north_in[i], pltpu.roll(rows[i], CY - 1, 1))
-            value = (
+            cells[step + 1, i] = (
                 keep * rows[i] + near_w * wide[i] - far_e * wide[i + 2] + near_s * south - far_n * north
             )
-            if step == STEPS - 1:
-                out_ref[i] = value
-            else:
-                cells[step + 1, i] = value
-    for copy in copies:
-        copy.wait_send()
-
-
-def transport(tracer, east, north, depth):
-    vmem = pl.BlockSpec(memory_space=pltpu.VMEM)
-    halo = pltpu.VMEM((STEPS, PAD, CY), F32)
-    return pl.pallas_call(
-        transport_kernel,
-        out_shape=jax.ShapeDtypeStruct((CX, PAD, CY), F32),
-        in_specs=[vmem] * 4,
-        out_specs=vmem,
-        scratch_shapes=[
-            pltpu.VMEM((STEPS, CX, PAD, CY), F32),
-            pltpu.VMEM((CX + 1, PAD, CY), F32),
-            halo, halo, halo, halo, halo, halo,
-            pltpu.VMEM((PAD, CY), F32),
-            pltpu.SemaphoreType.DMA((13,)),
-            pltpu.SemaphoreType.DMA((13,)),
-        ],
-        compiler_params=pltpu.CompilerParams(
-            collective_id=0, has_side_effects=True, vmem_limit_bytes=VMEM_LIMIT
-        ),
-        name="transport",
-    )(tracer, east, north, depth)
-
-
-def dot(a, b, dims):
-    return lax.dot_general(a, b, (dims, ((), ())), preferred_element_type=F32)
-
-
-def closure_kernel(
-    moved_ref, east_ref, north_ref, target_ref, depth_ref, w1_ref, b1_ref, w2_ref, b2_ref,
-    tendency_out, misfit_out, gathered,
-    feat, weights, hidden, slope, total, wanted, chunks, core_in, summed, sending, landed,
-    mine, strips, strips_in, strips_all, chunk, core_send, core_recv, send_sems, recv_sems,
-):
-    z, x, m = lax.axis_index("ocx"), lax.axis_index("ocy"), lax.axis_index("ml")
-    core = lax.rem(m, 2)
-    chip = x * 4 + m // 2
-    sibling = (z, x, m + 1 - 2 * core)
-    barrier = pltpu.get_barrier_semaphore()
-
-    def other_chip(k):
-        c = lax.rem(chip + k, CHIPS)
-        return c, (z, c // 4, (c % 4) * 2 + core)
-
-    def ring(k):
-        w = lax.rem(z + k, NZ)
-        return w, (w, x, m)
-
-    def far_first(j):
-        half = (j + 1) // 2
-        return NZ // 2 + half * (1 - 2 * lax.rem(j, 2))
-
-    def signal(target):
-        pl.semaphore_signal(barrier, inc=1, device_id=target, device_id_type=MESH)
-
-    def greet_ring(j, carry):
-        signal(ring(far_first(j))[1])
-        return carry
-
-    def greet_chips(k, carry):
-        signal(other_chip(k)[1])
-        return carry
-
-    lax.fori_loop(0, NZ - 1, greet_ring, 0)
-    lax.fori_loop(1, CHIPS, greet_chips, 0)
-    signal(sibling)
-
-    def remote(src, dst, send_sem, recv_sem, target):
-        return pltpu.make_async_remote_copy(
-            src_ref=src, dst_ref=dst, send_sem=send_sem, recv_sem=recv_sem,
-            device_id=target, device_id_type=MESH,
-        )
-
-    def whole(ref, number):
-        return remote(ref, ref, send_sems.at[number], recv_sems.at[number], sibling)
-
-    level = lax.broadcasted_iota(jnp.int32, (LEV, CY), 0).astype(F32)
-    masks = []
-    want = target_ref[...].astype(F32)
-    wanted[...] = want
+
     for i in range(CX):
         at = slice(CY * i, CY * (i + 1))
-        mask = level < depth_ref[i : i + 1, :].astype(F32)
-        masks.append(mask)
-        feat[0:LEV, at] = jnp.where(mask, moved_ref[i, 0:LEV, :], 0.0)
-        feat[LEV : 2 * LEV, at] = jnp.where(mask, east_ref[:, i, :], 0.0)
-        feat[2 * LEV : 3 * LEV, at] = jnp.where(mask, north_ref[:, i, :], 0.0)
-    last = lax.broadcasted_iota(jnp.int32, (ROWS - 3 * LEV, CELLS), 0)
-    feat[3 * LEV : ROWS, :] = jnp.where(last < 2, 1.0, 0.0)
+        feat[0:LEV, at] = jnp.where(masks[i], cells[STEPS, i, 0:LEV, :], 0.0)
     inputs = feat[...].astype(BF16)
-
-    edge = 3 * LEV // 16 * 16
-    weights[0:edge, :] = w1_ref[0:edge, :]
-    bias = b1_ref[...]
-    coarse = bias.astype(BF16).astype(F32)
-    row = lax.broadcasted_iota(jnp.int32, (ROWS - edge, HID), 0) + edge
-    final = jnp.where(row == 3 * LEV - 1, w1_ref[3 * LEV - 1 : 3 * LEV, :].astype(F32), 0.0)
-    final = jnp.where(row == 3 * LEV, coarse, final)
-    final = jnp.where(row == 3 * LEV + 1, bias - coarse, final)
-    weights[edge:ROWS, :] = final.astype(BF16)
 
     acc = None
     for b in range(HID // BLK):
@@ -270,7 +246,7 @@
         goal = jnp.where(masks[i], wanted[:, i, :], 0.0)
         misfit = tendency - goal
         total[0:LEV, at] = misfit * (1.0 / COLUMNS)
-        tendency_out[i, 0:LEV, :] = tendency
+        fresh_out[i, 0:LEV, :] = cells[STEPS, i, 0:LEV, :] + tendency
         misfit_out[i, 0:LEV, :] = misfit
     d_out = total[...].astype(BF16)
     ones = jnp.ones((16, CELLS), BF16)
@@ -294,8 +270,6 @@
                 row = jnp.concatenate([bias_grad[0:1, :], jnp.zeros((1, CY - PAD), F32)], axis=1)
                 last_part = jnp.where(spread, row, last_part)
             chunks[1, 2 * tile + 1] = last_part
-        if b == 0:
-            pl.semaphore_wait(barrier, NZ - 1 + CHIPS - 1 + 1)
         some = pl.ds(2 * per * b, 2 * per)
         copy = remote(chunks.at[1 - core, some], core_in.at[some], core_send.at[b], core_recv.at[b], sibling)
         copy.start()
@@ -331,6 +305,8 @@
     for k in range(NZ):
         strips[k] = mine[part * k : part * (k + 1), :]
 
+    pl.semaphore_wait(known.at[2], 2)
+
     def scatter_ring(j, carry):
         k = far_first(j)
         w, target = ring(k)
@@ -375,7 +351,7 @@
     whole(landed, 3).wait_recv()
     forward = remote(gathered.at[core], gathered.at[core], send_sems.at[4], recv_sems.at[4], sibling)
     forward.start()
-    for copy in to_sibling:
+    for copy in copies + to_sibling:
         copy.wait_send()
     whole(landed, 0).wait_send()
     whole(strips_in, 1).wait_send()
@@ -384,20 +360,29 @@
     forward.wait()
 
 
-def closure(moved, east, north, target, depth, w1, b1, w2, b2):
+def main(*operands):
     vmem = pl.BlockSpec(memory_space=pltpu.VMEM)
+    hbm = pl.BlockSpec(memory_space=pltpu.HBM)
     part = PAD // NZ
     halves = HID // BLK
+    halo = pltpu.VMEM((STEPS, PAD, CY), BF16)
     return pl.pallas_call(
-        closure_kernel,
+        main_kernel,
         out_shape=(
             jax.ShapeDtypeStruct((CX, PAD, CY), F32),
             jax.ShapeDtypeStruct((CX, PAD, CY), F32),
             jax.ShapeDtypeStruct((2, CHIPS, PAD, CY), BF16),
         ),
-        in_specs=[vmem] * 9,
+        in_specs=[hbm] * 9,
         out_specs=(vmem,) * 3,
-        scratch_shapes=[
+        scratch_shapes=[pltpu.VMEM(a.shape, a.dtype) for a in operands]
+        + [
+            pltpu.VMEM((STEPS + 1, CX, PAD, CY), F32),
+            pltpu.VMEM((2 * CX, PAD, CY), F32),
+            pltpu.VMEM((PAD, CY), BF16),
+            pltpu.VMEM((STEPS, 4, PAD, CY), BF16),
+            halo, halo, halo, halo,
+            pltpu.VMEM((PAD, CY), BF16),
             pltpu.VMEM((ROWS, CELLS), F32),
             pltpu.VMEM((ROWS, HID), BF16),
             pltpu.VMEM((HID, CELLS), BF16),
@@ -414,21 +399,25 @@
             pltpu.VMEM((NZ - 1, part, CY), F32),
             pltpu.VMEM((NZ, part, CY), F32),
             pltpu.VMEM((PAD, CY), BF16),
+            pltpu.SemaphoreType.DMA((len(operands),)),
+            pltpu.SemaphoreType.DMA((4 * STEPS + 1,)),
+            pltpu.SemaphoreType.DMA((4 * STEPS + 1,)),
             pltpu.SemaphoreType.DMA((halves,)),
             pltpu.SemaphoreType.DMA((halves,)),
             pltpu.SemaphoreType.DMA((5,)),
             pltpu.SemaphoreType.DMA((5,)),
+            pltpu.SemaphoreType.REGULAR((3,)),
         ],
         compiler_params=pltpu.CompilerParams(
-            collective_id=1, has_side_effects=True, vmem_limit_bytes=VMEM_LIMIT
+            collective_id=0, has_side_effects=True, vmem_limit_bytes=VMEM_LIMIT
         ),
-        name="closure",
-    )(moved, east, north, target, depth, w1, b1.reshape(1, HID), w2.T, b2.reshape(1, LEV))
-
-
-def unpack_kernel(moved, tendency, misfit, chunks, tracer_out, misfit_out, w1_ref, b1_ref, w2_ref, b2_ref, wide):
+        name="main",
+    )(*operands)
+
+
+def unpack_kernel(fresh, misfit, chunks, tracer_out, misfit_out, w1_ref, b1_ref, w2_ref, b2_ref, wide):
     for i in range(CX):
-        tracer_out[:, i, :] = moved[i, 0:LEV, :] + tendency[i, 0:LEV, :]
+        tracer_out[:, i, :] = fresh[i, 0:LEV, :]
         wide[:, i, :] = misfit[i, 0:LEV, :]
     misfit_out[...] = wide[...].astype(BF16)
     rest = 3 * LEV - 2 * PAD
@@ -445,7 +434,7 @@
             b2_ref[...] = fourth[LEV : LEV + 1, 0:LEV] + fourth[LEV + 1 : LEV + 2, 0:LEV]
 
 
-def unpack(moved, tendency, misfit, chunks):
+def unpack(fresh, misfit, chunks):
     vmem = pl.BlockSpec(memory_space=pltpu.VMEM)
     return pl.pallas_call(
         unpack_kernel,
@@ -457,18 +446,19 @@
             jax.ShapeDtypeStruct((LEV, HID), F32),
             jax.ShapeDtypeStruct((1, LEV), F32),
         ),
-        in_specs=[vmem] * 4,
+        in_specs=[vmem] * 3,
         out_specs=(vmem,) * 6,
         scratch_shapes=[pltpu.VMEM((LEV, CX, CY), F32)],
         compiler_params=pltpu.CompilerParams(vmem_limit_bytes=VMEM_LIMIT),
         name="unpack",
-    )(moved, tendency, misfit, chunks)
+    )(fresh, misfit, chunks)
 
 
 def on_device(tracer, east, north, target, depth, slots, w1, b1, w2, b2):
-    moved = transport(tracer, east, north, depth)
-    tendency, misfit, chunks = closure(moved, east, north, target, depth, w1, b1, w2, b2)
-    tracer_out, misfit_out, grad_w1, grad_b1, grad_w2, grad_b2 = unpack(moved, tendency, misfit, chunks)
+    fresh, misfit, chunks = main(
+        tracer, east, north, target, depth, w1, b1.reshape(1, HID), w2.T, b2.reshape(1, LEV)
+    )
+    tracer_out, misfit_out, grad_w1, grad_b1, grad_w2, grad_b2 = unpack(fresh, misfit, chunks)
     return tracer_out, misfit_out, grad_w1, grad_b1.reshape(HID), grad_w2.T, grad_b2.reshape(LEV)
 
 

time: 71.6 us -> 64.8 us (0.905)
  local copies, waits for them, and re-layouts: 4.45 us -> 0 us
  Pallas kernels: 66.1 us -> 64 us
    unnamed x22 -> x0, local copies, waits for them, and re-layouts: 4.45 us -> none
    pallas_call x2 -> x1, Pallas kernels: 64.7 us -> 61.3 us  [main(): pl.pallas_call(main_kernel, out_shape=(jax.ShapeDtypeStruct((CX, PAD, CY)...]
    pallas_call x1, Pallas kernels: 1.4 us -> 2.65 us  [unpack(): pl.pallas_call(unpack_kernel, out_shape=(jax.ShapeDtypeStruct((LEV, CX, C...]
where the time goes in v3:
time: 64.8 us; the launch traced here: 64.6 us
  Pallas kernels  64 us (99%)
    pallas_call x1, Pallas kernels, main(): pl.pallas_call(main_kernel, out_shape=(jax.ShapeDtypeStruct((CX, PAD, CY)...  61.3 us
    pallas_call x1, Pallas kernels, unpack(): pl.pallas_call(unpack_kernel, out_shape=(jax.ShapeDtypeStruct((LEV, CX, C...  2.65 us

profile of v3, /device:TPU:1, one launch (start us, length us, event | category | flops | bytes accessed | tf_op | source)
XLA Modules:
  0.0 64.6 jit_solution(12432365882107575236)
XLA Ops:
  0.6 61.3 %main.1 = (f32[4,80,128]{2,1,0:T(8,128)}, f32[4,80,128]{2,1,0:T(8,128)}, bf16[2,16,80,128]{3,2,1,0:T(8,128)(2,1)}) custom-call(f32[75,4,128]{2,1,0:T(4,128)} %tracer_hbm.1, f32[75,4,128]{2,1,0:T(4,128)} %east_hbm.1, f32[75,4,128]{2,1,0:T(4,128)} %north_hbm.1, bf16[75,4,128]{2,1,0:T(4,128)(2,1)} %target_hbm.1, s32[4,128]{1,0:T(4,128)} %depth_hbm.1, ...), custom_call_target="tpu_custom_call" | custom-call | tf_op jit(solution)/shard_map/main/pallas_call | solution.py:369
  62.0 2.6 %unpack.1 = (f32[75,4,128]{2,1,0:T(4,128)}, bf16[75,4,128]{2,1,0:T(4,128)(2,1)}, f32[225,1024]{1,0:T(8,128)}, f32[1,1024]{1,0:T(1,128)}, f32[75,1024]{1,0:T(8,128)}, /*index=5*/f32[1,75]{1,0:T(1,128)}) custom-call(f32[4,80,128]{2,1,0:T(8,128)} %get-tuple-element.15.fresh, f32[4,80,128]{2,1,0:T(8,128)} %get-tuple-element.16.misfit, ...), custom_call_target="tpu_custom_call" | custom-call | tf_op jit(solution)/shard_map/unpack/pallas_call | solution.py:439

commit v4 on v3

--- a/solution.py
+++ b/solution.py
@@ -22,7 +22,7 @@
 BLK = 256
 F32 = jnp.float32
 BF16 = jnp.bfloat16
-VMEM_LIMIT = 60 * 1024 * 1024
+VMEM_LIMIT = 40 * 1024 * 1024
 
 
 def place(p):
@@ -66,9 +66,11 @@
         half = lax.div(j + 1, 2)
         return NZ // 2 + half * (1 - 2 * lax.rem(j, 2))
 
+    def tile(k):
+        return (z, *place(lax.rem(p + k, TILES)))
+
     to_e, to_w = ring(1)[1], ring(NZ - 1)[1]
-    to_n = (z, *place(lax.rem(p + 1, TILES)))
-    to_s = (z, *place(lax.rem(p + TILES - 1, TILES)))
+    to_n, to_s = tile(1), tile(TILES - 1)
 
     pairs = (
         (depth_hbm, depth_ref), (tracer_hbm, tracer_ref), (north_hbm, north_ref), (east_hbm, east_ref),
@@ -83,18 +85,15 @@
     def signal(target):
         pl.semaphore_signal(barrier, inc=1, device_id=target, device_id_type=MESH)
 
-    def greet_chips(k, carry):
-        signal(other_chip(k)[1])
-        return carry
-
     for target in (to_e, to_w, to_n, to_s):
         signal(target)
-    lax.fori_loop(1, CHIPS, greet_chips, 0)
-    signal(sibling)
 
     def spread_word(number, places):
-        for k in (places, NZ - places):
-            pl.semaphore_signal(known.at[number], inc=1, device_id=ring(k)[1], device_id_type=MESH)
+        targets = [tile(places), tile(TILES - places)]
+        if places < NZ // 2:
+            targets += [ring(places)[1], ring(NZ - places)[1]]
+        for target in targets:
+            pl.semaphore_signal(known.at[number], inc=1, device_id=target, device_id_type=MESH)
 
     def remote(src, dst, send_sem, recv_sem, target):
         return pltpu.make_async_remote_copy(
@@ -146,7 +145,7 @@
     final = jnp.where(row == 3 * LEV + 1, bias - coarse, final)
     weights[edge:ROWS, :] = final.astype(BF16)
 
-    pl.semaphore_wait(barrier, 4 + CHIPS - 1 + 1)
+    pl.semaphore_wait(barrier, 4)
     spread_word(0, 1)
 
     copies = [halo(side_u, halo_u, 4 * STEPS, to_e)]
@@ -176,7 +175,7 @@
             copy.wait_recv()
         copies += now
         if step < 2:
-            pl.semaphore_wait(known.at[step], 2)
+            pl.semaphore_wait(known.at[step], 4)
             spread_word(step + 1, 2 * (step + 1))
         west, east = halo_w[step].astype(F32), halo_e[step].astype(F32)
         south_pack, north_pack = halo_s[step].astype(F32), halo_n[step].astype(F32)
@@ -236,6 +235,8 @@
         slope[at, :] = gate * (1.0 + stash * (1.0 - gate))
         part = dot(w2_ref[:, at], act, ((1,), (0,)))
         acc = part if acc is None else acc + part
+    pl.semaphore_wait(known.at[2], 4)
+    spread_word(3, 8)
     eye = lax.broadcasted_iota(jnp.int32, (LEV, LEV), 0) == lax.broadcasted_iota(jnp.int32, (LEV, LEV), 1)
     bias2 = jnp.sum(jnp.where(eye, b2_ref[...], 0.0), axis=1, keepdims=True)
     output = acc + bias2
@@ -290,6 +291,8 @@
             summed[2 * per * b + j] = value
             sending[2 * per * b + j] = sent.astype(BF16)
 
+    pl.semaphore_wait(known.at[3], 2)
+
     def scatter(k, carry):
         c, target = other_chip(k)
         remote(sending.at[c], landed.at[k - 1], send_sems.at[0], recv_sems.at[0], target).start()
@@ -304,8 +307,6 @@
     part = PAD // NZ
     for k in range(NZ):
         strips[k] = mine[part * k : part * (k + 1), :]
-
-    pl.semaphore_wait(known.at[2], 2)
 
     def scatter_ring(j, carry):
         k = far_first(j)
@@ -406,13 +407,13 @@
             pltpu.SemaphoreType.DMA((halves,)),
             pltpu.SemaphoreType.DMA((5,)),
             pltpu.SemaphoreType.DMA((5,)),
-            pltpu.SemaphoreType.REGULAR((3,)),
+            pltpu.SemaphoreType.REGULAR((4,)),
         ],
         compiler_params=pltpu.CompilerParams(
             collective_id=0, has_side_effects=True, vmem_limit_bytes=VMEM_LIMIT
         ),
         name="main",
-    )(*operands)
+    )(*(pltpu.with_memory_space_constraint(a, pltpu.HBM) for a in operands))
 
 
 def unpack_kernel(fresh, misfit, chunks, tracer_out, misfit_out, w1_ref, b1_ref, w2_ref, b2_ref, wide):

time: 64.8 us -> 61.9 us (0.955)
  Pallas kernels: 64 us -> 61.1 us
    pallas_call x1, Pallas kernels: 61.3 us -> 59.8 us  [main(): pl.pallas_call(main_kernel, out_shape=(jax.ShapeDtypeStruct((CX, PAD, CY)...]
    pallas_call x1, Pallas kernels: 2.65 us -> 1.39 us  [unpack(): pl.pallas_call(unpack_kernel, out_shape=(jax.ShapeDtypeStruct((LEV, CX, C...]
where the time goes in v4:
time: 61.9 us; the launch traced here: 61.8 us
  Pallas kernels  61.1 us (99%)
  between operations  0.64 us (1%)
    pallas_call x1, Pallas kernels, main(): pl.pallas_call(main_kernel, out_shape=(jax.ShapeDtypeStruct((CX, PAD, CY)...  59.8 us
    pallas_call x1, Pallas kernels, unpack(): pl.pallas_call(unpack_kernel, out_shape=(jax.ShapeDtypeStruct((LEV, CX, C...  1.39 us

profile of v4, /device:TPU:1, one launch (start us, length us, event | category | flops | bytes accessed | tf_op | source)
XLA Modules:
  0.0 61.8 jit_solution(3530833786459273946)
XLA Ops:
  0.6 59.8 %main.1 = (f32[4,80,128]{2,1,0:T(8,128)S(1)}, f32[4,80,128]{2,1,0:T(8,128)S(1)}, bf16[2,16,80,128]{3,2,1,0:T(8,128)(2,1)S(1)}) custom-call(f32[75,4,128]{2,1,0:T(4,128)} %tracer_hbm.1, f32[75,4,128]{2,1,0:T(4,128)} %east_hbm.1, f32[75,4,128]{2,1,0:T(4,128)} %north_hbm.1, bf16[75,4,128]{2,1,0:T(4,128)(2,1)} %target_hbm.1, s32[4,128]{1,0:T(4,128)} %depth_hbm.1, ...), custom_call_target="tpu_custom_call" | custom-call | tf_op jit(solution)/shard_map/main/pallas_call | solution.py:370
  60.4 1.4 %unpack.1 = (f32[75,4,128]{2,1,0:T(4,128)}, bf16[75,4,128]{2,1,0:T(4,128)(2,1)}, f32[225,1024]{1,0:T(8,128)}, f32[1,1024]{1,0:T(1,128)}, f32[75,1024]{1,0:T(8,128)}, /*index=5*/f32[1,75]{1,0:T(1,128)}) custom-call(f32[4,80,128]{2,1,0:T(8,128)S(1)} %get-tuple-element.15.fresh, f32[4,80,128]{2,1,0:T(8,128)S(1)} %get-tuple-element.16.misfit, ...), custom_call_target="tpu_custom_call" | custom-call | tf_op jit(solution)/shard_map/unpack/pallas_call | solution.py:440

commit v5 on v4

--- a/solution.py
+++ b/solution.py
@@ -19,6 +19,12 @@
 NZ = 16
 CHIPS = 16
 COLUMNS = 262144
+REACH = 3
+WIDE = CX + 2 * REACH
+STRIP = 2 * REACH
+NORTH_AT = (0, 1, 10, 11)
+EAST_AT = (2, 6, 8, 9)
+CELL_AT = (3, 4, 5, 7)
 BLK = 256
 F32 = jnp.float32
 BF16 = jnp.bfloat16
@@ -43,7 +49,7 @@
     tracer_hbm, east_hbm, north_hbm, target_hbm, depth_hbm, w1_hbm, b1_hbm, w2_hbm, b2_hbm,
     fresh_out, misfit_out, gathered,
     tracer_ref, east_ref, north_ref, target_ref, depth_ref, w1_ref, b1_ref, w2_ref, b2_ref,
-    cells, side, side_u, halo_out, halo_w, halo_e, halo_s, halo_n, halo_u,
+    cells, north_own, east_own, rows_out, edges_out, halo_w, halo_e, halo_edges, pick_out, pick_rows, pick_edges,
     feat, weights, hidden, slope, total, wanted, chunks, core_in, summed, sending, landed,
     mine, strips, strips_in, strips_all, chunk,
     load_sems, halo_send, halo_recv, core_send, core_recv, send_sems, recv_sems, known,
@@ -85,7 +91,12 @@
     def signal(target):
         pl.semaphore_signal(barrier, inc=1, device_id=target, device_id_type=MESH)
 
-    for target in (to_e, to_w, to_n, to_s):
+    def diagonal(dz, k):
+        return (lax.rem(z + dz, NZ), *tile(k)[1:])
+
+    to_ne, to_nw = diagonal(1, 1), diagonal(NZ - 1, 1)
+    to_se, to_sw = diagonal(1, TILES - 1), diagonal(NZ - 1, TILES - 1)
+    for target in (to_e, to_w, to_n, to_s, to_ne, to_nw, to_se, to_sw):
         signal(target)
 
     def spread_word(number, places):
@@ -108,6 +119,35 @@
         copy = remote(src, dst, halo_send.at[number], halo_recv.at[number], target)
         copy.start()
         return copy
+
+    lane_in = lax.broadcasted_iota(jnp.int32, (CY, 2 * CY), 0)
+    lane_out = lax.broadcasted_iota(jnp.int32, (CY, 2 * CY), 1)
+    shift = jnp.where(lane_in >= CY - REACH, lane_out - lane_in + (CY - REACH), -999)
+    shift = jnp.where(lane_in < REACH, lane_out - lane_in - CY, shift)
+    for f, order in enumerate((CELL_AT, EAST_AT, NORTH_AT)):
+        for i in range(CX):
+            at = slice(CY * order[i], CY * (order[i] + 1))
+            pick_out[at, :] = jnp.where(shift == 16 * f + 4 * i, 1.0, 0.0).astype(BF16)
+    lane_in = lax.broadcasted_iota(jnp.int32, (CY, CY), 0)
+    lane_out = lax.broadcasted_iota(jnp.int32, (CY, CY), 1)
+    shift = jnp.where(lane_in >= CY - REACH, lane_out - lane_in + (CY - REACH) - CY // 2, -999)
+    shift = jnp.where(lane_in < REACH, lane_out - lane_in - REACH, shift)
+    for n in range(WIDE):
+        pick_rows[CY * n : CY * (n + 1), :] = jnp.where(shift == STRIP * n, 1.0, 0.0).astype(BF16)
+    lane_in = lax.broadcasted_iota(jnp.int32, (CY, 3 * CY), 0)
+    lane_out = lax.broadcasted_iota(jnp.int32, (CY, 3 * CY), 1)
+    field, owner, nth = lane_in // 16, (lane_in // 4) % 4, lane_in % 4
+    shift = lane_out - (CY * field + STRIP * owner + nth)
+    shift = jnp.where(jnp.logical_and(field < 3, nth < REACH), shift, -999)
+    for n in range(6):
+        dz = (0, -1, 1)[n % 3]
+        here = (n // 3) * (CY // 2 + REACH) + STRIP * (REACH + CX * dz)
+        hit = shift == here
+        if dz == -1:
+            hit = jnp.logical_and(hit, owner >= 1)
+        if dz == 1:
+            hit = jnp.logical_and(hit, owner <= REACH - 1)
+        pick_edges[CY * n : CY * (n + 1), :] = jnp.where(hit, 1.0, 0.0).astype(BF16)
 
     level = lax.broadcasted_iota(jnp.int32, (PAD, CY), 0).astype(F32)
     lane = lax.broadcasted_iota(jnp.int32, (PAD, CY), 1)
@@ -116,22 +156,40 @@
     for load in loads[:4]:
         load.wait()
     depth = [depth_ref[i : i + 1, :].astype(F32) for i in range(CX)]
+    for i in range(CX):
+        cells[i, 0:LEV, :] = tracer_ref[:, i, :]
+        cells[i, LEV:PAD, :] = jnp.where(tail == 0, depth[i], 0.0)
+        north_own[i, 0:LEV, :] = north_ref[:, i, :]
+        north_own[i, LEV:PAD, :] = none
+        east_own[i, 0:LEV, :] = east_ref[:, i, :]
+        east_own[i, LEV:PAD, :] = none
+        rows_out[CELL_AT[i]] = cells[i].astype(BF16)
+        rows_out[EAST_AT[i]] = east_own[i].astype(BF16)
+        rows_out[NORTH_AT[i]] = north_own[i].astype(BF16)
+    edges = dot(jnp.concatenate([rows_out[n] for n in range(3 * CX)], axis=1), pick_out[...], ((1,), (0,)))
+    edges_out[0] = edges[:, 0:CY].astype(BF16)
+    edges_out[1] = edges[:, CY : 2 * CY].astype(BF16)
+
+    pl.semaphore_wait(barrier, 8)
+    copies = [
+        halo(rows_out.at[4:12], halo_w, 0, to_e),
+        halo(rows_out.at[0:7], halo_e, 1, to_w),
+        halo(edges_out.at[0], halo_edges.at[0], 2, to_n),
+        halo(edges_out.at[0], halo_edges.at[1], 3, to_ne),
+        halo(edges_out.at[0], halo_edges.at[2], 4, to_nw),
+        halo(edges_out.at[1], halo_edges.at[3], 5, to_s),
+        halo(edges_out.at[1], halo_edges.at[4], 6, to_se),
+        halo(edges_out.at[1], halo_edges.at[5], 7, to_sw),
+    ]
+    spread_word(0, 1)
+
     masks = [level[0:LEV, :] < depth[i] for i in range(CX)]
     for i in range(CX):
         at = slice(CY * i, CY * (i + 1))
-        cells[0, i, 0:LEV, :] = tracer_ref[:, i, :]
-        cells[0, i, LEV:PAD, :] = jnp.where(tail == 0, depth[i], 0.0)
-        north_i, east_i = north_ref[:, i, :], east_ref[:, i, :]
-        side[i, 0:LEV, :] = north_i
-        side[i, LEV:PAD, :] = none
-        side[CX + i, 0:LEV, :] = east_i
-        side[CX + i, LEV:PAD, :] = none
-        feat[LEV : 2 * LEV, at] = jnp.where(masks[i], east_i, 0.0)
-        feat[2 * LEV : 3 * LEV, at] = jnp.where(masks[i], north_i, 0.0)
+        feat[LEV : 2 * LEV, at] = jnp.where(masks[i], east_own[i, 0:LEV, :], 0.0)
+        feat[2 * LEV : 3 * LEV, at] = jnp.where(masks[i], north_own[i, 0:LEV, :], 0.0)
     last = lax.broadcasted_iota(jnp.int32, (ROWS - 3 * LEV, CELLS), 0)
     feat[3 * LEV : ROWS, :] = jnp.where(last < 2, 1.0, 0.0)
-    side_u[...] = side[2 * CX - 1].astype(BF16)
-
     for load in loads[4:]:
         load.wait()
     wanted[...] = target_ref[...].astype(F32)
@@ -145,83 +203,93 @@
     final = jnp.where(row == 3 * LEV + 1, bias - coarse, final)
     weights[edge:ROWS, :] = final.astype(BF16)
 
-    pl.semaphore_wait(barrier, 4)
-    spread_word(0, 1)
-
-    copies = [halo(side_u, halo_u, 4 * STEPS, to_e)]
-    coef = None
+    pl.semaphore_wait(known.at[0], 4)
+    spread_word(1, 2)
+    for copy in copies:
+        copy.wait_recv()
+
+    cell_rows = [halo_w[0], halo_w[1], halo_w[3]] + [rows_out[n] for n in CELL_AT] + [halo_e[3], halo_e[4], halo_e[5]]
+    east_rows = [halo_w[2], halo_w[4], halo_w[5]] + [rows_out[n] for n in EAST_AT] + [halo_e[2], halo_e[6]]
+    north_rows = [halo_w[6], halo_w[7]] + [rows_out[n] for n in NORTH_AT] + [halo_e[0], halo_e[1]]
+    beyond = dot(jnp.concatenate([halo_edges[n] for n in range(6)], axis=1), pick_edges[...], ((1,), (0,)))
+
+    def strip_of(some, first, f):
+        own = dot(
+            jnp.concatenate(some, axis=1), pick_rows[CY * first : CY * (first + len(some)), :], ((1,), (0,))
+        )
+        return own + beyond[:, CY * f : CY * (f + 1)]
+
+    def turn(value, by):
+        by = by % CY
+        return pltpu.roll(value, by, 1) if by else value
+
+    strip = strip_of(cell_rows, 0, 0)
+    deep_here = jnp.broadcast_to(strip[LEV : LEV + 1, :], (PAD, CY))
+    near_e, far_e = faces(level < jnp.minimum(deep_here, turn(deep_here, -STRIP)), strip_of(east_rows, 0, 1))
+    nth = lane % (CY // 2)
+    nth = nth - STRIP * ((nth * 43) // 256)
+    border = jnp.logical_or(
+        jnp.logical_and(lane < CY // 2, p == 0), jnp.logical_and(lane >= CY // 2, p == TILES - 1)
+    )
+    shut = jnp.logical_and(nth == REACH - 1, border)
+    opened = jnp.logical_and(level < jnp.minimum(deep_here, turn(deep_here, -1)), jnp.logical_not(shut))
+    strip_near, strip_far = faces(opened, strip_of(north_rows, 1, 2))
+    near_w, far_w = turn(near_e, STRIP), turn(far_e, STRIP)
+    near_s, far_s = turn(strip_near, 1), turn(strip_far, 1)
+    strip_coef = (1.0 + far_w - near_e + far_s - strip_near, near_w, far_e, near_s, strip_far)
+    strips_at = [strip]
+    for step in range(STEPS - 1):
+        keep, near_w, far_e, near_s, far_n = strip_coef
+        strip = (
+            keep * strip + near_w * turn(strip, STRIP) - far_e * turn(strip, -STRIP)
+            + near_s * turn(strip, 1) - far_n * turn(strip, -1)
+        )
+        strips_at.append(strip)
+
+    now = [
+        cells[n - REACH] if REACH <= n < REACH + CX else cell_rows[n].astype(F32) for n in range(WIDE)
+    ]
+    deep = [jnp.broadcast_to(value[LEV : LEV + 1, :], (PAD, CY)) for value in now]
+    east_faces = []
+    for n in range(WIDE - 1):
+        speed = east_own[n - REACH] if REACH <= n < REACH + CX else east_rows[n].astype(F32)
+        east_faces.append(faces(level < jnp.minimum(deep[n], deep[n + 1]), speed))
+    shut_n = jnp.logical_and(lane == CY - 1, p == TILES - 1)
+    coef = [None] * WIDE
+    for n in range(1, WIDE - 1):
+        speed = north_own[n - REACH] if REACH <= n < REACH + CX else north_rows[n - 1].astype(F32)
+        there = jnp.where(
+            lane == CY - 1, turn(deep_here, CY - 1 - (CY // 2 + STRIP * n + REACH)), turn(deep[n], -1)
+        )
+        opened = jnp.logical_and(level < jnp.minimum(deep[n], there), jnp.logical_not(shut_n))
+        near_n, far_n = faces(opened, speed)
+        below = -(STRIP * n + REACH - 1)
+        near_s = jnp.where(lane == 0, turn(strip_near, below), turn(near_n, 1))
+        far_s = jnp.where(lane == 0, turn(strip_far, below), turn(far_n, 1))
+        near_w, far_w = east_faces[n - 1]
+        near_e, far_e = east_faces[n]
+        coef[n] = (1.0 + far_w - near_e + far_s - near_n, near_w, far_e, near_s, far_n)
     for step in range(STEPS):
-        rows = [cells[step, i] for i in range(CX)]
-        halo_out[step, 0] = rows[CX - 1].astype(BF16)
-        halo_out[step, 1] = rows[0].astype(BF16)
-        now = [
-            halo(halo_out.at[step, 0], halo_w.at[step], 4 * step, to_e),
-            halo(halo_out.at[step, 1], halo_e.at[step], 4 * step + 1, to_w),
-        ]
-        up = jnp.zeros((PAD, CY), F32)
-        down = jnp.zeros((PAD, CY), F32)
-        for i in range(CX):
-            up = jnp.where(lane == i, pltpu.roll(rows[i], i + 1, 1), up)
-            down = jnp.where(lane == i, pltpu.roll(rows[i], i, 1) if i else rows[i], down)
-            if step == 0:
-                up = jnp.where(lane == CX + i, pltpu.roll(side[i], CX + i + 1, 1), up)
-        halo_out[step, 2] = up.astype(BF16)
-        halo_out[step, 3] = down.astype(BF16)
-        now += [
-            halo(halo_out.at[step, 2], halo_s.at[step], 4 * step + 2, to_n),
-            halo(halo_out.at[step, 3], halo_n.at[step], 4 * step + 3, to_s),
-        ]
-        for copy in now:
-            copy.wait_recv()
-        copies += now
-        if step < 2:
-            pl.semaphore_wait(known.at[step], 4)
-            spread_word(step + 1, 2 * (step + 1))
-        west, east = halo_w[step].astype(F32), halo_e[step].astype(F32)
-        south_pack, north_pack = halo_s[step].astype(F32), halo_n[step].astype(F32)
-        south_in = [pltpu.roll(south_pack, (CY - i) % CY, 1) if i else south_pack for i in range(CX)]
-        north_in = [pltpu.roll(north_pack, CY - 1 - i, 1) for i in range(CX)]
-        if step == 0:
-            copies[0].wait_recv()
-            deep = [west[LEV : LEV + 1, :]] + depth + [east[LEV : LEV + 1, :]]
-            east_faces = []
-            for i in range(CX + 1):
-                speed = side[CX + i - 1] if i else halo_u[...].astype(F32)
-                east_faces.append(faces(level < jnp.minimum(deep[i], deep[i + 1]), speed))
-            coef = []
-            for i in range(CX):
-                here = jnp.broadcast_to(depth[i], (PAD, CY))
-                there = jnp.where(
-                    lane == CY - 1,
-                    jnp.broadcast_to(north_in[i][LEV : LEV + 1, :], (PAD, CY)),
-                    pltpu.roll(here, CY - 1, 1),
-                )
-                shut_n = jnp.logical_and(lane == CY - 1, p == TILES - 1)
-                near_n, far_n = faces(
-                    jnp.logical_and(level < jnp.minimum(here, there), jnp.logical_not(shut_n)), side[i]
-                )
-                below = jnp.broadcast_to(south_in[i][LEV : LEV + 1, :], (PAD, CY))
-                near_b, far_b = faces(
-                    jnp.logical_and(level < jnp.minimum(here, below), p != 0),
-                    pltpu.roll(south_pack, CY - CX - i, 1),
-                )
-                near_s = jnp.where(lane == 0, near_b, pltpu.roll(near_n, 1, 1))
-                far_s = jnp.where(lane == 0, far_b, pltpu.roll(far_n, 1, 1))
-                near_w, far_w = east_faces[i]
-                near_e, far_e = east_faces[i + 1]
-                coef.append((1.0 + far_w - near_e + far_s - near_n, near_w, far_e, near_s, far_n))
-        wide = [west] + rows + [east]
-        for i in range(CX):
-            keep, near_w, far_e, near_s, far_n = coef[i]
-            south = jnp.where(lane == 0, south_in[i], pltpu.roll(rows[i], 1, 1))
-            north = jnp.where(lane == CY - 1, north_in[i], pltpu.roll(rows[i], CY - 1, 1))
-            cells[step + 1, i] = (
-                keep * rows[i] + near_w * wide[i] - far_e * wide[i + 2] + near_s * south - far_n * north
+        after = list(now)
+        for n in range(step + 1, WIDE - 1 - step):
+            keep, near_w, far_e, near_s, far_n = coef[n]
+            strip = strips_at[step]
+            south = jnp.where(lane == 0, turn(strip, -(STRIP * n + REACH - 1)), turn(now[n], 1))
+            north = jnp.where(
+                lane == CY - 1, turn(strip, CY - 1 - (CY // 2 + STRIP * n + REACH)), turn(now[n], -1)
             )
+            after[n] = (
+                keep * now[n] + near_w * now[n - 1] - far_e * now[n + 1] + near_s * south - far_n * north
+            )
+        now = after
+    for i in range(CX):
+        cells[i] = now[REACH + i]
+    pl.semaphore_wait(known.at[1], 4)
+    spread_word(2, 4)
 
     for i in range(CX):
         at = slice(CY * i, CY * (i + 1))
-        feat[0:LEV, at] = jnp.where(masks[i], cells[STEPS, i, 0:LEV, :], 0.0)
+        feat[0:LEV, at] = jnp.where(masks[i], cells[i, 0:LEV, :], 0.0)
     inputs = feat[...].astype(BF16)
 
     acc = None
@@ -247,7 +315,7 @@
         goal = jnp.where(masks[i], wanted[:, i, :], 0.0)
         misfit = tendency - goal
         total[0:LEV, at] = misfit * (1.0 / COLUMNS)
-        fresh_out[i, 0:LEV, :] = cells[STEPS, i, 0:LEV, :] + tendency
+        fresh_out[i, 0:LEV, :] = cells[i, 0:LEV, :] + tendency
         misfit_out[i, 0:LEV, :] = misfit
     d_out = total[...].astype(BF16)
     ones = jnp.ones((16, CELLS), BF16)
@@ -366,7 +434,6 @@
     hbm = pl.BlockSpec(memory_space=pltpu.HBM)
     part = PAD // NZ
     halves = HID // BLK
-    halo = pltpu.VMEM((STEPS, PAD, CY), BF16)
     return pl.pallas_call(
         main_kernel,
         out_shape=(
@@ -378,12 +445,17 @@
         out_specs=(vmem,) * 3,
         scratch_shapes=[pltpu.VMEM(a.shape, a.dtype) for a in operands]
         + [
-            pltpu.VMEM((STEPS + 1, CX, PAD, CY), F32),
-            pltpu.VMEM((2 * CX, PAD, CY), F32),
-            pltpu.VMEM((PAD, CY), BF16),
-            pltpu.VMEM((STEPS, 4, PAD, CY), BF16),
-            halo, halo, halo, halo,
-            pltpu.VMEM((PAD, CY), BF16),
+            pltpu.VMEM((CX, PAD, CY), F32),
+            pltpu.VMEM((CX, PAD, CY), F32),
+            pltpu.VMEM((CX, PAD, CY), F32),
+            pltpu.VMEM((3 * CX, PAD, CY), BF16),
+            pltpu.VMEM((2, PAD, CY), BF16),
+            pltpu.VMEM((8, PAD, CY), BF16),
+            pltpu.VMEM((7, PAD, CY), BF16),
+            pltpu.VMEM((6, PAD, CY), BF16),
+            pltpu.VMEM((3 * CX * CY, 2 * CY), BF16),
+            pltpu.VMEM((WIDE * CY, CY), BF16),
+            pltpu.VMEM((6 * CY, 3 * CY), BF16),
             pltpu.VMEM((ROWS, CELLS), F32),
             pltpu.VMEM((ROWS, HID), BF16),
             pltpu.VMEM((HID, CELLS), BF16),
@@ -401,8 +473,8 @@
             pltpu.VMEM((NZ, part, CY), F32),
             pltpu.VMEM((PAD, CY), BF16),
             pltpu.SemaphoreType.DMA((len(operands),)),
-            pltpu.SemaphoreType.DMA((4 * STEPS + 1,)),
-            pltpu.SemaphoreType.DMA((4 * STEPS + 1,)),
+            pltpu.SemaphoreType.DMA((8,)),
+            pltpu.SemaphoreType.DMA((8,)),
             pltpu.SemaphoreType.DMA((halves,)),
             pltpu.SemaphoreType.DMA((halves,)),
             pltpu.SemaphoreType.DMA((5,)),

time: 61.9 us -> 60.8 us (0.982)
  Pallas kernels: 61.1 us -> 60 us
    pallas_call x1, Pallas kernels: 59.8 us -> 58.7 us  [main(): pl.pallas_call(main_kernel, out_shape=(jax.ShapeDtypeStruct((CX, PAD, CY)...]
where the time goes in v5:
time: 60.8 us; the launch traced here: 60.7 us
  Pallas kernels  60 us (99%)
  between operations  0.64 us (1%)
    pallas_call x1, Pallas kernels, main(): pl.pallas_call(main_kernel, out_shape=(jax.ShapeDtypeStruct((CX, PAD, CY)...  58.7 us
    pallas_call x1, Pallas kernels, unpack(): pl.pallas_call(unpack_kernel, out_shape=(jax.ShapeDtypeStruct((LEV, CX, C...  1.39 us

profile of v5, /device:TPU:1, one launch (start us, length us, event | category | flops | bytes accessed | tf_op | source)
XLA Modules:
  0.0 60.7 jit_solution(17902938422498198482)
XLA Ops:
  0.6 58.7 %main.1 = (f32[4,80,128]{2,1,0:T(8,128)S(1)}, f32[4,80,128]{2,1,0:T(8,128)S(1)}, bf16[2,16,80,128]{3,2,1,0:T(8,128)(2,1)S(1)}) custom-call(f32[75,4,128]{2,1,0:T(4,128)} %tracer_hbm.1, f32[75,4,128]{2,1,0:T(4,128)} %east_hbm.1, f32[75,4,128]{2,1,0:T(4,128)} %north_hbm.1, bf16[75,4,128]{2,1,0:T(4,128)(2,1)} %target_hbm.1, s32[4,128]{1,0:T(4,128)} %depth_hbm.1, ...), custom_call_target="tpu_custom_call" | custom-call | tf_op jit(solution)/shard_map/main/pallas_call | solution.py:437
  59.3 1.4 %unpack.1 = (f32[75,4,128]{2,1,0:T(4,128)}, bf16[75,4,128]{2,1,0:T(4,128)(2,1)}, f32[225,1024]{1,0:T(8,128)}, f32[1,1024]{1,0:T(1,128)}, f32[75,1024]{1,0:T(8,128)}, /*index=5*/f32[1,75]{1,0:T(1,128)}) custom-call(f32[4,80,128]{2,1,0:T(8,128)S(1)} %get-tuple-element.15.fresh, f32[4,80,128]{2,1,0:T(8,128)S(1)} %get-tuple-element.16.misfit, ...), custom_call_target="tpu_custom_call" | custom-call | tf_op jit(solution)/shard_map/unpack/pallas_call | solution.py:512

commit v6 on v5

--- a/solution.py
+++ b/solution.py
@@ -26,6 +26,10 @@
 EAST_AT = (2, 6, 8, 9)
 CELL_AT = (3, 4, 5, 7)
 BLK = 256
+STEPS_XY = (
+    (2, 2), (2, 1), (2, 3), (1, 2), (3, 2), (1, 1), (1, 3), (3, 1), (3, 3), (2, 0), (0, 2), (1, 0), (3, 0), (0, 1), (0, 3)
+)
+STEPS_Z = (8, 7, 9, 6, 10, 5, 11, 4, 12, 3, 13, 2, 14, 1, 15)
 F32 = jnp.float32
 BF16 = jnp.bfloat16
 VMEM_LIMIT = 40 * 1024 * 1024
@@ -50,9 +54,9 @@
     fresh_out, misfit_out, gathered,
     tracer_ref, east_ref, north_ref, target_ref, depth_ref, w1_ref, b1_ref, w2_ref, b2_ref,
     cells, north_own, east_own, rows_out, edges_out, halo_w, halo_e, halo_edges, pick_out, pick_rows, pick_edges,
-    feat, weights, hidden, slope, total, wanted, chunks, core_in, summed, sending, landed,
+    feat, weights, hidden, slope, total, wanted, chunks, core_in, sending, landed,
     mine, strips, strips_in, strips_all, chunk,
-    load_sems, halo_send, halo_recv, core_send, core_recv, send_sems, recv_sems, known,
+    load_sems, halo_send, halo_recv, core_send, core_recv, send_sems, recv_sems, known_tiles, known_ring,
 ):
     z, x, m = lax.axis_index("ocx"), lax.axis_index("ocy"), lax.axis_index("ml")
     core = lax.rem(m, 2)
@@ -60,17 +64,13 @@
     p = x * 8 + m
     sibling = (z, x, m + 1 - 2 * core)
 
-    def other_chip(k):
-        c = lax.rem(chip + k, CHIPS)
-        return c, (z, lax.div(c, 4), lax.rem(c, 4) * 2 + core)
+    def other_chip(dx, dy):
+        to_x, to_m = lax.rem(x + dx, 4), lax.rem(m + 2 * dy, 8)
+        return to_x * 4 + lax.div(to_m, 2), (z, to_x, to_m)
 
     def ring(k):
         w = lax.rem(z + k, NZ)
         return w, (w, x, m)
-
-    def far_first(j):
-        half = lax.div(j + 1, 2)
-        return NZ // 2 + half * (1 - 2 * lax.rem(j, 2))
 
     def tile(k):
         return (z, *place(lax.rem(p + k, TILES)))
@@ -99,12 +99,15 @@
     for target in (to_e, to_w, to_n, to_s, to_ne, to_nw, to_se, to_sw):
         signal(target)
 
-    def spread_word(number, places):
-        targets = [tile(places), tile(TILES - places)]
-        if places < NZ // 2:
-            targets += [ring(places)[1], ring(NZ - places)[1]]
-        for target in targets:
+    def spread_word(known, number, ahead, behind):
+        for target in (ahead, behind):
             pl.semaphore_signal(known.at[number], inc=1, device_id=target, device_id_type=MESH)
+
+    def spread_tiles(number):
+        spread_word(known_tiles, number, tile(1 << number), tile(TILES - (1 << number)))
+
+    def spread_ring(number):
+        spread_word(known_ring, number, ring(1 << number)[1], ring(NZ - (1 << number))[1])
 
     def remote(src, dst, send_sem, recv_sem, target):
         return pltpu.make_async_remote_copy(
@@ -166,14 +169,14 @@
         rows_out[CELL_AT[i]] = cells[i].astype(BF16)
         rows_out[EAST_AT[i]] = east_own[i].astype(BF16)
         rows_out[NORTH_AT[i]] = north_own[i].astype(BF16)
+    pl.semaphore_wait(barrier, 8)
+    copies = [halo(rows_out.at[4:12], halo_w, 0, to_e), halo(rows_out.at[0:7], halo_e, 1, to_w)]
+    spread_tiles(0)
+    spread_ring(0)
     edges = dot(jnp.concatenate([rows_out[n] for n in range(3 * CX)], axis=1), pick_out[...], ((1,), (0,)))
     edges_out[0] = edges[:, 0:CY].astype(BF16)
     edges_out[1] = edges[:, CY : 2 * CY].astype(BF16)
-
-    pl.semaphore_wait(barrier, 8)
-    copies = [
-        halo(rows_out.at[4:12], halo_w, 0, to_e),
-        halo(rows_out.at[0:7], halo_e, 1, to_w),
+    copies += [
         halo(edges_out.at[0], halo_edges.at[0], 2, to_n),
         halo(edges_out.at[0], halo_edges.at[1], 3, to_ne),
         halo(edges_out.at[0], halo_edges.at[2], 4, to_nw),
@@ -181,7 +184,6 @@
         halo(edges_out.at[1], halo_edges.at[4], 6, to_se),
         halo(edges_out.at[1], halo_edges.at[5], 7, to_sw),
     ]
-    spread_word(0, 1)
 
     masks = [level[0:LEV, :] < depth[i] for i in range(CX)]
     for i in range(CX):
@@ -190,6 +192,10 @@
         feat[2 * LEV : 3 * LEV, at] = jnp.where(masks[i], north_own[i, 0:LEV, :], 0.0)
     last = lax.broadcasted_iota(jnp.int32, (ROWS - 3 * LEV, CELLS), 0)
     feat[3 * LEV : ROWS, :] = jnp.where(last < 2, 1.0, 0.0)
+    pl.semaphore_wait(known_tiles.at[0], 2)
+    spread_tiles(1)
+    pl.semaphore_wait(known_ring.at[0], 2)
+    spread_ring(1)
     for load in loads[4:]:
         load.wait()
     wanted[...] = target_ref[...].astype(F32)
@@ -203,10 +209,14 @@
     final = jnp.where(row == 3 * LEV + 1, bias - coarse, final)
     weights[edge:ROWS, :] = final.astype(BF16)
 
-    pl.semaphore_wait(known.at[0], 4)
-    spread_word(1, 2)
+    pl.semaphore_wait(known_tiles.at[1], 2)
+    spread_tiles(2)
     for copy in copies:
         copy.wait_recv()
+    pl.semaphore_wait(known_tiles.at[2], 2)
+    spread_tiles(3)
+    pl.semaphore_wait(known_ring.at[1], 2)
+    spread_ring(2)
 
     cell_rows = [halo_w[0], halo_w[1], halo_w[3]] + [rows_out[n] for n in CELL_AT] + [halo_e[3], halo_e[4], halo_e[5]]
     east_rows = [halo_w[2], halo_w[4], halo_w[5]] + [rows_out[n] for n in EAST_AT] + [halo_e[2], halo_e[6]]
@@ -284,9 +294,6 @@
         now = after
     for i in range(CX):
         cells[i] = now[REACH + i]
-    pl.semaphore_wait(known.at[1], 4)
-    spread_word(2, 4)
-
     for i in range(CX):
         at = slice(CY * i, CY * (i + 1))
         feat[0:LEV, at] = jnp.where(masks[i], cells[i, 0:LEV, :], 0.0)
@@ -303,8 +310,6 @@
         slope[at, :] = gate * (1.0 + stash * (1.0 - gate))
         part = dot(w2_ref[:, at], act, ((1,), (0,)))
         acc = part if acc is None else acc + part
-    pl.semaphore_wait(known.at[2], 4)
-    spread_word(3, 8)
     eye = lax.broadcasted_iota(jnp.int32, (LEV, LEV), 0) == lax.broadcasted_iota(jnp.int32, (LEV, LEV), 1)
     bias2 = jnp.sum(jnp.where(eye, b2_ref[...], 0.0), axis=1, keepdims=True)
     output = acc + bias2
@@ -354,21 +359,18 @@
             sent = value
             if j % 2:
                 low = value - value.astype(BF16).astype(F32)
-                value = jnp.where(row == bias_row + 1, 0.0, value)
                 sent = jnp.where(row == bias_row + 1, pltpu.roll(low, 1, 0), value)
-            summed[2 * per * b + j] = value
             sending[2 * per * b + j] = sent.astype(BF16)
 
-    pl.semaphore_wait(known.at[3], 2)
-
-    def scatter(k, carry):
-        c, target = other_chip(k)
-        remote(sending.at[c], landed.at[k - 1], send_sems.at[0], recv_sems.at[0], target).start()
-        return carry
-
-    lax.fori_loop(1, CHIPS, scatter, 0)
+    pl.semaphore_wait(known_tiles.at[3], 2)
+
+    for n, (dx, dy) in enumerate(STEPS_XY):
+        c, target = other_chip(dx, dy)
+        remote(sending.at[c], landed.at[n], send_sems.at[0], recv_sems.at[0], target).start()
+    has_bias = lax.rem(chip, 2) == 1
+    amount = chunks[core, chip] + core_in[chip]
+    amount = jnp.where(jnp.logical_and(row == bias_row + 1, has_bias), 0.0, amount)
     whole(landed, 0).wait_recv()
-    amount = summed[chip]
     for k in range(CHIPS - 1):
         amount = amount + landed[k].astype(F32)
     mine[...] = amount
@@ -376,34 +378,21 @@
     for k in range(NZ):
         strips[k] = mine[part * k : part * (k + 1), :]
 
-    def scatter_ring(j, carry):
-        k = far_first(j)
+    pl.semaphore_wait(known_ring.at[2], 2)
+    for n, k in enumerate(STEPS_Z):
         w, target = ring(k)
-        remote(strips.at[w], strips_in.at[k - 1], send_sems.at[1], recv_sems.at[1], target).start()
-        return carry
-
-    lax.fori_loop(0, NZ - 1, scatter_ring, 0)
+        remote(strips.at[w], strips_in.at[n], send_sems.at[1], recv_sems.at[1], target).start()
     whole(strips_in, 1).wait_recv()
     strip = strips[z]
-    for k in range(NZ - 1):
-        strip = strip + strips_in[k]
-    strips_all[NZ - 1] = strip
-
-    def gather_ring(j, carry):
-        k = far_first(j)
+    for n in range(NZ - 1):
+        strip = strip + strips_in[n]
+    strips_all[z] = strip
+    for k in STEPS_Z:
         _, target = ring(k)
-        remote(
-            strips_all.at[NZ - 1], strips_all.at[k - 1], send_sems.at[2], recv_sems.at[2], target
-        ).start()
-        return carry
-
-    lax.fori_loop(0, NZ - 1, gather_ring, 0)
-    arrived = strips_all.at[0 : NZ - 1]
-    whole(arrived, 2).wait_recv()
+        remote(strips_all.at[z], strips_all.at[z], send_sems.at[2], recv_sems.at[2], target).start()
+    whole(strips_in, 2).wait_recv()
     for k in range(NZ):
-        place_in = lax.rem(z - k + NZ - 1 + NZ, NZ)
-        mine[part * k : part * (k + 1), :] = strips_all[place_in]
-    has_bias = lax.rem(chip, 2) == 1
+        mine[part * k : part * (k + 1), :] = strips_all[k]
     value = mine[...]
     both = jnp.where(jnp.logical_and(row == bias_row, has_bias), pltpu.roll(value, PAD - 1, 0), 0.0) + value
     low = both - both.astype(BF16).astype(F32)
@@ -411,12 +400,9 @@
     chunk[...] = both.astype(BF16)
     gathered[core, chip] = chunk[...]
 
-    def gather(k, carry):
-        _, target = other_chip(k)
+    for dx, dy in STEPS_XY:
+        _, target = other_chip(dx, dy)
         remote(chunk, gathered.at[core, chip], send_sems.at[3], recv_sems.at[3], target).start()
-        return carry
-
-    lax.fori_loop(1, CHIPS, gather, 0)
     whole(landed, 3).wait_recv()
     forward = remote(gathered.at[core], gathered.at[core], send_sems.at[4], recv_sems.at[4], sibling)
     forward.start()
@@ -424,7 +410,7 @@
         copy.wait_send()
     whole(landed, 0).wait_send()
     whole(strips_in, 1).wait_send()
-    whole(arrived, 2).wait_send()
+    whole(strips_in, 2).wait_send()
     whole(landed, 3).wait_send()
     forward.wait()
 
@@ -464,7 +450,6 @@
             pltpu.VMEM((LEV, CX, CY), F32),
             pltpu.VMEM((2, CHIPS, PAD, CY), F32),
             pltpu.VMEM((CHIPS, PAD, CY), F32),
-            pltpu.VMEM((CHIPS, PAD, CY), F32),
             pltpu.VMEM((CHIPS, PAD, CY), BF16),
             pltpu.VMEM((CHIPS - 1, PAD, CY), BF16),
             pltpu.VMEM((PAD, CY), F32),
@@ -480,6 +465,7 @@
             pltpu.SemaphoreType.DMA((5,)),
             pltpu.SemaphoreType.DMA((5,)),
             pltpu.SemaphoreType.REGULAR((4,)),
+            pltpu.SemaphoreType.REGULAR((3,)),
         ],
         compiler_params=pltpu.CompilerParams(
             collective_id=0, has_side_effects=True, vmem_limit_bytes=VMEM_LIMIT

time: 60.8 us -> 57.1 us (0.939)
  Pallas kernels: 60 us -> 56.3 us
    pallas_call x1, Pallas kernels: 58.7 us -> 54.9 us  [main(): pl.pallas_call(main_kernel, out_shape=(jax.ShapeDtypeStruct((CX, PAD, CY)...]
where the time goes in v6:
time: 57.1 us; the launch traced here: 57 us
  Pallas kernels  56.3 us (99%)
  between operations  0.64 us (1%)
    pallas_call x1, Pallas kernels, main(): pl.pallas_call(main_kernel, out_shape=(jax.ShapeDtypeStruct((CX, PAD, CY)...  54.9 us
    pallas_call x1, Pallas kernels, unpack(): pl.pallas_call(unpack_kernel, out_shape=(jax.ShapeDtypeStruct((LEV, CX, C...  1.39 us

profile of v6, /device:TPU:1, one launch (start us, length us, event | category | flops | bytes accessed | tf_op | source)
XLA Modules:
  0.0 57.0 jit_solution(1417116551064243331)
XLA Ops:
  0.6 54.9 %main.1 = (f32[4,80,128]{2,1,0:T(8,128)S(1)}, f32[4,80,128]{2,1,0:T(8,128)S(1)}, bf16[2,16,80,128]{3,2,1,0:T(8,128)(2,1)S(1)}) custom-call(f32[75,4,128]{2,1,0:T(4,128)} %tracer_hbm.1, f32[75,4,128]{2,1,0:T(4,128)} %east_hbm.1, f32[75,4,128]{2,1,0:T(4,128)} %north_hbm.1, bf16[75,4,128]{2,1,0:T(4,128)(2,1)} %target_hbm.1, s32[4,128]{1,0:T(4,128)} %depth_hbm.1, ...), custom_call_target="tpu_custom_call" | custom-call | tf_op jit(solution)/shard_map/main/pallas_call | solution.py:423
  55.6 1.4 %unpack.1 = (f32[75,4,128]{2,1,0:T(4,128)}, bf16[75,4,128]{2,1,0:T(4,128)(2,1)}, f32[225,1024]{1,0:T(8,128)}, f32[1,1024]{1,0:T(1,128)}, f32[75,1024]{1,0:T(8,128)}, /*index=5*/f32[1,75]{1,0:T(1,128)}) custom-call(f32[4,80,128]{2,1,0:T(8,128)S(1)} %get-tuple-element.15.fresh, f32[4,80,128]{2,1,0:T(8,128)S(1)} %get-tuple-element.16.misfit, ...), custom_call_target="tpu_custom_call" | custom-call | tf_op jit(solution)/shard_map/unpack/pallas_call | solution.py:498

commit v7 on v6

--- a/solution.py
+++ b/solution.py
@@ -1,3 +1,5 @@
+import functools
+
 import jax
 import jax.numpy as jnp
 from jax import lax
@@ -51,10 +53,10 @@
 
 def main_kernel(
     tracer_hbm, east_hbm, north_hbm, target_hbm, depth_hbm, w1_hbm, b1_hbm, w2_hbm, b2_hbm,
-    fresh_out, misfit_out, gathered,
+    tracer_out, misfit_out, w1_out, b1_out, w2_out, b2_out,
     tracer_ref, east_ref, north_ref, target_ref, depth_ref, w1_ref, b1_ref, w2_ref, b2_ref,
     cells, north_own, east_own, rows_out, edges_out, halo_w, halo_e, halo_edges, pick_out, pick_rows, pick_edges,
-    feat, weights, hidden, slope, total, wanted, chunks, core_in, sending, landed,
+    fresh, misfits, gathered, feat, weights, hidden, slope, total, wanted, chunks, core_in, sending, landed,
     mine, strips, strips_in, strips_all, chunk,
     load_sems, halo_send, halo_recv, core_send, core_recv, send_sems, recv_sems, known_tiles, known_ring,
 ):
@@ -83,7 +85,7 @@
         (target_hbm, target_ref), (w1_hbm, w1_ref), (b1_hbm, b1_ref), (w2_hbm, w2_ref), (b2_hbm, b2_ref),
     )
     loads = [pltpu.make_async_copy(src, dst, load_sems.at[i]) for i, (src, dst) in enumerate(pairs)]
-    for load in loads:
+    for load in loads[:4]:
         load.start()
 
     barrier = pltpu.get_barrier_semaphore()
@@ -98,6 +100,8 @@
     to_se, to_sw = diagonal(1, TILES - 1), diagonal(NZ - 1, TILES - 1)
     for target in (to_e, to_w, to_n, to_s, to_ne, to_nw, to_se, to_sw):
         signal(target)
+    for load in loads[4:]:
+        load.start()
 
     def spread_word(known, number, ahead, behind):
         for target in (ahead, behind):
@@ -213,10 +217,6 @@
     spread_tiles(2)
     for copy in copies:
         copy.wait_recv()
-    pl.semaphore_wait(known_tiles.at[2], 2)
-    spread_tiles(3)
-    pl.semaphore_wait(known_ring.at[1], 2)
-    spread_ring(2)
 
     cell_rows = [halo_w[0], halo_w[1], halo_w[3]] + [rows_out[n] for n in CELL_AT] + [halo_e[3], halo_e[4], halo_e[5]]
     east_rows = [halo_w[2], halo_w[4], halo_w[5]] + [rows_out[n] for n in EAST_AT] + [halo_e[2], halo_e[6]]
@@ -294,6 +294,8 @@
         now = after
     for i in range(CX):
         cells[i] = now[REACH + i]
+    pl.semaphore_wait(known_tiles.at[2], 2)
+    spread_tiles(3)
     for i in range(CX):
         at = slice(CY * i, CY * (i + 1))
         feat[0:LEV, at] = jnp.where(masks[i], cells[i, 0:LEV, :], 0.0)
@@ -310,6 +312,8 @@
         slope[at, :] = gate * (1.0 + stash * (1.0 - gate))
         part = dot(w2_ref[:, at], act, ((1,), (0,)))
         acc = part if acc is None else acc + part
+    pl.semaphore_wait(known_ring.at[1], 2)
+    spread_ring(2)
     eye = lax.broadcasted_iota(jnp.int32, (LEV, LEV), 0) == lax.broadcasted_iota(jnp.int32, (LEV, LEV), 1)
     bias2 = jnp.sum(jnp.where(eye, b2_ref[...], 0.0), axis=1, keepdims=True)
     output = acc + bias2
@@ -320,8 +324,8 @@
         goal = jnp.where(masks[i], wanted[:, i, :], 0.0)
         misfit = tendency - goal
         total[0:LEV, at] = misfit * (1.0 / COLUMNS)
-        fresh_out[i, 0:LEV, :] = cells[i, 0:LEV, :] + tendency
-        misfit_out[i, 0:LEV, :] = misfit
+        fresh[i, 0:LEV, :] = cells[i, 0:LEV, :] + tendency
+        misfits[i, 0:LEV, :] = misfit
     d_out = total[...].astype(BF16)
     ones = jnp.ones((16, CELLS), BF16)
     bias_grad = dot(ones, d_out, ((1,), (1,)))
@@ -367,6 +371,10 @@
     for n, (dx, dy) in enumerate(STEPS_XY):
         c, target = other_chip(dx, dy)
         remote(sending.at[c], landed.at[n], send_sems.at[0], recv_sems.at[0], target).start()
+    for i in range(CX):
+        tracer_out[:, i, :] = fresh[i, 0:LEV, :]
+        wanted[:, i, :] = misfits[i, 0:LEV, :]
+    misfit_out[...] = wanted[...].astype(BF16)
     has_bias = lax.rem(chip, 2) == 1
     amount = chunks[core, chip] + core_in[chip]
     amount = jnp.where(jnp.logical_and(row == bias_row + 1, has_bias), 0.0, amount)
@@ -406,6 +414,23 @@
     whole(landed, 3).wait_recv()
     forward = remote(gathered.at[core], gathered.at[core], send_sems.at[4], recv_sems.at[4], sibling)
     forward.start()
+
+    def unpack(half):
+        rest = 3 * LEV - 2 * PAD
+        for t in range(HID // CY):
+            lanes = slice(t * CY, (t + 1) * CY)
+            w1_out[PAD * half : PAD * (half + 1), lanes] = gathered[half, 2 * t].astype(F32)
+            value = gathered[half, 2 * t + 1].astype(F32)
+            if half == 0:
+                w1_out[2 * PAD : 3 * LEV, lanes] = value[0:rest, :]
+                b1_out[:, lanes] = value[rest : rest + 1, :] + value[rest + 1 : rest + 2, :]
+            else:
+                w2_out[:, lanes] = value[0:LEV, :]
+                if t == 0:
+                    b2_out[...] = value[LEV : LEV + 1, 0:LEV] + value[LEV + 1 : LEV + 2, 0:LEV]
+
+    for half in range(2):
+        pl.when(core == half)(functools.partial(unpack, half))
     for copy in copies + to_sibling:
         copy.wait_send()
     whole(landed, 0).wait_send()
@@ -413,6 +438,8 @@
     whole(strips_in, 2).wait_send()
     whole(landed, 3).wait_send()
     forward.wait()
+    for half in range(2):
+        pl.when(core != half)(functools.partial(unpack, half))
 
 
 def main(*operands):
@@ -423,12 +450,15 @@
     return pl.pallas_call(
         main_kernel,
         out_shape=(
-            jax.ShapeDtypeStruct((CX, PAD, CY), F32),
-            jax.ShapeDtypeStruct((CX, PAD, CY), F32),
-            jax.ShapeDtypeStruct((2, CHIPS, PAD, CY), BF16),
+            jax.ShapeDtypeStruct((LEV, CX, CY), F32),
+            jax.ShapeDtypeStruct((LEV, CX, CY), BF16),
+            jax.ShapeDtypeStruct((3 * LEV, HID), F32),
+            jax.ShapeDtypeStruct((1, HID), F32),
+            jax.ShapeDtypeStruct((LEV, HID), F32),
+            jax.ShapeDtypeStruct((1, LEV), F32),
         ),
         in_specs=[hbm] * 9,
-        out_specs=(vmem,) * 3,
+        out_specs=(vmem,) * 6,
         scratch_shapes=[pltpu.VMEM(a.shape, a.dtype) for a in operands]
         + [
             pltpu.VMEM((CX, PAD, CY), F32),
@@ -442,6 +472,9 @@
             pltpu.VMEM((3 * CX * CY, 2 * CY), BF16),
             pltpu.VMEM((WIDE * CY, CY), BF16),
             pltpu.VMEM((6 * CY, 3 * CY), BF16),
+            pltpu.VMEM((CX, PAD, CY), F32),
+            pltpu.VMEM((CX, PAD, CY), F32),
+            pltpu.VMEM((2, CHIPS, PAD, CY), BF16),
             pltpu.VMEM((ROWS, CELLS), F32),
             pltpu.VMEM((ROWS, HID), BF16),
             pltpu.VMEM((HID, CELLS), BF16),
@@ -474,50 +507,32 @@
     )(*(pltpu.with_memory_space_constraint(a, pltpu.HBM) for a in operands))
 
 
-def unpack_kernel(fresh, misfit, chunks, tracer_out, misfit_out, w1_ref, b1_ref, w2_ref, b2_ref, wide):
-    for i in range(CX):
-        tracer_out[:, i, :] = fresh[i, 0:LEV, :]
-        wide[:, i, :] = misfit[i, 0:LEV, :]
-    misfit_out[...] = wide[...].astype(BF16)
-    rest = 3 * LEV - 2 * PAD
-    for t in range(HID // CY):
-        lanes = slice(t * CY, (t + 1) * CY)
-        for g in range(2):
-            w1_ref[PAD * g : PAD * (g + 1), lanes] = chunks[g % 2, 2 * t + g // 2].astype(F32)
-        third = chunks[0, 2 * t + 1].astype(F32)
-        w1_ref[2 * PAD : 3 * LEV, lanes] = third[0:rest, :]
-        b1_ref[:, lanes] = third[rest : rest + 1, :] + third[rest + 1 : rest + 2, :]
-        fourth = chunks[1, 2 * t + 1].astype(F32)
-        w2_ref[:, lanes] = fourth[0:LEV, :]
-        if t == 0:
-            b2_ref[...] = fourth[LEV : LEV + 1, 0:LEV] + fourth[LEV + 1 : LEV + 2, 0:LEV]
-
-
-def unpack(fresh, misfit, chunks):
+def store_kernel(*refs):
+    count = len(refs) // 2
+    copies = [pltpu.make_async_copy(refs[i], refs[count + i], refs[-1].at[i]) for i in (2, 4, 0, 1, 3, 5)]
+    for copy in copies:
+        copy.start()
+    for copy in copies:
+        copy.wait()
+
+
+def store(*results):
     vmem = pl.BlockSpec(memory_space=pltpu.VMEM)
+    hbm = pl.BlockSpec(memory_space=pltpu.HBM)
     return pl.pallas_call(
-        unpack_kernel,
-        out_shape=(
-            jax.ShapeDtypeStruct((LEV, CX, CY), F32),
-            jax.ShapeDtypeStruct((LEV, CX, CY), BF16),
-            jax.ShapeDtypeStruct((3 * LEV, HID), F32),
-            jax.ShapeDtypeStruct((1, HID), F32),
-            jax.ShapeDtypeStruct((LEV, HID), F32),
-            jax.ShapeDtypeStruct((1, LEV), F32),
-        ),
-        in_specs=[vmem] * 3,
-        out_specs=(vmem,) * 6,
-        scratch_shapes=[pltpu.VMEM((LEV, CX, CY), F32)],
-        compiler_params=pltpu.CompilerParams(vmem_limit_bytes=VMEM_LIMIT),
-        name="unpack",
-    )(fresh, misfit, chunks)
+        store_kernel,
+        out_shape=tuple(jax.ShapeDtypeStruct(a.shape, a.dtype) for a in results),
+        in_specs=[vmem] * len(results),
+        out_specs=(hbm,) * len(results),
+        scratch_shapes=[pltpu.SemaphoreType.DMA((len(results),))],
+        compiler_params=pltpu.CompilerParams(vmem_limit_bytes=16 * 1024 * 1024),
+        name="store",
+    )(*results)
 
 
 def on_device(tracer, east, north, target, depth, slots, w1, b1, w2, b2):
-    fresh, misfit, chunks = main(
-        tracer, east, north, target, depth, w1, b1.reshape(1, HID), w2.T, b2.reshape(1, LEV)
-    )
-    tracer_out, misfit_out, grad_w1, grad_b1, grad_w2, grad_b2 = unpack(fresh, misfit, chunks)
+    results = main(tracer, east, north, target, depth, w1, b1.reshape(1, HID), w2.T, b2.reshape(1, LEV))
+    tracer_out, misfit_out, grad_w1, grad_b1, grad_w2, grad_b2 = store(*results)
     return tracer_out, misfit_out, grad_w1, grad_b1.reshape(HID), grad_w2.T, grad_b2.reshape(LEV)
 
 

time: 57.1 us -> 57.1 us (level)
  no operation moved by 1% of the time
where the time goes in v7:
time: 57.1 us; the launch traced here: 56.9 us
  Pallas kernels  56.3 us (99%)
  between operations  0.64 us (1%)
    pallas_call x1, Pallas kernels, main(): pl.pallas_call(main_kernel, out_shape=(jax.ShapeDtypeStruct((LEV, CX, CY)...  55.1 us
    pallas_call x1, Pallas kernels, store(): pl.pallas_call(store_kernel, out_shape=tuple((jax.ShapeDtypeStruct(a.shap...  1.16 us

profile of v7, /device:TPU:1, one launch (start us, length us, event | category | flops | bytes accessed | tf_op | source)
XLA Modules:
  0.0 56.9 jit_solution(18144838652724540001)
XLA Ops:
  0.6 55.1 %main.1 = (f32[75,4,128]{2,1,0:T(4,128)S(1)}, bf16[75,4,128]{2,1,0:T(4,128)(2,1)S(1)}, f32[225,1024]{1,0:T(8,128)S(1)}, f32[1,1024]{1,0:T(1,128)S(1)}, f32[75,1024]{1,0:T(8,128)S(1)}, /*index=5*/f32[1,75]{1,0:T(1,128)S(1)}) custom-call(f32[75,4,128]{2,1,0:T(4,128)} %tracer_hbm.1, f32[75,4,128]{2,1,0:T(4,128)} %east_hbm.1, f32[75,4,128]{2,1,0:T(4,128)} %north_hbm.1, ...), custom_call_target="tpu_custom_call" | custom-call | tf_op jit(solution)/shard_map/main/pallas_call | solution.py:450
  55.8 1.2 %store.1 = (f32[75,4,128]{2,1,0:T(4,128)}, bf16[75,4,128]{2,1,0:T(4,128)(2,1)}, f32[225,1024]{1,0:T(8,128)}, f32[1,1024]{1,0:T(1,128)}, f32[75,1024]{1,0:T(8,128)}, /*index=5*/f32[1,75]{1,0:T(1,128)}) custom-call(f32[75,4,128]{2,1,0:T(4,128)S(1)} %get-tuple-element.18.refs_0_, bf16[75,4,128]{2,1,0:T(4,128)(2,1)S(1)} %get-tuple-element.19.refs_1_, ...), custom_call_target="tpu_custom_call" | custom-call | tf_op jit(solution)/shard_map/store/pallas_call | solution.py:522

commit v8 on v7

--- a/solution.py
+++ b/solution.py
@@ -23,7 +23,10 @@
 COLUMNS = 262144
 REACH = 3
 WIDE = CX + 2 * REACH
-STRIP = 2 * REACH
+STRIP = 4 * REACH
+LATS = 16 * 3
+CORNER = 16
+EDGE = LATS + 2 * CORNER
 NORTH_AT = (0, 1, 10, 11)
 EAST_AT = (2, 6, 8, 9)
 CELL_AT = (3, 4, 5, 7)
@@ -58,7 +61,8 @@
     cells, north_own, east_own, rows_out, edges_out, halo_w, halo_e, halo_edges, pick_out, pick_rows, pick_edges,
     fresh, misfits, gathered, feat, weights, hidden, slope, total, wanted, chunks, core_in, sending, landed,
     mine, strips, strips_in, strips_all, chunk,
-    load_sems, halo_send, halo_recv, core_send, core_recv, send_sems, recv_sems, known_tiles, known_ring,
+    load_sems, halo_send, halo_recv, core_send, core_recv, send_sems, recv_sems,
+    gather_send, gather_recv, forward_send, forward_recv, known_tiles, known_ring,
 ):
     z, x, m = lax.axis_index("ocx"), lax.axis_index("ocy"), lax.axis_index("ml")
     core = lax.rem(m, 2)
@@ -127,34 +131,20 @@
         copy.start()
         return copy
 
-    lane_in = lax.broadcasted_iota(jnp.int32, (CY, 2 * CY), 0)
-    lane_out = lax.broadcasted_iota(jnp.int32, (CY, 2 * CY), 1)
-    shift = jnp.where(lane_in >= CY - REACH, lane_out - lane_in + (CY - REACH), -999)
-    shift = jnp.where(lane_in < REACH, lane_out - lane_in - CY, shift)
+    item = lax.broadcasted_iota(jnp.int32, (2 * EDGE, CY), 0)
+    lane_in = lax.broadcasted_iota(jnp.int32, (2 * EDGE, CY), 1)
+    southern = item >= EDGE
+    item = jnp.where(southern, item - EDGE, item)
+    nth = jnp.where(southern, lane_in, lane_in - (CY - REACH))
+    key = jnp.where(jnp.logical_and(nth >= 0, nth < REACH), item - nth, -999)
+    nth = jnp.where(southern, nth, nth - 1)
+    corner_key = jnp.where(jnp.logical_and(nth >= 0, nth < 2), item - nth, -999)
     for f, order in enumerate((CELL_AT, EAST_AT, NORTH_AT)):
         for i in range(CX):
             at = slice(CY * order[i], CY * (order[i] + 1))
-            pick_out[at, :] = jnp.where(shift == 16 * f + 4 * i, 1.0, 0.0).astype(BF16)
-    lane_in = lax.broadcasted_iota(jnp.int32, (CY, CY), 0)
-    lane_out = lax.broadcasted_iota(jnp.int32, (CY, CY), 1)
-    shift = jnp.where(lane_in >= CY - REACH, lane_out - lane_in + (CY - REACH) - CY // 2, -999)
-    shift = jnp.where(lane_in < REACH, lane_out - lane_in - REACH, shift)
-    for n in range(WIDE):
-        pick_rows[CY * n : CY * (n + 1), :] = jnp.where(shift == STRIP * n, 1.0, 0.0).astype(BF16)
-    lane_in = lax.broadcasted_iota(jnp.int32, (CY, 3 * CY), 0)
-    lane_out = lax.broadcasted_iota(jnp.int32, (CY, 3 * CY), 1)
-    field, owner, nth = lane_in // 16, (lane_in // 4) % 4, lane_in % 4
-    shift = lane_out - (CY * field + STRIP * owner + nth)
-    shift = jnp.where(jnp.logical_and(field < 3, nth < REACH), shift, -999)
-    for n in range(6):
-        dz = (0, -1, 1)[n % 3]
-        here = (n // 3) * (CY // 2 + REACH) + STRIP * (REACH + CX * dz)
-        hit = shift == here
-        if dz == -1:
-            hit = jnp.logical_and(hit, owner >= 1)
-        if dz == 1:
-            hit = jnp.logical_and(hit, owner <= REACH - 1)
-        pick_edges[CY * n : CY * (n + 1), :] = jnp.where(hit, 1.0, 0.0).astype(BF16)
+            first = LATS + 4 * f + (2 * (i - 2) if i >= 2 else CORNER + 2 * i)
+            hit = jnp.logical_or(key == 16 * f + 4 * i, corner_key == first)
+            pick_out[:, at] = jnp.where(hit, 1.0, 0.0).astype(BF16)
 
     level = lax.broadcasted_iota(jnp.int32, (PAD, CY), 0).astype(F32)
     lane = lax.broadcasted_iota(jnp.int32, (PAD, CY), 1)
@@ -177,17 +167,36 @@
     copies = [halo(rows_out.at[4:12], halo_w, 0, to_e), halo(rows_out.at[0:7], halo_e, 1, to_w)]
     spread_tiles(0)
     spread_ring(0)
-    edges = dot(jnp.concatenate([rows_out[n] for n in range(3 * CX)], axis=1), pick_out[...], ((1,), (0,)))
-    edges_out[0] = edges[:, 0:CY].astype(BF16)
-    edges_out[1] = edges[:, CY : 2 * CY].astype(BF16)
-    copies += [
-        halo(edges_out.at[0], halo_edges.at[0], 2, to_n),
-        halo(edges_out.at[0], halo_edges.at[1], 3, to_ne),
-        halo(edges_out.at[0], halo_edges.at[2], 4, to_nw),
-        halo(edges_out.at[1], halo_edges.at[3], 5, to_s),
-        halo(edges_out.at[1], halo_edges.at[4], 6, to_se),
-        halo(edges_out.at[1], halo_edges.at[5], 7, to_sw),
-    ]
+    sources = jnp.concatenate([rows_out[n] for n in range(3 * CX)], axis=1)
+    sources = jnp.concatenate([sources, jnp.zeros((CY - PAD, 3 * CX * CY), BF16)], axis=0)
+    edges_out[...] = dot(pick_out[...], sources, ((1,), (1,))).astype(BF16)
+    to_east, to_west = slice(LATS, LATS + CORNER), slice(LATS + CORNER, EDGE)
+    for side, targets in enumerate(((to_n, to_ne, to_nw), (to_s, to_se, to_sw))):
+        for n, some in enumerate((slice(0, LATS), to_east, to_west)):
+            mine_at = edges_out.at[EDGE * side + some.start : EDGE * side + some.stop]
+            there_at = halo_edges.at[EDGE * side + some.start : EDGE * side + some.stop]
+            copies.append(halo(mine_at, there_at, 2 + 3 * side + n, targets[n]))
+
+    lane_in = lax.broadcasted_iota(jnp.int32, (CY, CY), 0)
+    lane_out = lax.broadcasted_iota(jnp.int32, (CY, CY), 1)
+    shift = jnp.where(lane_in >= CY - REACH, lane_out - 2 * (lane_in - (CY - REACH)) + REACH, -999)
+    shift = jnp.where(lane_in < REACH, lane_out - 2 * (lane_in + REACH), shift)
+    shift = jnp.where(shift >= CY, shift - CY, shift)
+    for n in range(WIDE):
+        pick_rows[CY * n : CY * (n + 1), :] = jnp.where(shift == STRIP * n, 1.0, 0.0).astype(BF16)
+    item = lax.broadcasted_iota(jnp.int32, (LATS, 3 * CY), 0)
+    lane_out = lax.broadcasted_iota(jnp.int32, (LATS, 3 * CY), 1)
+    shift = lane_out - (CY * (item // 16) + STRIP * (REACH + (item // 4) % 4) + 2 * (item % 4))
+    shift = jnp.where(item % 4 < REACH, shift, -999)
+    pick_edges[0:LATS, :] = jnp.where(shift == 0, 1.0, 0.0).astype(BF16)
+    pick_edges[EDGE : EDGE + LATS, :] = jnp.where(shift == REACH, 1.0, 0.0).astype(BF16)
+    item = lax.broadcasted_iota(jnp.int32, (CORNER, 3 * CY), 0)
+    lane_out = lax.broadcasted_iota(jnp.int32, (CORNER, 3 * CY), 1)
+    shift = lane_out - (CY * (item // 4) + STRIP * ((item // 2) % 2) + 2 * (item % 2))
+    shift = jnp.where(item < 12, shift, -999)
+    for n, (first, beside) in enumerate(((1, 2), (WIDE - REACH, 2), (1, REACH), (WIDE - REACH, REACH))):
+        at = EDGE * (n // 2) + LATS + CORNER * (n % 2)
+        pick_edges[at : at + CORNER, :] = jnp.where(shift == STRIP * first + beside, 1.0, 0.0).astype(BF16)
 
     masks = [level[0:LEV, :] < depth[i] for i in range(CX)]
     for i in range(CX):
@@ -221,7 +230,7 @@
     cell_rows = [halo_w[0], halo_w[1], halo_w[3]] + [rows_out[n] for n in CELL_AT] + [halo_e[3], halo_e[4], halo_e[5]]
     east_rows = [halo_w[2], halo_w[4], halo_w[5]] + [rows_out[n] for n in EAST_AT] + [halo_e[2], halo_e[6]]
     north_rows = [halo_w[6], halo_w[7]] + [rows_out[n] for n in NORTH_AT] + [halo_e[0], halo_e[1]]
-    beyond = dot(jnp.concatenate([halo_edges[n] for n in range(6)], axis=1), pick_edges[...], ((1,), (0,)))
+    beyond = dot(halo_edges[...], pick_edges[...], ((0,), (0,)))[0:PAD, :]
 
     def strip_of(some, first, f):
         own = dot(
@@ -236,23 +245,20 @@
     strip = strip_of(cell_rows, 0, 0)
     deep_here = jnp.broadcast_to(strip[LEV : LEV + 1, :], (PAD, CY))
     near_e, far_e = faces(level < jnp.minimum(deep_here, turn(deep_here, -STRIP)), strip_of(east_rows, 0, 1))
-    nth = lane % (CY // 2)
-    nth = nth - STRIP * ((nth * 43) // 256)
-    border = jnp.logical_or(
-        jnp.logical_and(lane < CY // 2, p == 0), jnp.logical_and(lane >= CY // 2, p == TILES - 1)
-    )
-    shut = jnp.logical_and(nth == REACH - 1, border)
-    opened = jnp.logical_and(level < jnp.minimum(deep_here, turn(deep_here, -1)), jnp.logical_not(shut))
+    at_south = jnp.logical_and(lane % STRIP == 2 * (REACH - 1), p == 0)
+    at_north = jnp.logical_and(lane % STRIP == 2 * (REACH - 1) - REACH, p == TILES - 1)
+    shut = jnp.logical_or(at_south, at_north)
+    opened = jnp.logical_and(level < jnp.minimum(deep_here, turn(deep_here, -2)), jnp.logical_not(shut))
     strip_near, strip_far = faces(opened, strip_of(north_rows, 1, 2))
     near_w, far_w = turn(near_e, STRIP), turn(far_e, STRIP)
-    near_s, far_s = turn(strip_near, 1), turn(strip_far, 1)
+    near_s, far_s = turn(strip_near, 2), turn(strip_far, 2)
     strip_coef = (1.0 + far_w - near_e + far_s - strip_near, near_w, far_e, near_s, strip_far)
     strips_at = [strip]
     for step in range(STEPS - 1):
         keep, near_w, far_e, near_s, far_n = strip_coef
         strip = (
             keep * strip + near_w * turn(strip, STRIP) - far_e * turn(strip, -STRIP)
-            + near_s * turn(strip, 1) - far_n * turn(strip, -1)
+            + near_s * turn(strip, 2) - far_n * turn(strip, -2)
         )
         strips_at.append(strip)
 
@@ -264,18 +270,16 @@
     for n in range(WIDE - 1):
         speed = east_own[n - REACH] if REACH <= n < REACH + CX else east_rows[n].astype(F32)
         east_faces.append(faces(level < jnp.minimum(deep[n], deep[n + 1]), speed))
-    shut_n = jnp.logical_and(lane == CY - 1, p == TILES - 1)
     coef = [None] * WIDE
     for n in range(1, WIDE - 1):
         speed = north_own[n - REACH] if REACH <= n < REACH + CX else north_rows[n - 1].astype(F32)
-        there = jnp.where(
-            lane == CY - 1, turn(deep_here, CY - 1 - (CY // 2 + STRIP * n + REACH)), turn(deep[n], -1)
-        )
-        opened = jnp.logical_and(level < jnp.minimum(deep[n], there), jnp.logical_not(shut_n))
-        near_n, far_n = faces(opened, speed)
-        below = -(STRIP * n + REACH - 1)
-        near_s = jnp.where(lane == 0, turn(strip_near, below), turn(near_n, 1))
-        far_s = jnp.where(lane == 0, turn(strip_far, below), turn(far_n, 1))
+        near_n, far_n = faces(level < jnp.minimum(deep[n], turn(deep[n], -1)), speed)
+        edge_at = -(STRIP * n + 2)
+        near_n = jnp.where(lane == CY - 1, turn(strip_near, edge_at), near_n)
+        far_n = jnp.where(lane == CY - 1, turn(strip_far, edge_at), far_n)
+        beyond_at = -(STRIP * n + 2 * (REACH - 1))
+        near_s = jnp.where(lane == 0, turn(strip_near, beyond_at), turn(near_n, 1))
+        far_s = jnp.where(lane == 0, turn(strip_far, beyond_at), turn(far_n, 1))
         near_w, far_w = east_faces[n - 1]
         near_e, far_e = east_faces[n]
         coef[n] = (1.0 + far_w - near_e + far_s - near_n, near_w, far_e, near_s, far_n)
@@ -283,11 +287,9 @@
         after = list(now)
         for n in range(step + 1, WIDE - 1 - step):
             keep, near_w, far_e, near_s, far_n = coef[n]
-            strip = strips_at[step]
-            south = jnp.where(lane == 0, turn(strip, -(STRIP * n + REACH - 1)), turn(now[n], 1))
-            north = jnp.where(
-                lane == CY - 1, turn(strip, CY - 1 - (CY // 2 + STRIP * n + REACH)), turn(now[n], -1)
-            )
+            past = turn(strips_at[step], -(STRIP * n + 2 * (REACH - 1)))
+            south = jnp.where(lane == 0, past, turn(now[n], 1))
+            north = jnp.where(lane == CY - 1, past, turn(now[n], -1))
             after[n] = (
                 keep * now[n] + near_w * now[n - 1] - far_e * now[n + 1] + near_s * south - far_n * north
             )
@@ -406,21 +408,31 @@
     low = both - both.astype(BF16).astype(F32)
     both = jnp.where(jnp.logical_and(row == bias_row + 1, has_bias), pltpu.roll(low, 1, 0), both)
     chunk[...] = both.astype(BF16)
-    gathered[core, chip] = chunk[...]
-
-    for dx, dy in STEPS_XY:
-        _, target = other_chip(dx, dy)
-        remote(chunk, gathered.at[core, chip], send_sems.at[3], recv_sems.at[3], target).start()
-    whole(landed, 3).wait_recv()
-    forward = remote(gathered.at[core], gathered.at[core], send_sems.at[4], recv_sems.at[4], sibling)
-    forward.start()
+    gathered[core, 0] = chunk[...]
+    forwards = []
+    for dx in (2, 1, 3, 0):
+        for dy in (2, 1, 3, 0):
+            if dx or dy:
+                _, target = other_chip(dx, dy)
+                slot = gathered.at[core, 4 * dx + dy]
+                remote(chunk, slot, gather_send.at[dx], gather_recv.at[dx], target).start()
+    for dx in (2, 1, 3, 0):
+        some = gathered.at[core, 4 * dx + (dx == 0) : 4 * dx + 4]
+        remote(some, some, gather_send.at[dx], gather_recv.at[dx], sibling).wait_recv()
+        some = gathered.at[core, 4 * dx : 4 * dx + 4]
+        forwards.append(remote(some, some, forward_send.at[dx], forward_recv.at[dx], sibling))
+        forwards[-1].start()
 
     def unpack(half):
         rest = 3 * LEV - 2 * PAD
+        y = lax.div(m, 2)
         for t in range(HID // CY):
             lanes = slice(t * CY, (t + 1) * CY)
-            w1_out[PAD * half : PAD * (half + 1), lanes] = gathered[half, 2 * t].astype(F32)
-            value = gathered[half, 2 * t + 1].astype(F32)
+            from_x = lax.rem(x + 4 - t // 2, 4) * 4
+            first = from_x + lax.rem(y + 4 - 2 * (t % 2), 4)
+            second = from_x + lax.rem(y + 3 - 2 * (t % 2), 4)
+            w1_out[PAD * half : PAD * (half + 1), lanes] = gathered[half, first].astype(F32)
+            value = gathered[half, second].astype(F32)
             if half == 0:
                 w1_out[2 * PAD : 3 * LEV, lanes] = value[0:rest, :]
                 b1_out[:, lanes] = value[rest : rest + 1, :] + value[rest + 1 : rest + 2, :]
@@ -436,8 +448,11 @@
     whole(landed, 0).wait_send()
     whole(strips_in, 1).wait_send()
     whole(strips_in, 2).wait_send()
-    whole(landed, 3).wait_send()
-    forward.wait()
+    for dx in (2, 1, 3, 0):
+        some = gathered.at[core, 4 * dx + (dx == 0) : 4 * dx + 4]
+        remote(some, some, gather_send.at[dx], gather_recv.at[dx], sibling).wait_send()
+    for forward in forwards:
+        forward.wait()
     for half in range(2):
         pl.when(core != half)(functools.partial(unpack, half))
 
@@ -465,13 +480,13 @@
             pltpu.VMEM((CX, PAD, CY), F32),
             pltpu.VMEM((CX, PAD, CY), F32),
             pltpu.VMEM((3 * CX, PAD, CY), BF16),
-            pltpu.VMEM((2, PAD, CY), BF16),
+            pltpu.VMEM((2 * EDGE, CY), BF16),
             pltpu.VMEM((8, PAD, CY), BF16),
             pltpu.VMEM((7, PAD, CY), BF16),
-            pltpu.VMEM((6, PAD, CY), BF16),
-            pltpu.VMEM((3 * CX * CY, 2 * CY), BF16),
+            pltpu.VMEM((2 * EDGE, CY), BF16),
+            pltpu.VMEM((2 * EDGE, 3 * CX * CY), BF16),
             pltpu.VMEM((WIDE * CY, CY), BF16),
-            pltpu.VMEM((6 * CY, 3 * CY), BF16),
+            pltpu.VMEM((2 * EDGE, 3 * CY), BF16),
             pltpu.VMEM((CX, PAD, CY), F32),
             pltpu.VMEM((CX, PAD, CY), F32),
             pltpu.VMEM((2, CHIPS, PAD, CY), BF16),
@@ -495,8 +510,12 @@
             pltpu.SemaphoreType.DMA((8,)),
             pltpu.SemaphoreType.DMA((halves,)),
             pltpu.SemaphoreType.DMA((halves,)),
-            pltpu.SemaphoreType.DMA((5,)),
-            pltpu.SemaphoreType.DMA((5,)),
+            pltpu.SemaphoreType.DMA((3,)),
+            pltpu.SemaphoreType.DMA((3,)),
+            pltpu.SemaphoreType.DMA((4,)),
+            pltpu.SemaphoreType.DMA((4,)),
+            pltpu.SemaphoreType.DMA((4,)),
+            pltpu.SemaphoreType.DMA((4,)),
             pltpu.SemaphoreType.REGULAR((4,)),
             pltpu.SemaphoreType.REGULAR((3,)),
         ],

time: 57.1 us -> 56.7 us (level)
  no operation moved by 1% of the time
where the time goes in v8:
time: 56.7 us; the launch traced here: 56.5 us
  Pallas kernels  55.9 us (99%)
  between operations  0.64 us (1%)
    pallas_call x1, Pallas kernels, main(): pl.pallas_call(main_kernel, out_shape=(jax.ShapeDtypeStruct((LEV, CX, CY)...  54.7 us
    pallas_call x1, Pallas kernels, store(): pl.pallas_call(store_kernel, out_shape=tuple((jax.ShapeDtypeStruct(a.shap...  1.16 us

profile of v8, /device:TPU:1, one launch (start us, length us, event | category | flops | bytes accessed | tf_op | source)
XLA Modules:
  0.0 56.5 jit_solution(5690646065089953218)
XLA Ops:
  0.6 54.7 %main.1 = (f32[75,4,128]{2,1,0:T(4,128)S(1)}, bf16[75,4,128]{2,1,0:T(4,128)(2,1)S(1)}, f32[225,1024]{1,0:T(8,128)S(1)}, f32[1,1024]{1,0:T(1,128)S(1)}, f32[75,1024]{1,0:T(8,128)S(1)}, /*index=5*/f32[1,75]{1,0:T(1,128)S(1)}) custom-call(f32[75,4,128]{2,1,0:T(4,128)} %tracer_hbm.1, f32[75,4,128]{2,1,0:T(4,128)} %east_hbm.1, f32[75,4,128]{2,1,0:T(4,128)} %north_hbm.1, ...), custom_call_target="tpu_custom_call" | custom-call | tf_op jit(solution)/shard_map/main/pallas_call | solution.py:465
  55.4 1.2 %store.1 = (f32[75,4,128]{2,1,0:T(4,128)}, bf16[75,4,128]{2,1,0:T(4,128)(2,1)}, f32[225,1024]{1,0:T(8,128)}, f32[1,1024]{1,0:T(1,128)}, f32[75,1024]{1,0:T(8,128)}, /*index=5*/f32[1,75]{1,0:T(1,128)}) custom-call(f32[75,4,128]{2,1,0:T(4,128)S(1)} %get-tuple-element.18.refs_0_, bf16[75,4,128]{2,1,0:T(4,128)(2,1)S(1)} %get-tuple-element.19.refs_1_, ...), custom_call_target="tpu_custom_call" | custom-call | tf_op jit(solution)/shard_map/store/pallas_call | solution.py:541

commit v9 on v8

--- a/solution.py
+++ b/solution.py
@@ -27,9 +27,9 @@
 LATS = 16 * 3
 CORNER = 16
 EDGE = LATS + 2 * CORNER
-NORTH_AT = (0, 1, 10, 11)
-EAST_AT = (2, 6, 8, 9)
-CELL_AT = (3, 4, 5, 7)
+NORTH_AT = (0, 1, 2, 3)
+EAST_AT = (4, 5, 6, 7)
+CELL_AT = (8, 9, 10, 11)
 BLK = 256
 STEPS_XY = (
     (2, 2), (2, 1), (2, 3), (1, 2), (3, 2), (1, 1), (1, 3), (3, 1), (3, 3), (2, 0), (0, 2), (1, 0), (3, 0), (0, 1), (0, 3)
@@ -85,7 +85,7 @@
     to_n, to_s = tile(1), tile(TILES - 1)
 
     pairs = (
-        (depth_hbm, depth_ref), (tracer_hbm, tracer_ref), (north_hbm, north_ref), (east_hbm, east_ref),
+        (north_hbm, north_ref), (east_hbm, east_ref), (depth_hbm, depth_ref), (tracer_hbm, tracer_ref),
         (target_hbm, target_ref), (w1_hbm, w1_ref), (b1_hbm, b1_ref), (w2_hbm, w2_ref), (b2_hbm, b2_ref),
     )
     loads = [pltpu.make_async_copy(src, dst, load_sems.at[i]) for i, (src, dst) in enumerate(pairs)]
@@ -104,8 +104,6 @@
     to_se, to_sw = diagonal(1, TILES - 1), diagonal(NZ - 1, TILES - 1)
     for target in (to_e, to_w, to_n, to_s, to_ne, to_nw, to_se, to_sw):
         signal(target)
-    for load in loads[4:]:
-        load.start()
 
     def spread_word(known, number, ahead, behind):
         for target in (ahead, behind):
@@ -150,21 +148,41 @@
     lane = lax.broadcasted_iota(jnp.int32, (PAD, CY), 1)
     tail = lax.broadcasted_iota(jnp.int32, (PAD - LEV, CY), 0)
     none = jnp.zeros((PAD - LEV, CY), F32)
-    for load in loads[:4]:
+    copies = []
+
+    def send_rows(first, east_from, east_rows_n, west_rows_n, east_at, west_at):
+        number = len(copies)
+        start = first + east_from
+        copies.append(
+            halo(rows_out.at[start : start + east_rows_n], halo_w.at[east_at : east_at + east_rows_n], number, to_e)
+        )
+        copies.append(
+            halo(rows_out.at[first : first + west_rows_n], halo_e.at[west_at : west_at + west_rows_n], number + 1, to_w)
+        )
+
+    loads[0].wait()
+    for i in range(CX):
+        north_own[i, 0:LEV, :] = north_ref[:, i, :]
+        north_own[i, LEV:PAD, :] = none
+        rows_out[NORTH_AT[i]] = north_own[i].astype(BF16)
+    pl.semaphore_wait(barrier, 8)
+    send_rows(NORTH_AT[0], 2, 2, 2, 0, 0)
+    loads[1].wait()
+    for i in range(CX):
+        east_own[i, 0:LEV, :] = east_ref[:, i, :]
+        east_own[i, LEV:PAD, :] = none
+        rows_out[EAST_AT[i]] = east_own[i].astype(BF16)
+    send_rows(EAST_AT[0], 1, 3, 2, 2, 2)
+    for load in loads[2:4]:
         load.wait()
     depth = [depth_ref[i : i + 1, :].astype(F32) for i in range(CX)]
     for i in range(CX):
         cells[i, 0:LEV, :] = tracer_ref[:, i, :]
         cells[i, LEV:PAD, :] = jnp.where(tail == 0, depth[i], 0.0)
-        north_own[i, 0:LEV, :] = north_ref[:, i, :]
-        north_own[i, LEV:PAD, :] = none
-        east_own[i, 0:LEV, :] = east_ref[:, i, :]
-        east_own[i, LEV:PAD, :] = none
         rows_out[CELL_AT[i]] = cells[i].astype(BF16)
-        rows_out[EAST_AT[i]] = east_own[i].astype(BF16)
-        rows_out[NORTH_AT[i]] = north_own[i].astype(BF16)
-    pl.semaphore_wait(barrier, 8)
-    copies = [halo(rows_out.at[4:12], halo_w, 0, to_e), halo(rows_out.at[0:7], halo_e, 1, to_w)]
+    send_rows(CELL_AT[0], 1, 3, 3, 5, 4)
+    for load in loads[4:]:
+        load.start()
     spread_tiles(0)
     spread_ring(0)
     sources = jnp.concatenate([rows_out[n] for n in range(3 * CX)], axis=1)
@@ -175,7 +193,7 @@
         for n, some in enumerate((slice(0, LATS), to_east, to_west)):
             mine_at = edges_out.at[EDGE * side + some.start : EDGE * side + some.stop]
             there_at = halo_edges.at[EDGE * side + some.start : EDGE * side + some.stop]
-            copies.append(halo(mine_at, there_at, 2 + 3 * side + n, targets[n]))
+            copies.append(halo(mine_at, there_at, len(copies), targets[n]))
 
     lane_in = lax.broadcasted_iota(jnp.int32, (CY, CY), 0)
     lane_out = lax.broadcasted_iota(jnp.int32, (CY, CY), 1)
@@ -227,9 +245,9 @@
     for copy in copies:
         copy.wait_recv()
 
-    cell_rows = [halo_w[0], halo_w[1], halo_w[3]] + [rows_out[n] for n in CELL_AT] + [halo_e[3], halo_e[4], halo_e[5]]
-    east_rows = [halo_w[2], halo_w[4], halo_w[5]] + [rows_out[n] for n in EAST_AT] + [halo_e[2], halo_e[6]]
-    north_rows = [halo_w[6], halo_w[7]] + [rows_out[n] for n in NORTH_AT] + [halo_e[0], halo_e[1]]
+    cell_rows = [halo_w[5 + n] for n in range(3)] + [rows_out[n] for n in CELL_AT] + [halo_e[4 + n] for n in range(3)]
+    east_rows = [halo_w[2 + n] for n in range(3)] + [rows_out[n] for n in EAST_AT] + [halo_e[2 + n] for n in range(2)]
+    north_rows = [halo_w[n] for n in range(2)] + [rows_out[n] for n in NORTH_AT] + [halo_e[n] for n in range(2)]
     beyond = dot(halo_edges[...], pick_edges[...], ((0,), (0,)))[0:PAD, :]
 
     def strip_of(some, first, f):
@@ -506,8 +524,8 @@
             pltpu.VMEM((NZ, part, CY), F32),
             pltpu.VMEM((PAD, CY), BF16),
             pltpu.SemaphoreType.DMA((len(operands),)),
-            pltpu.SemaphoreType.DMA((8,)),
-            pltpu.SemaphoreType.DMA((8,)),
+            pltpu.SemaphoreType.DMA((12,)),
+            pltpu.SemaphoreType.DMA((12,)),
             pltpu.SemaphoreType.DMA((halves,)),
             pltpu.SemaphoreType.DMA((halves,)),
             pltpu.SemaphoreType.DMA((3,)),

time: 56.7 us -> 56.9 us (level)
  no operation moved by 1% of the time
where the time goes in v9:
time: 56.9 us; the launch traced here: 56.8 us
  Pallas kernels  56.1 us (99%)
  between operations  0.64 us (1%)
    pallas_call x1, Pallas kernels, main(): pl.pallas_call(main_kernel, out_shape=(jax.ShapeDtypeStruct((LEV, CX, CY)...  55 us
    pallas_call x1, Pallas kernels, store(): pl.pallas_call(store_kernel, out_shape=tuple((jax.ShapeDtypeStruct(a.shap...  1.16 us

profile of v9, /device:TPU:1, one launch (start us, length us, event | category | flops | bytes accessed | tf_op | source)
XLA Modules:
  0.0 56.8 jit_solution(10961037701919528459)
XLA Ops:
  0.6 55.0 %main.1 = (f32[75,4,128]{2,1,0:T(4,128)S(1)}, bf16[75,4,128]{2,1,0:T(4,128)(2,1)S(1)}, f32[225,1024]{1,0:T(8,128)S(1)}, f32[1,1024]{1,0:T(1,128)S(1)}, f32[75,1024]{1,0:T(8,128)S(1)}, /*index=5*/f32[1,75]{1,0:T(1,128)S(1)}) custom-call(f32[75,4,128]{2,1,0:T(4,128)} %tracer_hbm.1, f32[75,4,128]{2,1,0:T(4,128)} %east_hbm.1, f32[75,4,128]{2,1,0:T(4,128)} %north_hbm.1, ...), custom_call_target="tpu_custom_call" | custom-call | tf_op jit(solution)/shard_map/main/pallas_call | solution.py:483
  55.6 1.2 %store.1 = (f32[75,4,128]{2,1,0:T(4,128)}, bf16[75,4,128]{2,1,0:T(4,128)(2,1)}, f32[225,1024]{1,0:T(8,128)}, f32[1,1024]{1,0:T(1,128)}, f32[75,1024]{1,0:T(8,128)}, /*index=5*/f32[1,75]{1,0:T(1,128)}) custom-call(f32[75,4,128]{2,1,0:T(4,128)S(1)} %get-tuple-element.18.refs_0_, bf16[75,4,128]{2,1,0:T(4,128)(2,1)S(1)} %get-tuple-element.19.refs_1_, ...), custom_call_target="tpu_custom_call" | custom-call | tf_op jit(solution)/shard_map/store/pallas_call | solution.py:559

commit v10 on v8

--- a/solution.py
+++ b/solution.py
@@ -59,7 +59,7 @@
     tracer_out, misfit_out, w1_out, b1_out, w2_out, b2_out,
     tracer_ref, east_ref, north_ref, target_ref, depth_ref, w1_ref, b1_ref, w2_ref, b2_ref,
     cells, north_own, east_own, rows_out, edges_out, halo_w, halo_e, halo_edges, pick_out, pick_rows, pick_edges,
-    fresh, misfits, gathered, feat, weights, hidden, slope, total, wanted, chunks, core_in, sending, landed,
+    staged, fresh, misfits, gathered, feat, weights, hidden, slope, total, wanted, chunks, core_in, sending, landed,
     mine, strips, strips_in, strips_all, chunk,
     load_sems, halo_send, halo_recv, core_send, core_recv, send_sems, recv_sems,
     gather_send, gather_recv, forward_send, forward_recv, known_tiles, known_ring,
@@ -85,7 +85,7 @@
     to_n, to_s = tile(1), tile(TILES - 1)
 
     pairs = (
-        (depth_hbm, depth_ref), (tracer_hbm, tracer_ref), (north_hbm, north_ref), (east_hbm, east_ref),
+        (depth_hbm, depth_ref), (tracer_hbm, tracer_ref.at[0:LEV]), (north_hbm, north_ref.at[0:LEV]), (east_hbm, east_ref.at[0:LEV]),
         (target_hbm, target_ref), (w1_hbm, w1_ref), (b1_hbm, b1_ref), (w2_hbm, w2_ref), (b2_hbm, b2_ref),
     )
     loads = [pltpu.make_async_copy(src, dst, load_sems.at[i]) for i, (src, dst) in enumerate(pairs)]
@@ -154,11 +154,11 @@
         load.wait()
     depth = [depth_ref[i : i + 1, :].astype(F32) for i in range(CX)]
     for i in range(CX):
-        cells[i, 0:LEV, :] = tracer_ref[:, i, :]
+        cells[i, 0:LEV, :] = tracer_ref[0:LEV, i, :]
         cells[i, LEV:PAD, :] = jnp.where(tail == 0, depth[i], 0.0)
-        north_own[i, 0:LEV, :] = north_ref[:, i, :]
+        north_own[i, 0:LEV, :] = north_ref[0:LEV, i, :]
         north_own[i, LEV:PAD, :] = none
-        east_own[i, 0:LEV, :] = east_ref[:, i, :]
+        east_own[i, 0:LEV, :] = east_ref[0:LEV, i, :]
         east_own[i, LEV:PAD, :] = none
         rows_out[CELL_AT[i]] = cells[i].astype(BF16)
         rows_out[EAST_AT[i]] = east_own[i].astype(BF16)
@@ -211,7 +211,7 @@
     spread_ring(1)
     for load in loads[4:]:
         load.wait()
-    wanted[...] = target_ref[...].astype(F32)
+    wanted[0:LEV] = target_ref[...].astype(F32)
     edge = 3 * LEV // 16 * 16
     weights[0:edge, :] = w1_ref[0:edge, :]
     bias = b1_ref[...]
@@ -323,7 +323,7 @@
     for i in range(CX):
         at = slice(CY * i, CY * (i + 1))
         tendency = jnp.where(masks[i], output[:, at], 0.0).astype(BF16).astype(F32)
-        goal = jnp.where(masks[i], wanted[:, i, :], 0.0)
+        goal = jnp.where(masks[i], wanted[0:LEV, i, :], 0.0)
         misfit = tendency - goal
         total[0:LEV, at] = misfit * (1.0 / COLUMNS)
         fresh[i, 0:LEV, :] = cells[i, 0:LEV, :] + tendency
@@ -374,9 +374,10 @@
         c, target = other_chip(dx, dy)
         remote(sending.at[c], landed.at[n], send_sems.at[0], recv_sems.at[0], target).start()
     for i in range(CX):
-        tracer_out[:, i, :] = fresh[i, 0:LEV, :]
-        wanted[:, i, :] = misfits[i, 0:LEV, :]
-    misfit_out[...] = wanted[...].astype(BF16)
+        staged[0:LEV, i, :] = fresh[i, 0:LEV, :]
+        wanted[0:LEV, i, :] = misfits[i, 0:LEV, :]
+    tracer_out[...] = staged[0:LEV]
+    misfit_out[...] = wanted[0:LEV].astype(BF16)
     has_bias = lax.rem(chip, 2) == 1
     amount = chunks[core, chip] + core_in[chip]
     amount = jnp.where(jnp.logical_and(row == bias_row + 1, has_bias), 0.0, amount)
@@ -474,7 +475,8 @@
         ),
         in_specs=[hbm] * 9,
         out_specs=(vmem,) * 6,
-        scratch_shapes=[pltpu.VMEM(a.shape, a.dtype) for a in operands]
+        scratch_shapes=[pltpu.VMEM((PAD, CX, CY), F32)] * 3
+        + [pltpu.VMEM(a.shape, a.dtype) for a in operands[3:]]
         + [
             pltpu.VMEM((CX, PAD, CY), F32),
             pltpu.VMEM((CX, PAD, CY), F32),
@@ -487,6 +489,7 @@
             pltpu.VMEM((2 * EDGE, 3 * CX * CY), BF16),
             pltpu.VMEM((WIDE * CY, CY), BF16),
             pltpu.VMEM((2 * EDGE, 3 * CY), BF16),
+            pltpu.VMEM((PAD, CX, CY), F32),
             pltpu.VMEM((CX, PAD, CY), F32),
             pltpu.VMEM((CX, PAD, CY), F32),
             pltpu.VMEM((2, CHIPS, PAD, CY), BF16),
@@ -495,7 +498,7 @@
             pltpu.VMEM((HID, CELLS), BF16),
             pltpu.VMEM((HID, CELLS), F32),
             pltpu.VMEM((PAD, CELLS), F32),
-            pltpu.VMEM((LEV, CX, CY), F32),
+            pltpu.VMEM((PAD, CX, CY), F32),
             pltpu.VMEM((2, CHIPS, PAD, CY), F32),
             pltpu.VMEM((CHIPS, PAD, CY), F32),
             pltpu.VMEM((CHIPS, PAD, CY), BF16),

time: 56.7 us -> 56.7 us (level)
  no operation moved by 1% of the time
where the time goes in v10:
time: 56.7 us; the launch traced here: 56.5 us
  Pallas kernels  55.9 us (99%)
  between operations  0.64 us (1%)
    pallas_call x1, Pallas kernels, main(): pl.pallas_call(main_kernel, out_shape=(jax.ShapeDtypeStruct((LEV, CX, CY)...  54.7 us
    pallas_call x1, Pallas kernels, store(): pl.pallas_call(store_kernel, out_shape=tuple((jax.ShapeDtypeStruct(a.shap...  1.16 us

profile of v10, /device:TPU:1, one launch (start us, length us, event | category | flops | bytes accessed | tf_op | source)
XLA Modules:
  0.0 56.5 jit_solution(15790961861683699242)
XLA Ops:
  0.6 54.7 %main.1 = (f32[75,4,128]{2,1,0:T(4,128)S(1)}, bf16[75,4,128]{2,1,0:T(4,128)(2,1)S(1)}, f32[225,1024]{1,0:T(8,128)S(1)}, f32[1,1024]{1,0:T(1,128)S(1)}, f32[75,1024]{1,0:T(8,128)S(1)}, /*index=5*/f32[1,75]{1,0:T(1,128)S(1)}) custom-call(f32[75,4,128]{2,1,0:T(4,128)} %tracer_hbm.1, f32[75,4,128]{2,1,0:T(4,128)} %east_hbm.1, f32[75,4,128]{2,1,0:T(4,128)} %north_hbm.1, ...), custom_call_target="tpu_custom_call" | custom-call | tf_op jit(solution)/shard_map/main/pallas_call | solution.py:466
  55.4 1.2 %store.1 = (f32[75,4,128]{2,1,0:T(4,128)}, bf16[75,4,128]{2,1,0:T(4,128)(2,1)}, f32[225,1024]{1,0:T(8,128)}, f32[1,1024]{1,0:T(1,128)}, f32[75,1024]{1,0:T(8,128)}, /*index=5*/f32[1,75]{1,0:T(1,128)}) custom-call(f32[75,4,128]{2,1,0:T(4,128)S(1)} %get-tuple-element.18.refs_0_, bf16[75,4,128]{2,1,0:T(4,128)(2,1)S(1)} %get-tuple-element.19.refs_1_, ...), custom_call_target="tpu_custom_call" | custom-call | tf_op jit(solution)/shard_map/store/pallas_call | solution.py:544

commit v11 on v10

--- a/solution.py
+++ b/solution.py
@@ -31,9 +31,7 @@
 EAST_AT = (2, 6, 8, 9)
 CELL_AT = (3, 4, 5, 7)
 BLK = 256
-STEPS_XY = (
-    (2, 2), (2, 1), (2, 3), (1, 2), (3, 2), (1, 1), (1, 3), (3, 1), (3, 3), (2, 0), (0, 2), (1, 0), (3, 0), (0, 1), (0, 3)
-)
+STEPS_XY = tuple((dx, dy) for dx in (2, 1, 3, 0) for dy in (2, 1, 3, 0) if dx or dy)
 STEPS_Z = (8, 7, 9, 6, 10, 5, 11, 4, 12, 3, 13, 2, 14, 1, 15)
 F32 = jnp.float32
 BF16 = jnp.bfloat16
@@ -61,7 +59,7 @@
     cells, north_own, east_own, rows_out, edges_out, halo_w, halo_e, halo_edges, pick_out, pick_rows, pick_edges,
     staged, fresh, misfits, gathered, feat, weights, hidden, slope, total, wanted, chunks, core_in, sending, landed,
     mine, strips, strips_in, strips_all, chunk,
-    load_sems, halo_send, halo_recv, core_send, core_recv, send_sems, recv_sems,
+    load_sems, halo_send, halo_recv, core_send, core_recv, send_sems, recv_sems, scatter_recv,
     gather_send, gather_recv, forward_send, forward_recv, known_tiles, known_ring,
 ):
     z, x, m = lax.axis_index("ocx"), lax.axis_index("ocy"), lax.axis_index("ml")
@@ -372,7 +370,7 @@
 
     for n, (dx, dy) in enumerate(STEPS_XY):
         c, target = other_chip(dx, dy)
-        remote(sending.at[c], landed.at[n], send_sems.at[0], recv_sems.at[0], target).start()
+        remote(sending.at[c], landed.at[n], send_sems.at[0], scatter_recv.at[n // 4], target).start()
     for i in range(CX):
         staged[0:LEV, i, :] = fresh[i, 0:LEV, :]
         wanted[0:LEV, i, :] = misfits[i, 0:LEV, :]
@@ -381,9 +379,11 @@
     has_bias = lax.rem(chip, 2) == 1
     amount = chunks[core, chip] + core_in[chip]
     amount = jnp.where(jnp.logical_and(row == bias_row + 1, has_bias), 0.0, amount)
-    whole(landed, 0).wait_recv()
-    for k in range(CHIPS - 1):
-        amount = amount + landed[k].astype(F32)
+    for group in range(4):
+        some = landed.at[4 * group : min(4 * group + 4, CHIPS - 1)]
+        remote(some, some, send_sems.at[0], scatter_recv.at[group], sibling).wait_recv()
+        for k in range(4 * group, min(4 * group + 4, CHIPS - 1)):
+            amount = amount + landed[k].astype(F32)
     mine[...] = amount
     part = PAD // NZ
     for k in range(NZ):
@@ -519,6 +519,7 @@
             pltpu.SemaphoreType.DMA((4,)),
             pltpu.SemaphoreType.DMA((4,)),
             pltpu.SemaphoreType.DMA((4,)),
+            pltpu.SemaphoreType.DMA((4,)),
             pltpu.SemaphoreType.REGULAR((4,)),
             pltpu.SemaphoreType.REGULAR((3,)),
         ],

time: 56.7 us -> 57 us (level)
  no operation moved by 1% of the time
where the time goes in v11:
time: 57 us; the launch traced here: 56.9 us
  Pallas kernels  56.2 us (99%)
  between operations  0.64 us (1%)
    pallas_call x1, Pallas kernels, main(): pl.pallas_call(main_kernel, out_shape=(jax.ShapeDtypeStruct((LEV, CX, CY)...  55.1 us
    pallas_call x1, Pallas kernels, store(): pl.pallas_call(store_kernel, out_shape=tuple((jax.ShapeDtypeStruct(a.shap...  1.16 us

profile of v11, /device:TPU:1, one launch (start us, length us, event | category | flops | bytes accessed | tf_op | source)
XLA Modules:
  0.0 56.9 jit_solution(3636186351118564934)
XLA Ops:
  0.6 55.1 %main.1 = (f32[75,4,128]{2,1,0:T(4,128)S(1)}, bf16[75,4,128]{2,1,0:T(4,128)(2,1)S(1)}, f32[225,1024]{1,0:T(8,128)S(1)}, f32[1,1024]{1,0:T(1,128)S(1)}, f32[75,1024]{1,0:T(8,128)S(1)}, /*index=5*/f32[1,75]{1,0:T(1,128)S(1)}) custom-call(f32[75,4,128]{2,1,0:T(4,128)} %tracer_hbm.1, f32[75,4,128]{2,1,0:T(4,128)} %east_hbm.1, f32[75,4,128]{2,1,0:T(4,128)} %north_hbm.1, ...), custom_call_target="tpu_custom_call" | custom-call | tf_op jit(solution)/shard_map/main/pallas_call | solution.py:466
  55.7 1.2 %store.1 = (f32[75,4,128]{2,1,0:T(4,128)}, bf16[75,4,128]{2,1,0:T(4,128)(2,1)}, f32[225,1024]{1,0:T(8,128)}, f32[1,1024]{1,0:T(1,128)}, f32[75,1024]{1,0:T(8,128)}, /*index=5*/f32[1,75]{1,0:T(1,128)}) custom-call(f32[75,4,128]{2,1,0:T(4,128)S(1)} %get-tuple-element.18.refs_0_, bf16[75,4,128]{2,1,0:T(4,128)(2,1)S(1)} %get-tuple-element.19.refs_1_, ...), custom_call_target="tpu_custom_call" | custom-call | tf_op jit(solution)/shard_map/store/pallas_call | solution.py:545
